TPU v7x, 32 devices: a whole 2x2x4 slice. The times are simulated.
32 devices in a mesh: cell: 8 (over z, x), spot: 4 (over y, core).
Axes of the slice: x: 2, y: 2, z: 4, core: 2. Of those that a mesh axis runs over, the one named last changes fastest.
Arguments:
- logits: float32 [16384, 4096], P('cell', 'spot'), may hold values from -8 to 8
- expression: float32 [16384, 2048], P('cell'), may hold values from -6 to 6
- spatial: float32 [2048, 4096], P('cell', 'spot'), may hold values from -6 to 6
- masks: int32 [4, 2048], replicated, may hold values 0 or 1
- slide_ids: int32 [4096], P('spot'), may hold values from 0 to 3
- counts: int32 [4], replicated, may hold values from 1024 to 2048
Outputs:
- loss: float32 [], replicated
- logit_grad: float32 [16384, 4096], P('cell', 'spot')
- expr_grad: float32 [16384, 2048], P('cell', 'spot')
All inputs are finite; a program needn't handle non-finite values.
Results may differ from a plain program's by a relative error of at most 0.0003.
Values sent between devices are 32-bit elements; how exact they have to be, the bound alone decides.
No kernel may reach another device: no remote copies, remote signals or barrier semaphores. Data moves between devices by JAX's collectives and lax.ppermute only.
A program may use at most 128 MiB of HBM per device.

v0:
```python
import jax
import jax.numpy as jnp
from jax import lax
from jax.sharding import PartitionSpec as P

eps = 1e-06


def on_device(logits, expression, spatial, masks, slide_ids, counts):
    cell_rows = logits.shape[0]
    cells_total = cell_rows * lax.axis_size("cell")
    spots_total = logits.shape[1] * lax.axis_size("spot")
    slide_count = masks.shape[0]
    col_top = lax.pmax(jnp.max(logits, axis=0), "cell")
    exp_vals = jnp.exp(logits - col_top)
    col_total = lax.psum(jnp.sum(exp_vals, axis=0), "cell")
    mapping = exp_vals / col_total
    mass = lax.psum(jnp.sum(mapping, axis=1), "spot") / spots_total
    density_part = -jnp.sum(jnp.log(cells_total * mass)) / cells_total
    onehot = (slide_ids[None, :] == jnp.arange(slide_count, dtype=jnp.int32)[:, None]).astype(
        jnp.float32
    )
    mask_f = masks.astype(jnp.float32)
    lead_cell = lax.axis_index("cell") == 0
    lead_spot = lax.axis_index("spot") == 0
    gene_block = spatial.shape[0]
    offset_genes = lax.axis_index("cell") * gene_block
    columns = expression
    predicted = lax.psum_scatter(
        lax.dot_general(
            columns, mapping, (((0,), (0,)), ((), ())), precision=lax.Precision.HIGHEST
        ),
        "cell",
        scatter_dimension=0,
        tiled=True,
    )
    mask_block = lax.dynamic_slice_in_dim(mask_f, offset_genes, gene_block, 1)
    spot_mask = jnp.dot(mask_block.T, onehot, precision=lax.Precision.HIGHEST)
    product = predicted * spatial
    squared = predicted * predicted
    spat_sq = spatial * spatial

    def by_slide(values):
        return lax.dot_general(
            onehot, values, (((1,), (1,)), ((), ())), precision=lax.Precision.HIGHEST
        )

    spot_local = jnp.stack(
        [
            jnp.sum(spot_mask * product, axis=0),
            jnp.sum(spot_mask * squared, axis=0),
            jnp.sum(spot_mask * spat_sq, axis=0),
        ]
    )
    spot_stats = lax.psum(spot_local, "cell")
    gene_dot, gene_pp, gene_gg = lax.psum(
        (by_slide(product), by_slide(squared), by_slide(spat_sq)), "spot"
    )
    norm_pred = jnp.sqrt(gene_pp + eps)
    norm_spat = jnp.sqrt(gene_gg + eps)
    gene_cos = gene_dot / (norm_pred * norm_spat)
    weights = mask_block / counts.astype(jnp.float32)[:, None]
    gene_part = jnp.sum(weights * gene_cos) / slide_count
    spot_norm_pred = jnp.sqrt(spot_stats[1] + eps)
    spot_norm_spat = jnp.sqrt(spot_stats[2] + eps)
    spot_cos = spot_stats[0] / (spot_norm_pred * spot_norm_spat)
    spot_part = jnp.sum(spot_cos) / spots_total
    pieces = (
        jnp.where(lead_spot, density_part, 0.0)
        - jnp.where(lead_spot, gene_part, 0.0)
        - jnp.where(lead_cell, spot_part, 0.0)
    )
    loss = lax.psum(pieces, ("cell", "spot"))
    gene_weight = -weights / slide_count
    coef_spat = gene_weight / (norm_pred * norm_spat)
    coef_pred = gene_weight * gene_dot / (norm_pred**3 * norm_spat)

    def to_spots(values):
        return lax.dot_general(
            values, onehot, (((0,), (0,)), ((), ())), precision=lax.Precision.HIGHEST
        )

    spot_weight = -1.0 / spots_total
    edge_spat = spot_weight / (spot_norm_pred * spot_norm_spat)
    edge_pred = spot_weight * spot_stats[0] / (spot_norm_pred**3 * spot_norm_spat)
    dpred = spatial * (to_spots(coef_spat) + spot_mask * edge_spat) - predicted * (
        to_spots(coef_pred) + spot_mask * edge_pred
    )
    density_grad = -1.0 / (cells_total * spots_total * mass)
    init_map = jnp.broadcast_to(density_grad[:, None], mapping.shape)
    init_expr = jnp.zeros(expression.shape, jnp.float32)
    section = lax.all_gather(dpred, "cell", axis=0, tiled=True)
    columns = expression
    grad_map = (init_map, init_expr)[0] + jnp.dot(columns, section, precision=lax.Precision.HIGHEST)
    block_vals = lax.dot_general(
        mapping, section, (((1,), (1,)), ((), ())), precision=lax.Precision.HIGHEST
    )
    inner = lax.psum(jnp.sum(mapping * grad_map, axis=0), "cell")
    scale = float(cells_total * spots_total)
    logit_grad = mapping * (grad_map - inner) * scale
    expr_grad = lax.psum_scatter(block_vals, "spot", scatter_dimension=1, tiled=True) * scale
    return (loss, logit_grad, expr_grad)


def solution(mesh):
    placed = (P("cell", "spot"), P("cell", None), P("cell", "spot"), P(), P("spot"), P())
    return jax.shard_map(
        on_device,
        mesh=mesh,
        in_specs=placed,
        out_specs=(P(), P("cell", "spot"), P("cell", "spot")),
        check_vma=False,
    )
```

profile of v0, /device:TPU:0, one launch (start us, length us, event | category | flops | bytes accessed | tf_op | source)
XLA Modules:
  0.0 690.6 jit_solution(14580755537295719456)
XLA Ops:
  7.2 9.1 %copy.19 = f32[2048,1024]{0,1:T(8,128)} copy(f32[2048,1024]{1,0:T(8,128)} %param.6) | data formatting | bytes 16777216 | tf_op args[0]
  16.3 3.9 reduce_max.9
  20.3 23.1 %pmax.7 = f32[1024]{0:T(1024)S(1)} all-reduce(f32[1024]{0:T(1024)S(1)} %reduce_max.9), channel_id=1, replica_groups=mesh['cell'=8,'spot'=4] {'cell'}, use_global_device_ids=true, to_apply=%region_1.0 | all-reduce | flops 1024 | bytes 8192 | tf_op jit(solution)/shard_map/pmax | solution.py:14
  43.4 4.6 fusion.4
  48.0 17.1 %psum.56 = f32[1024]{0:T(1024)S(1)} all-reduce(f32[1024]{0:T(1024)S(1)} %fusion.4), channel_id=1, replica_groups=mesh['cell'=8,'spot'=4] {'cell'}, use_global_device_ids=true, to_apply=%region_3.0 | all-reduce | flops 1024 | bytes 8192 | tf_op jit(solution)/shard_map/psum | solution.py:16
  65.1 72.0 %convolution_bitcast_fusion = f32[2048,1024]{0,1:T(8,128)} fusion(f32[2048,2048]{1,0:T(8,128)} %param.7, f32[2048,1024]{0,1:T(8,128)} %copy.19, f32[1024]{0:T(1024)S(1)} %psum.56, f32[1024]{0:T(1024)S(1)} %pmax.7), kind=kOutput, calls=%fused_computation.8 | convolution fusion | flops 51543801856 | bytes 33562624 | tf_op jit(solution)/shard_map/dot_general | solution.py:30
  138.7 1.6 multiply_reduce_fusion
  140.3 1.6 copy.21
  142.5 4.9 fusion.45
  147.4 138.0 %reduce-scatter.3.cloned.1.call-done = f32[256,1024]{0,1:T(8,128)} async-done(((f32[2048,1024]{0,1:T(8,128)}), f32[256,1024]{0,1:T(8,128)}) %reduce-scatter.3.cloned.1.call-update) | async-done | bytes 1048592 | tf_op jit(solution)/shard_map/reduce_scatter | solution.py:29
  285.5 1.7 multiply_reduce_fusion.2
  287.1 35.2 %psum.61 = f32[3,1024]{1,0:T(4,128)S(1)} all-reduce(f32[3,1024]{1,0:T(4,128)S(1)} %pad_maximum_fusion), channel_id=1, replica_groups=mesh['cell'=8,'spot'=4] {'cell'}, use_global_device_ids=true, to_apply=%region_15.0 | all-reduce | flops 3072 | bytes 24576 | tf_op jit(solution)/shard_map/psum | solution.py:55
  323.0 1.7 fusion.12
  324.7 1.7 fusion.10
  326.4 10.3 %all-reduce = (f32[2048]{0:T(1024)S(1)}, f32[4,256]{1,0:T(4,128)S(1)}, f32[4,256]{1,0:T(4,128)S(1)}, f32[4,256]{1,0:T(4,128)S(1)}) all-reduce(f32[2048]{0:T(1024)S(1)} %fusion.45, f32[4,256]{1,0:T(4,128)S(1)} %fusion.12, f32[4,256]{1,0:T(4,128)S(1)} %fusion.8, f32[4,256]{1,0:T(4,128)S(1)} %fusion.10), channel_id=1, replica_groups=mesh['cell'=8,'spot'=4] {'spot'}, use_global_device_ids=true, to_apply=%region_5.0 | all-reduce | flops 5120 | bytes 40960 | tf_op jit(solution)/shard_map/psum | solution.py:18
  337.4 1.7 fusion.6
  339.4 122.6 %all-gather.2.cloned.1.call-done = f32[2048,1024]{0,1:T(8,128)} async-done(((f32[256,1024]{0,1:T(8,128)}), f32[2048,1024]{0,1:T(8,128)}) %all-gather.2.cloned.1.call-update) | async-done | bytes 8388624 | tf_op jit(solution)/shard_map/all_gather | solution.py:92
  462.0 62.4 %fusion.42 = f32[2048,2048]{1,0:T(8,128)} fusion(f32[2048,1024]{0,1:T(8,128)} %all-gather.2.cloned.1.call-done, f32[2048,1024]{0,1:T(8,128)} %copy.19, f32[1024]{0:T(1024)S(1)} %psum.56, f32[1024]{0:T(1024)S(1)} %pmax.7), kind=kOutput, calls=%fused_computation.63 | convolution fusion | flops 51543801856 | bytes 33562624 | tf_op jit(solution)/shard_map/dot_general | solution.py:95
  527.7 38.7 %psum.62 = f32[]{:T(128)} all-reduce(f32[]{:T(128)S(6)} %sub.28), channel_id=1, replica_groups=mesh['cell'=8,'spot'=4] {'cell','spot'}, use_global_device_ids=true, to_apply=%region_17.18 | all-reduce | flops 1 | bytes 8 | tf_op jit(solution)/shard_map/psum | solution.py:73
  566.4 73.3 %fusion = (f32[1024]{0:T(1024)S(1)}, f32[1024,2048]{1,0:T(8,128)}) fusion(f32[2048]{0:T(1024)S(1)} %get-tuple-element.18, f32[1024]{0:T(1024)S(1)} %psum.56, f32[2048,1024]{0,1:T(8,128)} %copy.19, f32[1024]{0:T(1024)S(1)} %pmax.7, f32[2048,1024]{0,1:T(8,128)} %all-gather.2.cloned.1.call-done, f32[2048,2048]{1,0:T(8,128)} %param.7), kind=kOutput, calls=%fused_computation.2 | convolution fusion | flops 51550093312 | bytes 41963520 | tf_op jit(solution)/shard_map/dot_general | solution.py:94
  639.7 21.1 %psum.63 = f32[1024]{0:T(1024)S(1)} all-reduce(f32[1024]{0:T(1024)S(1)} %get-tuple-element.22), channel_id=1, replica_groups=mesh['cell'=8,'spot'=4] {'cell'}, use_global_device_ids=true, to_apply=%region_19.20 | all-reduce | flops 1024 | bytes 8192 | tf_op jit(solution)/shard_map/psum | solution.py:98
  660.7 9.4 %fusion.2 = f32[2048,1024]{0,1:T(8,128)} fusion(f32[1024,2048]{1,0:T(8,128)} %get-tuple-element.23, f32[1024]{0:T(1024)S(1)} %psum.63, f32[2048]{0:T(1024)S(1)} %get-tuple-element.18, f32[1024]{0:T(1024)S(1)} %psum.56, f32[2048,1024]{0,1:T(8,128)} %copy.19, f32[1024]{0:T(1024)S(1)} %pmax.7), kind=kLoop, calls=%fused_computation.4 | loop fusion | flops 12582912 | bytes 25186304 | tf_op jit(solution)/shard_map/mul | solution.py:100
  670.1 9.2 %copy.28 = f32[2048,1024]{1,0:T(8,128)} copy(f32[2048,1024]{0,1:T(8,128)} %fusion.2) | data formatting | bytes 16777216
  679.4 4.7 broadcast_multiply_fusion
  (25 shorter events, 5.1 us)
Async XLA Ops:
  7.2 278.3 %reduce-scatter.3.cloned.1.call-start = ((), (), s32[]{:S(2)}) async-start(), calls=%async_computation.2 | async-start | bytes 9437184 | tf_op jit(solution)/shard_map/reduce_scatter | solution.py:29
  137.1 1.2 copy-start.1
  137.1 1.6 copy-start.2
  137.1 1.6 copy-start.3
  137.1 4.8 copy-start.4
  137.1 324.8 %all-gather.2.cloned.1.call-start = ((), (), s32[]{:S(2)}) async-start(), calls=%async_computation.3 | async-start | bytes 9437184 | tf_op jit(solution)/shard_map/all_gather | solution.py:92
  285.5 51.9 %copy-start = (f32[256,1024]{0,1:T(8,128)S(1)}, f32[256,1024]{0,1:T(8,128)}, u32[]{:S(2)}) copy-start(f32[256,1024]{0,1:T(8,128)} %reduce-scatter.3.cloned.1.call-done) | copy-start | bytes 3145732
  339.1 340.2 %reduce-scatter.5.cloned.1.call-start = ((), (), s32[]{:S(2)}) async-start(), calls=%async_computation.4 | async-start | bytes 20971520 | tf_op jit(solution)/shard_map/reduce_scatter | solution.py:101
Sparse Core Ops, SparseCore 0:
  137.3 148.1 reduce-scatter.2
  339.2 122.6 all-gather.1
  524.5 124.8 reduce-scatter.4
where the time goes:
time: 691 us
  waiting for transfers between devices  261 us (38%)
  matrix products  216 us (31%)
  blocking collectives  145 us (21%)
  other arithmetic  31.1 us (5%)
  local copies, waits for them, and re-layouts  21.4 us (3%)
  between operations  15.8 us (2%)
    reduce_scatter x1, waiting for transfers between devices, on_device(): lax.psum_scatter(lax.dot_general(columns, mapping, (((0,), (0,)), ((), ()...  138 us
    all_gather x1, waiting for transfers between devices, on_device(): section = lax.all_gather(dpred, 'cell', axis=0, tiled=True)  123 us
    dot_general x1, matrix products, on_device(): jnp.dot(columns, section, precision=lax.Precision.HIGHEST)  73.3 us
    dot_general x1, matrix products, on_device(): lax.dot_general(columns, mapping, (((0,), (0,)), ((), ())), precision=lax...  72 us
    dot_general x1, matrix products, on_device(): lax.dot_general(mapping, section, (((1,), (1,)), ((), ())), precision=lax...  62.4 us
    psum x1, blocking collectives, on_device(): loss = lax.psum(pieces, ('cell', 'spot'))  38.7 us
    psum x1, blocking collectives, on_device(): spot_stats = lax.psum(spot_local, 'cell')  35.2 us
    pmax x1, blocking collectives, on_device(): col_top = lax.pmax(jnp.max(logits, axis=0), 'cell')  23.1 us
  transfers between devices with their start and end apart: 3, of which 2 were waited for; matrix products, arithmetic and copies ran while one was open for 15% of the time, Pallas kernels for 0%

commit v1 on v0

v1 whole, which is shorter than its diff:
```python
import functools

import jax
import jax.numpy as jnp
from jax import lax
from jax.experimental import pallas as pl
from jax.experimental.pallas import tpu as pltpu
from jax.sharding import PartitionSpec as P

eps = 1e-06
F32 = jnp.float32
BF16 = jnp.bfloat16
MIB = 1024 * 1024


def shape_of(*dims, dtype=F32):
    return jax.ShapeDtypeStruct(dims, dtype)


def params(mib):
    return pltpu.CompilerParams(vmem_limit_bytes=mib * MIB)


def split(v):
    high = v.astype(BF16)
    return high, (v - high.astype(F32)).astype(BF16)


def dot(a, b, ca, cb, precision=None):
    return lax.dot_general(
        a, b, (((ca,), (cb,)), ((), ())), precision=precision, preferred_element_type=F32
    )


def dot3(ah, al, bh, bl, ca, cb):
    return dot(ah, bh, ca, cb) + dot(al, bh, ca, cb) + dot(ah, bl, ca, cb)


def exact(a, b, ca, cb):
    return dot(a, b, ca, cb, lax.Precision.HIGHEST)


def cost(flops, nbytes):
    return pl.CostEstimate(flops=int(flops), bytes_accessed=int(nbytes), transcendentals=0)


def exp_body(logits, high, low, sums):
    vals = jnp.exp(logits[...])
    high[...], low[...] = split(vals)

    @pl.when(pl.program_id(0) == 0)
    def _():
        sums[...] = jnp.zeros_like(sums)

    sums[...] += jnp.sum(vals.reshape(-1, 8, vals.shape[1]), axis=0)


def exp_split(logits):
    rows, cols = logits.shape
    step = 256
    tile = pl.BlockSpec((step, cols), lambda i: (i, 0))
    return pl.pallas_call(
        exp_body,
        grid=(rows // step,),
        in_specs=[tile],
        out_specs=[tile, tile, pl.BlockSpec((8, cols), lambda i: (0, 0))],
        out_shape=[shape_of(rows, cols, dtype=BF16)] * 2 + [shape_of(8, cols)],
        compiler_params=params(32),
        cost_estimate=cost(rows * cols * 10, rows * cols * 8),
    )(logits)


def part_body(order, source, high, low):
    high[...], low[...] = split(source[...])


def part_split(expression, order, shard):
    rows, genes = expression.shape
    step = rows // 2
    if shard % 128:
        expression = expression.reshape(rows, -1, shard)[:, order].reshape(rows, genes)
        shard = genes // 8
        order = jnp.arange(8, dtype=jnp.int32)
    tile = pl.BlockSpec((step, shard), lambda p, i, order: (i, p))
    return pl.pallas_call(
        part_body,
        grid_spec=pltpu.PrefetchScalarGridSpec(
            num_scalar_prefetch=1,
            grid=(genes // shard, rows // step),
            in_specs=[pl.BlockSpec((step, shard), lambda p, i, order: (i, order[p]))],
            out_specs=[tile, tile],
        ),
        out_shape=[shape_of(rows, genes, dtype=BF16)] * 2,
        compiler_params=params(32),
        cost_estimate=cost(rows * genes * 4, rows * genes * 8),
    )(order, expression)


def send_body(eh, el, mh, ml, out):
    out[...] = dot3(eh[...], el[...], mh[...], ml[...], 0, 0)


def keep_body(half, eh, el, mh, ml, add, keep, send):
    vals = dot3(eh[...], el[...], mh[...], ml[...], 0, 0) + add[...]

    @pl.when(pl.program_id(0) < half)
    def _():
        keep[...] = vals

    @pl.when(pl.program_id(0) >= half)
    def _():
        send[...] = vals


def predict(eparts, mparts, unit, where, count, column, width, add=None):
    rows = mparts[0].shape[0]
    etile = pl.BlockSpec((rows, unit), lambda i: (0, where(i)))
    mtile = pl.BlockSpec((rows, width), lambda i: (0, column))
    flops = 6 * rows * unit * count * width
    traffic = 4 * rows * (unit * count + width) + 4 * unit * count * width
    if add is None:
        return pl.pallas_call(
            send_body,
            grid=(count,),
            in_specs=[etile, etile, mtile, mtile],
            out_specs=pl.BlockSpec((unit, width), lambda i: (i, 0)),
            out_shape=shape_of(unit * count, width),
            compiler_params=params(40),
            cost_estimate=cost(flops, traffic),
        )(*eparts, *mparts)
    half = count // 2
    return pl.pallas_call(
        functools.partial(keep_body, half),
        grid=(count,),
        in_specs=[etile, etile, mtile, mtile, pl.BlockSpec((unit, width), lambda i: (i, 0))],
        out_specs=[
            pl.BlockSpec((unit, width), lambda i: (jnp.minimum(i, half - 1), 0)),
            pl.BlockSpec((unit, width), lambda i: (jnp.maximum(i - half, 0), 0)),
        ],
        out_shape=[shape_of(unit * half, width)] * 2,
        compiler_params=params(40),
        cost_estimate=cost(flops, traffic),
    )(*eparts, *mparts, add)


def stats_body(kept, came, sums, spatial, mask, onehot, pred, spots, genes):
    total = jnp.sum(sums[...], axis=0, keepdims=True)
    vals = (kept[...] + came[...]) / total
    pred[...] = vals
    spat = spatial[...]
    seen = dot(mask[...].astype(BF16), onehot[...].astype(BF16), 0, 0)
    terms = (vals * spat, vals * vals, spat * spat)
    rows = [jnp.sum(seen * t, axis=0, keepdims=True) for t in terms]
    spots[...] = jnp.concatenate(rows + [jnp.zeros((5, rows[0].shape[1]), F32)], axis=0)
    genes[...] = jnp.concatenate([exact(onehot[...], t, 1, 1) for t in terms], axis=0)


def stats(kept, came, sums, spatial, mask, onehot, column):
    shard, width = kept.shape
    whole = pl.BlockSpec((shard, width), lambda i: (0, 0))
    strip = pl.BlockSpec((8, width), lambda i: (0, column))
    return pl.pallas_call(
        stats_body,
        grid=(1,),
        in_specs=[
            whole,
            whole,
            strip,
            pl.BlockSpec((shard, width), lambda i: (0, column)),
            pl.BlockSpec((8, shard), lambda i: (0, 0)),
            strip,
        ],
        out_specs=[
            whole,
            pl.BlockSpec((8, width), lambda i: (0, 0)),
            pl.BlockSpec((24, shard), lambda i: (0, 0)),
        ],
        out_shape=[shape_of(shard, width), shape_of(8, width), shape_of(24, shard)],
        compiler_params=params(32),
        cost_estimate=cost(shard * width * 40, shard * width * 16),
    )(kept, came, sums, spatial, mask, onehot)


def grad_body(slides, spots_total, parts, *refs):
    preds = refs[:parts]
    sums, spatial, mask, onehot, counts, gene_sums, spot_sums = refs[parts : parts + 7]
    outs = refs[parts + 7 : -2]
    inner, losses = refs[-2:]
    size = mask.shape[1]
    dot_g, pp_g, gg_g = (gene_sums[8 * i : 8 * i + 8, :] for i in range(3))
    norm_p, norm_s = jnp.sqrt(pp_g + eps), jnp.sqrt(gg_g + eps)
    weights = mask[...] / counts[...][:, :1]
    gene_part = jnp.sum(weights * (dot_g / (norm_p * norm_s))) / slides
    gene_weight = -weights / slides
    coef_s = gene_weight / (norm_p * norm_s)
    coef_p = gene_weight * dot_g / (norm_p * norm_p * norm_p * norm_s)
    a, b, c = (spot_sums[i : i + 1, :] for i in range(3))
    near_p, near_s = jnp.sqrt(b + eps), jnp.sqrt(c + eps)
    spot_part = jnp.sum(a / (near_p * near_s)) / spots_total
    edge_s = (-1.0 / spots_total) / (near_p * near_s)
    edge_p = (-1.0 / spots_total) * a / (near_p * near_p * near_p * near_s)
    total = jnp.sum(sums[...], axis=0, keepdims=True)
    hot = onehot[...]
    seen = dot(mask[...].astype(BF16), hot.astype(BF16), 0, 0)
    pred = jnp.concatenate([r[...] for r in preds], axis=1)
    grad = spatial[...] * (exact(coef_s, hot, 0, 0) + seen * edge_s) - pred * (
        exact(coef_p, hot, 0, 0) + seen * edge_p
    )
    row = jnp.sum(pred * grad, axis=0, keepdims=True)
    inner[...] = jnp.broadcast_to(row, inner.shape)
    grad = grad / total
    start = 0
    for out in outs:
        out[...] = grad[start : start + out.shape[0]]
        start += out.shape[0]
    lane = lax.broadcasted_iota(jnp.int32, losses.shape, 1)
    losses[...] = jnp.where(lane == 0, gene_part, jnp.where(lane == 1, spot_part, 0.0))


def gradient(preds, sums, spatial, mask, onehot, counts, gene_sums, spot_sums, heights, slides, spots_total):
    shard, cols = spatial.shape
    args = (*preds, sums, spatial, mask, onehot, counts, gene_sums, spot_sums)
    outs = [shape_of(h, cols) for h in heights] + [shape_of(8, cols), shape_of(8, 128)]
    return pl.pallas_call(
        functools.partial(grad_body, float(slides), float(spots_total), len(preds)),
        grid=(1,),
        in_specs=[pl.BlockSpec(a.shape, lambda i: (0, 0)) for a in args],
        out_specs=[pl.BlockSpec(o.shape, lambda i: (0, 0)) for o in outs],
        out_shape=outs,
        compiler_params=params(40),
        cost_estimate=cost(shard * cols * 60, shard * cols * 12),
    )(*args)


def mass_body(sums, mh, ml, out):
    inv = 1.0 / jnp.sum(sums[...], axis=0, keepdims=True)
    ih, il = split(jnp.broadcast_to(inv, (8, inv.shape[1])))
    out[...] = dot3(ih, il, mh[...], ml[...], 1, 1)


def mass_rows(sums, mparts):
    rows, cols = mparts[0].shape
    step = 512
    tile = pl.BlockSpec((step, cols), lambda i: (i, 0))
    return pl.pallas_call(
        mass_body,
        grid=(rows // step,),
        in_specs=[pl.BlockSpec((8, cols), lambda i: (0, 0)), tile, tile],
        out_specs=pl.BlockSpec((8, step), lambda i: (0, i)),
        out_shape=shape_of(8, rows),
        compiler_params=params(32),
        cost_estimate=cost(rows * cols * 48, rows * cols * 4),
    )(sums, *mparts)


def pull_body(dens, sums, mh, ml, out):
    dh, dl = split(jnp.broadcast_to(dens[...][:1], dens.shape))

    @pl.when(pl.program_id(0) == 0)
    def _():
        out[...] = jnp.zeros_like(out)

    out[...] += dot3(dh, dl, mh[...], ml[...], 1, 0) / jnp.sum(sums[...], axis=0, keepdims=True)


def pull_cols(dens, sums, mparts):
    rows, cols = mparts[0].shape
    step = 512
    tile = pl.BlockSpec((step, cols), lambda i: (i, 0))
    strip = pl.BlockSpec((8, cols), lambda i: (0, 0))
    return pl.pallas_call(
        pull_body,
        grid=(rows // step,),
        in_specs=[pl.BlockSpec((8, step), lambda i: (0, i)), strip, tile, tile],
        out_specs=strip,
        out_shape=shape_of(8, cols),
        compiler_params=params(32),
        cost_estimate=cost(rows * cols * 48, rows * cols * 4),
    )(dens, sums, *mparts)


def expr_body(number, height, half, ids, near, far, across, mh, ml, ph, pls, *refs):
    outs, (oh, ol, ch, cl) = refs[:-4], refs[-4:]

    @pl.when(pl.program_id(0) == 0)
    def _():
        for n in range(number):
            at = ids[n]
            inside = pl.ds(pl.multiple_of((at % half) * height, 16), height)
            own = jnp.where(at < half, near[inside, :], far[inside, :])
            other = across[pl.ds(pl.multiple_of(ids[number + n] * height, 16), height), :]
            put = slice(n * height, (n + 1) * height)
            oh[put, :], ol[put, :] = split(own)
            ch[put, :], cl[put, :] = split(other)

    vals = dot3(mh[...], ml[...], oh[...], ol[...], 1, 1) + dot3(
        ph[...], pls[...], ch[...], cl[...], 1, 1
    )
    width = vals.shape[1] // len(outs)
    for n, out in enumerate(outs):
        out[...] = vals[:, n * width : (n + 1) * width]


def expr_part(ids, near, far, across, mparts, pparts, height, blocks, number):
    rows, cols = mparts[0].shape
    step = 512
    half = near.shape[0] // height
    tile = pl.BlockSpec((step, cols), lambda i, ids: (i, 0))
    width = number * height // blocks
    return pl.pallas_call(
        functools.partial(expr_body, number, height, half),
        grid_spec=pltpu.PrefetchScalarGridSpec(
            num_scalar_prefetch=1,
            grid=(rows // step,),
            in_specs=[pl.BlockSpec(a.shape, lambda i, ids: (0, 0)) for a in (near, far, across)]
            + [tile] * 4,
            out_specs=[pl.BlockSpec((step, width), lambda i, ids: (i, 0))] * blocks,
            scratch_shapes=[pltpu.VMEM((number * height, cols), BF16)] * 4,
        ),
        out_shape=[shape_of(rows, width)] * blocks,
        compiler_params=params(48),
        cost_estimate=cost(12 * rows * cols * number * height, rows * cols * 8),
    )(ids, near, far, across, *mparts, *pparts)


def logit_body(pieces, heights, scale, dens, sums, inner, eh, el, mh, ml, *refs):
    grads, (out, dh, dl) = refs[:-3], refs[-3:]

    @pl.when(pl.program_id(0) == 0)
    def _():
        at = 0
        for p in range(pieces):
            for q, height in enumerate(heights):
                source = grads[2 * q + (p >= pieces // 2)]
                inside = p % (pieces // 2)
                dh[at : at + height, :], dl[at : at + height, :] = split(
                    source[inside * height : (inside + 1) * height, :]
                )
                at += height

    inv = 1.0 / jnp.sum(sums[...], axis=0, keepdims=True)
    column = jnp.transpose(dens[...])[:, :1]
    vals = dot3(eh[...], el[...], dh[...], dl[...], 1, 0) + (column - inner[...][:1]) * inv
    out[...] = (mh[...].astype(F32) + ml[...].astype(F32)) * vals * scale


def logit_part(dens, sums, inner, eparts, mparts, grads, heights, pieces, scale):
    rows, cols = mparts[0].shape
    genes = eparts[0].shape[1]
    step = 256
    strip = pl.BlockSpec((8, cols), lambda i: (0, 0))
    tile = pl.BlockSpec((step, cols), lambda i: (i, 0))
    return pl.pallas_call(
        functools.partial(logit_body, pieces, heights, scale),
        grid=(rows // step,),
        in_specs=[pl.BlockSpec((8, step), lambda i: (0, i)), strip, strip]
        + [pl.BlockSpec((step, genes), lambda i: (i, 0))] * 2
        + [tile] * 2
        + [pl.BlockSpec(g.shape, lambda i: (0, 0), pipeline_mode=pl.Buffered(1)) for g in grads],
        out_specs=tile,
        out_shape=shape_of(rows, cols),
        scratch_shapes=[pltpu.VMEM((genes, cols), BF16)] * 2,
        compiler_params=params(52),
        cost_estimate=cost(6 * rows * cols * genes, rows * genes * 4 + rows * cols * 8),
    )(dens, sums, inner, *eparts, *mparts, *grads)


def join_body(shards, heights, scale, *refs):
    out = refs[-1]
    shard = sum(heights)
    at = 0
    for q, height in enumerate(heights):
        vals = (refs[2 * q][...] + refs[2 * q + 1][...]) * scale
        for b in range(shards):
            out[:, b * shard + at : b * shard + at + height] = vals[:, b * height : (b + 1) * height]
        at += height


def join(pairs, heights, shards, scale):
    flat = [v for pair in pairs for v in pair]
    rows = flat[0].shape[0]
    step = 512
    genes = shards * sum(heights)
    return pl.pallas_call(
        functools.partial(join_body, shards, heights, scale),
        grid=(rows // step,),
        in_specs=[pl.BlockSpec((step, v.shape[1]), lambda i: (i, 0)) for v in flat],
        out_specs=pl.BlockSpec((step, genes), lambda i: (i, 0)),
        out_shape=shape_of(rows, genes),
        compiler_params=params(32),
        cost_estimate=cost(rows * genes * 2, rows * genes * 12),
    )(*flat)


def swap(v, axis, bit):
    size = lax.axis_size(axis)
    return lax.ppermute(v, axis, [(i, i ^ (1 << bit)) for i in range(size)])


def add_all(v, axis):
    for bit in range(lax.axis_size(axis).bit_length() - 1):
        v = v + swap(v, axis, bit)
    return v


def reverse(value, bits):
    return sum(((value >> b) & 1) << (bits - 1 - b) for b in range(bits))


def on_device(logits, expression, spatial, masks, slide_ids, counts):
    cells, spots_n = lax.axis_size("cell"), lax.axis_size("spot")
    me, mine = lax.axis_index("cell"), lax.axis_index("spot")
    rows, cols = logits.shape
    shard = spatial.shape[0]
    slides, genes = masks.shape
    cells_total, spots_total = rows * cells, cols * spots_n
    cell_bits = cells.bit_length() - 1
    per_block = cells // spots_n
    block_bits = per_block.bit_length() - 1
    scale = float(cells_total * spots_total)

    other_logits = swap(logits, "spot", 0)
    *mparts, sums = exp_split(logits)
    order = me ^ reverse(jnp.arange(cells, dtype=jnp.int32), cell_bits)
    eparts = part_split(expression, order, shard)
    sums = add_all(sums, "cell")

    mask8 = jnp.pad(masks.astype(F32), ((0, 8 - slides), (0, 0)))
    mask8 = lax.dynamic_slice_in_dim(mask8, me * shard, shard, 1)
    onehot = (slide_ids[None, :] == jnp.arange(8, dtype=jnp.int32)[:, None]).astype(F32)
    counts8 = jnp.broadcast_to(
        jnp.pad(counts.astype(F32), (0, 8 - slides), constant_values=1.0)[:, None], (8, 128)
    )

    unit = 256
    count = genes // 2 // unit
    width = 256
    preds, spot_stats, gene_stats = [], [], 0.0
    for q in range(cols // width):
        z_first = cells == 8 and shard == unit and q == 1
        if z_first:
            bits = (1, 0, 2)
            send_at = lambda i: (i // 2) * 4 + 2 + i % 2
            keep_at = lambda i: (i // 2) * 4 + i % 2
        else:
            bits = tuple(range(cell_bits))
            send_at = lambda i: count + i
            keep_at = lambda i: i
        send = predict(eparts, mparts, unit, send_at, count, q, width)
        came = swap(send, "cell", bits[0])
        kept, send = predict(eparts, mparts, unit, keep_at, count, q, width, came)
        for bit in bits[1:-1]:
            both = kept, swap(send, "cell", bit)
            half = kept.shape[0] // 2
            send = both[0][half:] + both[1][half:]
            kept = both[0][:half] + both[1][:half]
        came = swap(send, "cell", bits[-1])
        pred, spot_q, gene_q = stats(kept, came, sums, spatial, mask8, onehot, q)
        preds.append(pred)
        spot_stats.append(spot_q)
        gene_stats = gene_stats + gene_q
    spot_stats = add_all(jnp.concatenate(spot_stats, axis=1), "cell")
    mass = mass_rows(sums, mparts)[:1].reshape(-1, shard)
    joint = add_all(jnp.concatenate([gene_stats, mass], axis=0), "spot")
    gene_stats = joint[:24]
    mass = joint[24:].reshape(1, rows) / spots_total
    density_part = -jnp.sum(jnp.log(cells_total * mass)) / cells_total
    dens = jnp.broadcast_to(-1.0 / (cells_total * spots_total * mass), (8, rows))

    heights = (shard // 4,) * 4
    *grads, inner, losses = gradient(
        preds, sums, spatial, mask8, onehot, counts8, gene_stats, spot_stats, heights, slides, spots_total
    )

    pparts = exp_split(other_logits)[:2]
    inner = inner + pull_cols(dens, sums, mparts)
    first = jnp.broadcast_to(density_part - losses[0, 0], (8, 128))
    tail = add_all(jnp.concatenate([inner, first], axis=1), "cell")
    inner = tail[:, :cols]
    loss = tail[0, cols] - add_all(jnp.broadcast_to(losses[0, 1], (8, 128)), "spot")[0, 0]

    blocks = spots_n // 2
    far_w = jnp.arange(blocks, dtype=jnp.int32)[:, None] << 1
    wanted = ((mine ^ far_w) * per_block + jnp.arange(per_block, dtype=jnp.int32)[None, :]) ^ me
    wanted = wanted.reshape(-1)
    place = reverse(wanted, cell_bits)
    low_bits = cell_bits - block_bits - 1
    short = ((place >> (low_bits + 1)) << low_bits) | (place & ((1 << low_bits) - 1))
    ids = jnp.concatenate([place, short]).astype(jnp.int32)
    core_bit = ((me >> block_bits) ^ mine) & 1

    gathered, pairs = [], []
    for q, height in enumerate(heights):
        near = grads[q]
        for bit in range(cell_bits - 1, 0, -1):
            near = jnp.concatenate([near, swap(near, "cell", bit)], axis=0)
        far = swap(near, "cell", 0)
        gathered += [near, far]

        def part(v):
            v = v.reshape(1 << (block_bits - 1), 2, 1 << low_bits, height, cols)
            return lax.dynamic_index_in_dim(v, 1 - core_bit, 1, keepdims=False).reshape(-1, cols)

        across = swap(jnp.concatenate([part(near), part(far)], axis=0), "spot", 0)
        outs = expr_part(ids, near, far, across, mparts, pparts, height, blocks, wanted.size)
        outs = list(outs)
        bit = spots_n.bit_length() - 2
        while len(outs) > 2:
            half = len(outs) // 2
            came = swap(jnp.concatenate(outs[half:], axis=1), "spot", bit)
            came = jnp.split(came, half, axis=1)
            outs = [a + b for a, b in zip(outs[:half], came)]
            bit -= 1
        pairs.append((outs[0], swap(outs[1], "spot", bit)))

    logit_grad = logit_part(dens, sums, inner, eparts, mparts, gathered, heights, cells, scale)
    expr_grad = join(pairs, heights, per_block, scale)
    return (loss, logit_grad, expr_grad)


def solution(mesh):
    placed = (P("cell", "spot"), P("cell", None), P("cell", "spot"), P(), P("spot"), P())
    return jax.shard_map(
        on_device,
        mesh=mesh,
        in_specs=placed,
        out_specs=(P(), P("cell", "spot"), P("cell", "spot")),
        check_vma=False,
    )
```

time: 691 us -> 459 us (0.66)
  matrix products: 216 us -> 0 us
  Pallas kernels: 0 us -> 173 us
  blocking collectives: 145 us -> 0 us
  waiting for transfers between devices: 261 us -> 167 us
  starting transfers between devices: 0.3 us -> 56.8 us
  local copies, waits for them, and re-layouts: 21.4 us -> 43.8 us
  other arithmetic: 31.1 us -> 11 us
  between operations: 15.8 us -> 5.08 us
    dot_general x9 -> x0, matrix products: 216 us -> none  [the longest x1 73.3 us: on_device(): jnp.dot(columns, section, precision=lax.Precision.HIGHEST)]
    pallas_call x0 -> x24, Pallas kernels: none -> 173 us  [the longest x4 46.8 us: expr_part(): pl.pallas_call(functools.partial(expr_body, number, height, half), grid_s...]
    ppermute x0 -> x46, waiting for transfers between devices: none -> 167 us  [swap(): return lax.ppermute(v, axis, [(i, i ^ 1 << bit) for i in range(size)])]
    reduce_scatter x2 -> x0, waiting for transfers between devices: 138 us -> none  [the longest x1 138 us: on_device(): lax.psum_scatter(lax.dot_general(columns, mapping, (((0,), (0,)), ((), ()...]
    all_gather x1 -> x0, waiting for transfers between devices: 123 us -> none  [on_device(): section = lax.all_gather(dpred, 'cell', axis=0, tiled=True)]
    psum x5 -> x0, blocking collectives: 122 us -> none  [the longest x1 38.7 us: on_device(): loss = lax.psum(pieces, ('cell', 'spot'))]
    ppermute x0 -> x46, starting transfers between devices: none -> 56.8 us  [swap(): return lax.ppermute(v, axis, [(i, i ^ 1 << bit) for i in range(size)])]
    pmax x1 -> x0, blocking collectives: 23.1 us -> none  [on_device(): col_top = lax.pmax(jnp.max(logits, axis=0), 'cell')]
  transfers between devices with their start and end apart: 3 -> 46, of which waited for: 2 -> 22; matrix products, arithmetic and copies ran while one was open for 15% -> 3% of each run, Pallas kernels for 0% -> 37%
where the time goes in v1:
time: 459 us; the launch traced here: 457 us
  Pallas kernels  173 us (38%)
  waiting for transfers between devices  167 us (36%)
  starting transfers between devices  56.8 us (12%)
  local copies, waits for them, and re-layouts  43.8 us (10%)
  other arithmetic  11 us (2%)
  between operations  5.08 us (1%)
    ppermute x46, waiting for transfers between devices, swap(): return lax.ppermute(v, axis, [(i, i ^ 1 << bit) for i in range(size)])  167 us
    ppermute x46, starting transfers between devices, swap(): return lax.ppermute(v, axis, [(i, i ^ 1 << bit) for i in range(size)])  56.8 us
    pallas_call x4, Pallas kernels, expr_part(): pl.pallas_call(functools.partial(expr_body, number, height, half), grid_s...  46.8 us
    unnamed x84, local copies, waits for them, and re-layouts  40.8 us
    pallas_call x1, Pallas kernels, logit_part(): pl.pallas_call(functools.partial(logit_body, pieces, heights, scale), gri...  34.4 us
    pallas_call x4, Pallas kernels, predict(): pl.pallas_call(send_body, grid=(count,), in_specs=[etile, etile, mtile, m...  27.9 us
    pallas_call x4, Pallas kernels, predict(): pl.pallas_call(functools.partial(keep_body, half), grid=(count,), in_spec...  26 us
    pallas_call x1, Pallas kernels, part_split(): pl.pallas_call(part_body, grid_spec=pltpu.PrefetchScalarGridSpec(num_scal...  14.5 us
  transfers between devices with their start and end apart: 46, of which 22 were waited for; matrix products, arithmetic and copies ran while one was open for 3% of the time, Pallas kernels for 37%

profile of v1, /device:TPU:0, one launch (start us, length us, event | category | flops | bytes accessed | tf_op | source)
XLA Modules:
  0.0 457.0 jit_solution(3428416261306661072)
XLA Ops:
  11.0 14.5 %shard_map.85 = (bf16[2048,2048]{1,0:T(8,128)(2,1)S(1)}, bf16[2048,2048]{1,0:T(8,128)(2,1)S(1)}) custom-call(s32[8]{0:T(128)S(1)} %fusion.7.order, f32[2048,2048]{1,0:T(8,128)} %source.1), custom_call_target="tpu_custom_call" | custom-call | flops 16777216 | bytes 33554432 | tf_op jit(solution)/shard_map/pallas_call | solution.py:85
  32.2 7.2 %shard_map.87 = f32[1024,256]{1,0:T(8,128)} custom-call(bf16[2048,2048]{1,0:T(8,128)(2,1)} %copy-done, bf16[2048,2048]{1,0:T(8,128)(2,1)} %copy-done.1, bf16[2048,1024]{1,0:T(8,128)(2,1)S(1)} %copy-done.3, bf16[2048,1024]{1,0:T(8,128)(2,1)S(1)} %copy-done.9), custom_call_target="tpu_custom_call" | custom-call | flops 3221225472 | bytes 11534336 | tf_op jit(solution)/shard_map/pallas_call | solution.py:122
  41.9 7.2 %shard_map.90 = f32[1024,256]{1,0:T(8,128)} custom-call(bf16[2048,2048]{1,0:T(8,128)(2,1)} %copy-done, bf16[2048,2048]{1,0:T(8,128)(2,1)} %copy-done.1, bf16[2048,1024]{1,0:T(8,128)(2,1)S(1)} %copy-done.3, bf16[2048,1024]{1,0:T(8,128)(2,1)S(1)} %copy-done.9), custom_call_target="tpu_custom_call" | custom-call | flops 3221225472 | bytes 11534336 | tf_op jit(solution)/shard_map/pallas_call | solution.py:122
  51.2 7.2 %shard_map.93 = f32[1024,256]{1,0:T(8,128)} custom-call(bf16[2048,2048]{1,0:T(8,128)(2,1)} %copy-done, bf16[2048,2048]{1,0:T(8,128)(2,1)} %copy-done.1, bf16[2048,1024]{1,0:T(8,128)(2,1)S(1)} %copy-done.3, bf16[2048,1024]{1,0:T(8,128)(2,1)S(1)} %copy-done.9), custom_call_target="tpu_custom_call" | custom-call | flops 3221225472 | bytes 11534336 | tf_op jit(solution)/shard_map/pallas_call | solution.py:122
  84.0 6.6 %shard_map.88 = (f32[512,256]{1,0:T(8,128)S(1)}, f32[512,256]{1,0:T(8,128)S(1)}) custom-call(bf16[2048,2048]{1,0:T(8,128)(2,1)} %copy-done, bf16[2048,2048]{1,0:T(8,128)(2,1)} %copy-done.1, bf16[2048,1024]{1,0:T(8,128)(2,1)S(1)} %copy-done.5, bf16[2048,1024]{1,0:T(8,128)(2,1)S(1)} %copy-done.11, f32[1024,256]{1,0:T(8,128)} %collective-permute-done.add), custom_call_target="tpu_custom_call" | custom-call | flops 3221225472 | bytes 11534336 | tf_op jit(solution)/shard_map/pallas_call | solution.py:132
  113.8 6.6 %shard_map.97 = (f32[512,256]{1,0:T(8,128)S(1)}, f32[512,256]{1,0:T(8,128)S(1)}) custom-call(bf16[2048,2048]{1,0:T(8,128)(2,1)} %copy-done, bf16[2048,2048]{1,0:T(8,128)(2,1)} %copy-done.1, bf16[2048,1024]{1,0:T(8,128)(2,1)S(1)} %copy-done.5, bf16[2048,1024]{1,0:T(8,128)(2,1)S(1)} %copy-done.11, f32[1024,256]{1,0:T(8,128)S(1)} %collective-permute-done.12.add), custom_call_target="tpu_custom_call" | custom-call | flops 3221225472 | bytes 11534336 | tf_op jit(solution)/shard_map/pallas_call | solution.py:132
  126.4 8.6 %collective-permute-done.10 = f32[512,256]{1,0:T(8,128)S(1)} collective-permute-done((f32[512,256]{1,0:T(8,128)S(1)}, f32[512,256]{1,0:T(8,128)S(1)}, u32[]{:S(2)}, u32[]{:S(2)}) %collective-permute-start.10) | collective-permute-done | bytes 524320 | tf_op jit(solution)/shard_map/ppermute | solution.py:397
  137.7 7.6 %collective-permute-done.13 = f32[512,256]{1,0:T(8,128)S(1)} collective-permute-done((f32[512,256]{1,0:T(8,128)S(1)}, f32[512,256]{1,0:T(8,128)S(1)}, u32[]{:S(2)}, u32[]{:S(2)}) %collective-permute-start.13) | collective-permute-done | bytes 524320 | tf_op jit(solution)/shard_map/ppermute | solution.py:397
  158.8 7.0 %collective-permute-done.8.came = f32[256,256]{1,0:T(8,128)S(1)} collective-permute-done((f32[256,256]{1,0:T(8,128)}, f32[256,256]{1,0:T(8,128)S(1)}, u32[]{:S(2)}, u32[]{:S(2)}) %collective-permute-start.8) | collective-permute-done | bytes 262176 | tf_op jit(solution)/shard_map/ppermute | solution.py:397
  206.8 11.5 %collective-permute-done.25 = f32[64,1024]{1,0:T(8,128)S(1)} collective-permute-done((f32[64,1024]{1,0:T(8,128)S(1)}, f32[64,1024]{1,0:T(8,128)S(1)}, u32[]{:S(2)}, u32[]{:S(2)}) %collective-permute-start.25) | collective-permute-done | bytes 262176 | tf_op jit(solution)/shard_map/ppermute | solution.py:397
  222.6 13.0 %collective-permute-done.22 = f32[8,1152]{1,0:T(8,128)S(1)} collective-permute-done((f32[8,1152]{1,0:T(8,128)S(1)}, f32[8,1152]{1,0:T(8,128)S(1)}, u32[]{:S(2)}, u32[]{:S(2)}) %collective-permute-start.22) | collective-permute-done | bytes 36896 | tf_op jit(solution)/shard_map/ppermute | solution.py:397
  251.1 8.7 %collective-permute-done.29 = f32[128,1024]{1,0:T(8,128)S(1)} collective-permute-done((f32[128,1024]{1,0:T(8,128)S(1)}, f32[128,1024]{1,0:T(8,128)S(1)}, u32[]{:S(2)}, u32[]{:S(2)}) %collective-permute-start.29) | collective-permute-done | bytes 524320 | tf_op jit(solution)/shard_map/ppermute | solution.py:397
  262.1 8.9 %collective-permute-done.32 = f32[128,1024]{1,0:T(8,128)S(1)} collective-permute-done((f32[128,1024]{1,0:T(8,128)S(1)}, f32[128,1024]{1,0:T(8,128)S(1)}, u32[]{:S(2)}, u32[]{:S(2)}) %collective-permute-start.32) | collective-permute-done | bytes 524320 | tf_op jit(solution)/shard_map/ppermute | solution.py:397
  273.4 7.2 %collective-permute-done.35 = f32[128,1024]{1,0:T(8,128)S(1)} collective-permute-done((f32[128,1024]{1,0:T(8,128)S(1)}, f32[128,1024]{1,0:T(8,128)S(1)}, u32[]{:S(2)}, u32[]{:S(2)}) %collective-permute-start.35) | collective-permute-done | bytes 524320 | tf_op jit(solution)/shard_map/ppermute | solution.py:397
  283.8 7.6 %collective-permute-done.30.refs_3_.far = f32[256,1024]{1,0:T(8,128)S(1)} collective-permute-done((f32[256,1024]{1,0:T(8,128)S(1)}, f32[256,1024]{1,0:T(8,128)S(1)}, u32[]{:S(2)}, u32[]{:S(2)}) %collective-permute-start.30) | collective-permute-done | bytes 1048608 | tf_op jit(solution)/shard_map/ppermute | solution.py:397
  292.7 21.2 %collective-permute-done.33.refs_5_.far = f32[256,1024]{1,0:T(8,128)S(1)} collective-permute-done((f32[256,1024]{1,0:T(8,128)S(1)}, f32[256,1024]{1,0:T(8,128)S(1)}, u32[]{:S(2)}, u32[]{:S(2)}) %collective-permute-start.33) | collective-permute-done | bytes 1048608 | tf_op jit(solution)/shard_map/ppermute | solution.py:397
  315.2 20.2 %collective-permute-done.36.refs_7_.far = f32[256,1024]{1,0:T(8,128)S(1)} collective-permute-done((f32[256,1024]{1,0:T(8,128)S(1)}, f32[256,1024]{1,0:T(8,128)S(1)}, u32[]{:S(2)}, u32[]{:S(2)}) %collective-permute-start.36) | collective-permute-done | bytes 1048608 | tf_op jit(solution)/shard_map/ppermute | solution.py:397
  336.7 7.2 %shard_map.103 = (bf16[2048,1024]{1,0:T(8,128)(2,1)S(1)}, bf16[2048,1024]{1,0:T(8,128)(2,1)S(1)}, f32[8,1024]{1,0:T(8,128)}) custom-call(f32[2048,1024]{1,0:T(8,128)} %collective-permute-done.38.logits), custom_call_target="tpu_custom_call" | custom-call | flops 20971520 | bytes 16777216 | tf_op jit(solution)/shard_map/pallas_call | solution.py:62
  347.9 11.7 %shard_map.104 = (f32[2048,128]{1,0:T(8,128)S(1)}, f32[2048,128]{1,0:T(8,128)}) custom-call(s32[8]{0:T(128)S(1)} %pad_add_fusion.ids, f32[256,1024]{1,0:T(8,128)S(1)} %constant_dynamic-update-slice_fusion.4.refs_0_.near, f32[256,1024]{1,0:T(8,128)S(1)} %collective-permute-done.27.refs_1_.far, f32[256,1024]{1,0:T(8,128)S(1)} %collective-permute-done.37.across, ...), custom_call_target="tpu_custom_call" | custom-call | flops 6442450944 | bytes 16777216 | tf_op jit(solution)/shard_map/pallas_call | solution.py:310
  361.0 11.9 %shard_map.105 = (f32[2048,128]{1,0:T(8,128)S(1)}, f32[2048,128]{1,0:T(8,128)}) custom-call(s32[8]{0:T(128)S(1)} %pad_add_fusion.ids, f32[256,1024]{1,0:T(8,128)S(1)} %constant_dynamic-update-slice_fusion.7.refs_2_.near, f32[256,1024]{1,0:T(8,128)S(1)} %collective-permute-done.30.refs_3_.far, f32[256,1024]{1,0:T(8,128)S(1)} %collective-permute-done.40.across, ...), custom_call_target="tpu_custom_call" | custom-call | flops 6442450944 | bytes 16777216 | tf_op jit(solution)/shard_map/pallas_call | solution.py:310
  375.9 11.7 %shard_map.106 = (f32[2048,128]{1,0:T(8,128)S(1)}, f32[2048,128]{1,0:T(8,128)}) custom-call(s32[8]{0:T(128)S(1)} %pad_add_fusion.ids, f32[256,1024]{1,0:T(8,128)S(1)} %constant_dynamic-update-slice_fusion.10.refs_4_.near, f32[256,1024]{1,0:T(8,128)S(1)} %copy-done.26, f32[256,1024]{1,0:T(8,128)S(1)} %copy-done.32, bf16[2048,1024]{1,0:T(8,128)(2,1)} %copy-done.2, ...), custom_call_target="tpu_custom_call" | custom-call | flops 6442450944 | bytes 16777216 | tf_op jit(solution)/shard_map/pallas_call | solution.py:310
  388.9 11.5 %shard_map.107 = (f32[2048,128]{1,0:T(8,128)S(1)}, f32[2048,128]{1,0:T(8,128)S(1)}) custom-call(s32[8]{0:T(128)S(1)} %pad_add_fusion.ids, f32[256,1024]{1,0:T(8,128)S(1)} %constant_dynamic-update-slice_fusion.13.refs_6_.near, f32[256,1024]{1,0:T(8,128)S(1)} %copy-done.28, f32[256,1024]{1,0:T(8,128)} %collective-permute-done.44.across, ...), custom_call_target="tpu_custom_call" | custom-call | flops 6442450944 | bytes 16777216 | tf_op jit(solution)/shard_map/pallas_call | solution.py:310
  401.2 34.4 %shard_map.102 = f32[2048,1024]{1,0:T(8,128)} custom-call(f32[8,2048]{1,0:T(8,128)S(1)} %broadcast_in_dim.7.dens, f32[8,1024]{1,0:T(8,128)S(1)} %add.129.sums.refs_4_, f32[8,1024]{1,0:T(8,128)S(1)} %slice.108.inner, bf16[2048,2048]{1,0:T(8,128)(2,1)} %copy-done, bf16[2048,2048]{1,0:T(8,128)(2,1)} %copy-done.1, bf16[2048,1024]{1,0:T(8,128)(2,1)} %copy-done.2, ...), custom_call_target="tpu_custom_call" | custom-call | flops 25769803776 | bytes 33554432 | tf_op jit(solution)/shard_map/pallas_call | solution.py:353
  435.6 17.3 %collective-permute-done.45.refs_7_ = f32[2048,128]{1,0:T(8,128)S(1)} collective-permute-done((f32[2048,128]{1,0:T(8,128)S(1)}, f32[2048,128]{1,0:T(8,128)S(1)}, u32[]{:S(2)}, u32[]{:S(2)}) %collective-permute-start.45) | collective-permute-done | bytes 1048608 | tf_op jit(solution)/shard_map/ppermute | solution.py:397
  (240 shorter events, 175.5 us)
Async XLA Ops:
  0.6 336.0 %collective-permute-start.38 = (f32[2048,1024]{1,0:T(8,128)}, f32[2048,1024]{1,0:T(8,128)}, u32[]{:S(2)}, u32[]{:S(2)}) collective-permute-start(f32[2048,1024]{1,0:T(8,128)} %logits.1), channel_id=1, source_target_pairs={{0,1},{1,0},{2,3},{3,2},{4,5},{5,4},{6,7},{7,6},{8,9},{9,8},{10,11... | collective-permute-start | bytes 25165832 | tf_op jit(solution)/shard_map/ppermute | solution.py:397
  39.4 37.6 %collective-permute-start = (f32[1024,256]{1,0:T(8,128)}, f32[1024,256]{1,0:T(8,128)}, u32[]{:S(2)}, u32[]{:S(2)}) collective-permute-start(f32[1024,256]{1,0:T(8,128)} %shard_map.87), channel_id=1, source_target_pairs={{0,4},{4,0},{8,12},{12,8},{16,20},{20,16},{24,28},{28,24},{1,5},{5... | collective-permute-start | bytes 3145736 | tf_op jit(solution)/shard_map/ppermute | solution.py:397
  41.9 28.8 %collective-permute-start.3 = (f32[8,1024]{1,0:T(8,128)S(1)}, f32[8,1024]{1,0:T(8,128)S(1)}, u32[]{:S(2)}, u32[]{:S(2)}) collective-permute-start(f32[8,1024]{1,0:T(8,128)S(1)} %get-tuple-element.50), channel_id=1, source_target_pairs={{0,4},{4,0},{8,12},{12,8},{16,20},{20,16},{24,28},{28,24},{1,5},{5... | collective-permute-start | bytes 98312 | tf_op jit(solution)/shard_map/ppermute | solution.py:397
  49.1 41.5 %collective-permute-start.6 = (f32[1024,256]{1,0:T(8,128)}, f32[1024,256]{1,0:T(8,128)S(1)}, u32[]{:S(2)}, u32[]{:S(2)}) collective-permute-start(f32[1024,256]{1,0:T(8,128)} %shard_map.90), channel_id=1, source_target_pairs={{0,8},{4,12},{8,0},{12,4},{16,24},{20,28},{24,16},{28,20},{1,9},{5... | collective-permute-start | bytes 3145736 | tf_op jit(solution)/shard_map/ppermute | solution.py:397
  58.3 40.4 %collective-permute-start.9 = (f32[1024,256]{1,0:T(8,128)}, f32[1024,256]{1,0:T(8,128)S(1)}, u32[]{:S(2)}, u32[]{:S(2)}) collective-permute-start(f32[1024,256]{1,0:T(8,128)} %shard_map.93), channel_id=1, source_target_pairs={{0,4},{4,0},{8,12},{12,8},{16,20},{20,16},{24,28},{28,24},{1,5},{5... | collective-permute-start | bytes 3145736 | tf_op jit(solution)/shard_map/ppermute | solution.py:397
  75.3 36.4 %collective-permute-start.12 = (f32[1024,256]{1,0:T(8,128)S(1)}, f32[1024,256]{1,0:T(8,128)S(1)}, u32[]{:S(2)}, u32[]{:S(2)}) collective-permute-start(f32[1024,256]{1,0:T(8,128)S(1)} %shard_map.96), channel_id=1, source_target_pairs={{0,4},{4,0},{8,12},{12,8},{16,20},{20,16},{24,28},{28,24},{1,5},{5... | collective-permute-start | bytes 3145736 | tf_op jit(solution)/shard_map/ppermute | solution.py:397
  77.0 70.6 %collective-permute-start.5 = (f32[8,1024]{1,0:T(8,128)S(1)}, f32[8,1024]{1,0:T(8,128)S(1)}, u32[]{:S(2)}, u32[]{:S(2)}) collective-permute-start(f32[8,1024]{1,0:T(8,128)S(1)} %add.128), channel_id=1, source_target_pairs={{0,16},{4,20},{8,24},{12,28},{16,0},{20,4},{24,8},{28,12},{1,17},{... | collective-permute-start | bytes 98312 | tf_op jit(solution)/shard_map/ppermute | solution.py:397
  90.6 29.7 %collective-permute-start.1 = (f32[512,256]{1,0:T(8,128)S(1)}, f32[512,256]{1,0:T(8,128)S(1)}, u32[]{:S(2)}, u32[]{:S(2)}) collective-permute-start(f32[512,256]{1,0:T(8,128)S(1)} %get-tuple-element.49), channel_id=1, source_target_pairs={{0,8},{4,12},{8,0},{12,4},{16,24},{20,28},{24,16},{28,20},{1,9},{5... | collective-permute-start | bytes 1572872 | tf_op jit(solution)/shard_map/ppermute | solution.py:397
  122.8 35.3 %collective-permute-start.2 = (f32[256,256]{1,0:T(8,128)}, f32[256,256]{1,0:T(8,128)S(1)}, u32[]{:S(2)}, u32[]{:S(2)}) collective-permute-start(f32[256,256]{1,0:T(8,128)} %get-tuple-element.91), channel_id=1, source_target_pairs={{0,16},{4,20},{8,24},{12,28},{16,0},{20,4},{24,8},{28,12},{1,17},{... | collective-permute-start | bytes 786440 | tf_op jit(solution)/shard_map/ppermute | solution.py:397
  135.0 30.9 %collective-permute-start.8 = (f32[256,256]{1,0:T(8,128)}, f32[256,256]{1,0:T(8,128)S(1)}, u32[]{:S(2)}, u32[]{:S(2)}) collective-permute-start(f32[256,256]{1,0:T(8,128)} %get-tuple-element.89), channel_id=1, source_target_pairs={{0,16},{4,20},{8,24},{12,28},{16,0},{20,4},{24,8},{28,12},{1,17},{... | collective-permute-start | bytes 786440 | tf_op jit(solution)/shard_map/ppermute | solution.py:397
  199.8 41.1 %collective-permute-start.28 = (f32[64,1024]{1,0:T(8,128)S(1)}, f32[64,1024]{1,0:T(8,128)}, u32[]{:S(2)}, u32[]{:S(2)}) collective-permute-start(f32[64,1024]{1,0:T(8,128)S(1)} %get-tuple-element.72), channel_id=1, source_target_pairs={{0,16},{4,20},{8,24},{12,28},{16,0},{20,4},{24,8},{28,12},{1,17},{... | collective-permute-start | bytes 786440 | tf_op jit(solution)/shard_map/ppermute | solution.py:397
  242.9 40.5 %collective-permute-start.27 = (f32[256,1024]{1,0:T(8,128)S(1)}, f32[256,1024]{1,0:T(8,128)S(1)}, u32[]{:S(2)}, u32[]{:S(2)}) collective-permute-start(f32[256,1024]{1,0:T(8,128)S(1)} %constant_dynamic-update-slice_fusion.4.refs_0_.near), channel_id=1, source_target_pairs={{0,4},{4,0},{8,12},{12,8},{16,20},{20,16},{24,28},{28,24},{1,5},{5... | collective-permute-start | bytes 3145736 | tf_op jit(solution)/shard_map/ppermute | solution.py:397
  250.0 30.6 %collective-permute-start.35 = (f32[128,1024]{1,0:T(8,128)S(1)}, f32[128,1024]{1,0:T(8,128)S(1)}, u32[]{:S(2)}, u32[]{:S(2)}) collective-permute-start(f32[128,1024]{1,0:T(8,128)S(1)} %pad_maximum_fusion.7), channel_id=1, source_target_pairs={{0,8},{4,12},{8,0},{12,4},{16,24},{20,28},{24,16},{28,20},{1,9},{5... | collective-permute-start | bytes 1572872 | tf_op jit(solution)/shard_map/ppermute | solution.py:397
  259.8 31.6 %collective-permute-start.30 = (f32[256,1024]{1,0:T(8,128)S(1)}, f32[256,1024]{1,0:T(8,128)S(1)}, u32[]{:S(2)}, u32[]{:S(2)}) collective-permute-start(f32[256,1024]{1,0:T(8,128)S(1)} %constant_dynamic-update-slice_fusion.7.refs_2_.near), channel_id=1, source_target_pairs={{0,4},{4,0},{8,12},{12,8},{16,20},{20,16},{24,28},{28,24},{1,5},{5... | collective-permute-start | bytes 3145736 | tf_op jit(solution)/shard_map/ppermute | solution.py:397
  271.1 42.8 %collective-permute-start.33 = (f32[256,1024]{1,0:T(8,128)S(1)}, f32[256,1024]{1,0:T(8,128)S(1)}, u32[]{:S(2)}, u32[]{:S(2)}) collective-permute-start(f32[256,1024]{1,0:T(8,128)S(1)} %constant_dynamic-update-slice_fusion.10.refs_4_.near), channel_id=1, source_target_pairs={{0,4},{4,0},{8,12},{12,8},{16,20},{20,16},{24,28},{28,24},{1,5},{5... | collective-permute-start | bytes 3145736 | tf_op jit(solution)/shard_map/ppermute | solution.py:397
  280.7 54.7 %collective-permute-start.36 = (f32[256,1024]{1,0:T(8,128)S(1)}, f32[256,1024]{1,0:T(8,128)S(1)}, u32[]{:S(2)}, u32[]{:S(2)}) collective-permute-start(f32[256,1024]{1,0:T(8,128)S(1)} %constant_dynamic-update-slice_fusion.13.refs_6_.near), channel_id=1, source_target_pairs={{0,4},{4,0},{8,12},{12,8},{16,20},{20,16},{24,28},{28,24},{1,5},{5... | collective-permute-start | bytes 3145736 | tf_op jit(solution)/shard_map/ppermute | solution.py:397
  283.5 64.4 %collective-permute-start.37 = (f32[256,1024]{1,0:T(8,128)S(1)}, f32[256,1024]{1,0:T(8,128)S(1)}, u32[]{:S(2)}, u32[]{:S(2)}) collective-permute-start(f32[256,1024]{1,0:T(8,128)S(1)} %pad_maximum_fusion), channel_id=1, source_target_pairs={{0,1},{1,0},{2,3},{3,2},{4,5},{5,4},{6,7},{7,6},{8,9},{9,8},{10,11... | collective-permute-start | bytes 3145736 | tf_op jit(solution)/shard_map/ppermute | solution.py:397
  292.7 68.3 %collective-permute-start.40 = (f32[256,1024]{1,0:T(8,128)}, f32[256,1024]{1,0:T(8,128)S(1)}, u32[]{:S(2)}, u32[]{:S(2)}) collective-permute-start(f32[256,1024]{1,0:T(8,128)} %pad_maximum_fusion.1), channel_id=1, source_target_pairs={{0,1},{1,0},{2,3},{3,2},{4,5},{5,4},{6,7},{7,6},{8,9},{9,8},{10,11... | collective-permute-start | bytes 3145736 | tf_op jit(solution)/shard_map/ppermute | solution.py:397
  315.2 58.4 %collective-permute-start.42 = (f32[256,1024]{1,0:T(8,128)}, f32[256,1024]{1,0:T(8,128)S(1)}, u32[]{:S(2)}, u32[]{:S(2)}) collective-permute-start(f32[256,1024]{1,0:T(8,128)} %pad_maximum_fusion.2), channel_id=1, source_target_pairs={{0,1},{1,0},{2,3},{3,2},{4,5},{5,4},{6,7},{7,6},{8,9},{9,8},{10,11... | collective-permute-start | bytes 3145736 | tf_op jit(solution)/shard_map/ppermute | solution.py:397
  336.7 52.2 %collective-permute-start.44 = (f32[256,1024]{1,0:T(8,128)}, f32[256,1024]{1,0:T(8,128)}, u32[]{:S(2)}, u32[]{:S(2)}) collective-permute-start(f32[256,1024]{1,0:T(8,128)} %pad_maximum_fusion.3), channel_id=1, source_target_pairs={{0,1},{1,0},{2,3},{3,2},{4,5},{5,4},{6,7},{7,6},{8,9},{9,8},{10,11... | collective-permute-start | bytes 3145736 | tf_op jit(solution)/shard_map/ppermute | solution.py:397
  359.6 75.9 %collective-permute-start.39 = (f32[2048,128]{1,0:T(8,128)}, f32[2048,128]{1,0:T(8,128)S(1)}, u32[]{:S(2)}, u32[]{:S(2)}) collective-permute-start(f32[2048,128]{1,0:T(8,128)} %get-tuple-element.78), channel_id=1, source_target_pairs={{0,2},{1,3},{2,0},{3,1},{4,6},{5,7},{6,4},{7,5},{8,10},{9,11},{10,... | collective-permute-start | bytes 3145736 | tf_op jit(solution)/shard_map/ppermute | solution.py:397
  372.9 62.7 %collective-permute-start.41 = (f32[2048,128]{1,0:T(8,128)}, f32[2048,128]{1,0:T(8,128)S(1)}, u32[]{:S(2)}, u32[]{:S(2)}) collective-permute-start(f32[2048,128]{1,0:T(8,128)} %get-tuple-element.80), channel_id=1, source_target_pairs={{0,2},{1,3},{2,0},{3,1},{4,6},{5,7},{6,4},{7,5},{8,10},{9,11},{10,... | collective-permute-start | bytes 3145736 | tf_op jit(solution)/shard_map/ppermute | solution.py:397
  387.5 48.0 %collective-permute-start.43 = (f32[2048,128]{1,0:T(8,128)}, f32[2048,128]{1,0:T(8,128)S(1)}, u32[]{:S(2)}, u32[]{:S(2)}) collective-permute-start(f32[2048,128]{1,0:T(8,128)} %get-tuple-element.82), channel_id=1, source_target_pairs={{0,2},{1,3},{2,0},{3,1},{4,6},{5,7},{6,4},{7,5},{8,10},{9,11},{10,... | collective-permute-start | bytes 3145736 | tf_op jit(solution)/shard_map/ppermute | solution.py:397
  400.4 52.4 %collective-permute-start.45 = (f32[2048,128]{1,0:T(8,128)S(1)}, f32[2048,128]{1,0:T(8,128)S(1)}, u32[]{:S(2)}, u32[]{:S(2)}) collective-permute-start(f32[2048,128]{1,0:T(8,128)S(1)} %get-tuple-element.84), channel_id=1, source_target_pairs={{0,2},{1,3},{2,0},{3,1},{4,6},{5,7},{6,4},{7,5},{8,10},{9,11},{10,... | collective-permute-start | bytes 3145736 | tf_op jit(solution)/shard_map/ppermute | solution.py:397
  (59 other events, 1189.2 us)

commit v2 on v1

v2 whole, which is shorter than its diff:
```python
import functools

import jax
import jax.numpy as jnp
from jax import lax
from jax.experimental import pallas as pl
from jax.experimental.pallas import tpu as pltpu
from jax.sharding import PartitionSpec as P

eps = 1e-06
F32 = jnp.float32
BF16 = jnp.bfloat16
MIB = 1024 * 1024


def shape_of(*dims, dtype=F32):
    return jax.ShapeDtypeStruct(dims, dtype)


def hbm(*dims):
    return pltpu.HBM(dims[:-1], dims[-1])


def after(value, *others):
    return lax.optimization_barrier((value, *others))[0]


def params(mib):
    return pltpu.CompilerParams(vmem_limit_bytes=mib * MIB)


def split(v):
    high = v.astype(BF16)
    return high, (v - high.astype(F32)).astype(BF16)


def dot(a, b, ca, cb, precision=None):
    return lax.dot_general(
        a, b, (((ca,), (cb,)), ((), ())), precision=precision, preferred_element_type=F32
    )


def dot3(ah, al, bh, bl, ca, cb):
    return dot(ah, bh, ca, cb) + dot(al, bh, ca, cb) + dot(ah, bl, ca, cb)


def exact(a, b, ca, cb):
    return dot(a, b, ca, cb, lax.Precision.HIGHEST)


def cost(flops, nbytes):
    return pl.CostEstimate(flops=0, bytes_accessed=0, transcendentals=0)


def simple(body, outs, *args, prefetch=None):
    def spec(v):
        return pl.BlockSpec(v.shape, lambda i, *_: (0,) * len(v.shape))

    number = 0 if prefetch is None else 1
    return pl.pallas_call(
        body,
        grid_spec=pltpu.PrefetchScalarGridSpec(
            num_scalar_prefetch=number,
            grid=(1,),
            in_specs=[spec(a) for a in args],
            out_specs=[spec(o) for o in outs],
        ),
        out_shape=list(outs),
        compiler_params=params(32),
        cost_estimate=cost(0, 0),
    )(*([] if prefetch is None else [prefetch]), *args)


def add_body(a, b, out):
    out[...] = a[...] + b[...]


def add(a, b):
    return simple(add_body, [shape_of(*a.shape)], a, b)[0]


def add_split_body(kept, came, low, high):
    if len(kept.shape) == 3:
        low[...], high[...] = kept[0] + came[0], kept[1] + came[1]
    else:
        half = kept.shape[1] // 2
        low[...] = kept[:, :half] + came[:, :half]
        high[...] = kept[:, half:] + came[:, half:]


def add_split(kept, came):
    rows, cols = kept.shape[-2:]
    out = shape_of(rows, cols if kept.ndim == 3 else cols // 2)
    return simple(add_split_body, [out, out], kept, came)


def glue_body(*refs):
    *sources, out = refs
    at = 0
    for source in sources:
        out[at : at + source.shape[0], :] = source[...]
        at += source.shape[0]


def glue(*parts):
    return simple(glue_body, [shape_of(sum(p.shape[0] for p in parts), parts[0].shape[1])], *parts)[0]


def pick_body(outer, size, which, *refs):
    *sources, out = refs
    at = 0
    for source in sources:
        for n in range(outer):
            start = pl.multiple_of((2 * n + which[0]) * size, 8)
            out[at : at + size, :] = source[pl.ds(start, size), :]
            at += size


def pick(which, outer, size, *sources):
    out = shape_of(outer * size * len(sources), sources[0].shape[1])
    body = functools.partial(pick_body, outer, size)
    return simple(body, [out], *sources, prefetch=which)[0]


def exp_body(with_sums, logits, high, low, *sums):
    vals = jnp.exp(logits[...])
    high[...], low[...] = split(vals)
    if with_sums:

        @pl.when(pl.program_id(0) == 0)
        def _():
            sums[0][...] = jnp.zeros_like(sums[0])

        sums[0][...] += jnp.sum(vals.reshape(-1, 8, vals.shape[1]), axis=0)


def exp_split(logits, with_sums):
    rows, cols = logits.shape
    step = 1024
    tile = pl.BlockSpec((step, cols), lambda i: (i, 0))
    outs, shapes = [tile, tile], [hbm(rows, cols, BF16)] * 2
    if with_sums:
        outs += [pl.BlockSpec((8, cols), lambda i: (0, 0))]
        shapes += [shape_of(8, cols)]
    return pl.pallas_call(
        functools.partial(exp_body, with_sums),
        grid=(rows // step,),
        in_specs=[tile],
        out_specs=outs,
        out_shape=shapes,
        compiler_params=params(56),
        cost_estimate=cost(rows * cols * 10, rows * cols * 8),
    )(logits)


def mass_body(sums, mh, ml, out):
    inv = 1.0 / jnp.sum(sums[...], axis=0, keepdims=True)
    ih, il = split(jnp.broadcast_to(inv, (8, inv.shape[1])))
    out[...] = dot3(ih, il, mh[...], ml[...], 1, 1)


def mass_rows(sums, mparts):
    rows, cols = mparts[0].shape
    step = 512
    tile = pl.BlockSpec((step, cols), lambda i: (i, 0))
    return pl.pallas_call(
        mass_body,
        grid=(rows // step,),
        in_specs=[pl.BlockSpec((8, cols), lambda i: (0, 0)), tile, tile],
        out_specs=pl.BlockSpec((8, step), lambda i: (0, i)),
        out_shape=shape_of(8, rows),
        compiler_params=params(56),
        cost_estimate=cost(rows * cols * 48, rows * cols * 4),
    )(sums, *mparts)


def turn(logits, th, tl):
    @pl.when(pl.program_id(0) == 0)
    def _():
        th[...], tl[...] = split(jnp.transpose(jnp.exp(logits[...])))


def send_body(order, logits, source, out, th, tl):
    turn(logits, th, tl)
    out[...] = dot3(th[...], tl[...], *split(source[...]), 1, 0)


def keep_body(order, th, tl, source, out):
    out[...] = dot3(th[...], tl[...], *split(source[...]), 1, 0)


def both_body(across, order, logits, near, far, keep, send, th, tl):
    turn(logits, th, tl)
    first = dot3(th[...], tl[...], *split(near[...]), 1, 0)
    second = dot3(th[...], tl[...], *split(far[...]), 1, 0)
    if not across:
        keep[...], send[...] = first, second
        return
    number = pl.num_programs(0) // 2

    @pl.when(pl.program_id(0) < number)
    def _():
        keep[0], keep[1] = first, second

    @pl.when(pl.program_id(0) >= number)
    def _():
        send[0], send[1] = first, second


def predict(kind, order, expression, unit, column, width, logits, turned=None):
    rows, genes = expression.shape
    count = genes // 2 // unit
    near = pl.BlockSpec((rows, unit), lambda i, order: (0, order[i]))
    far = pl.BlockSpec((rows, unit), lambda i, order: (0, order[count + i]))
    piece = pl.BlockSpec((rows, width), lambda i, order: (0, column))
    flipped = pl.BlockSpec((width, rows), lambda i, order: (0, 0))
    block = pl.BlockSpec((width, unit), lambda i, order: (0, i))
    half = shape_of(width, genes // 2)
    scratch = []
    if kind == "send":
        body, args, ins = send_body, (logits, expression), [piece, far]
        outs, shapes = [block, flipped, flipped], [half] + [hbm(width, rows, BF16)] * 2
    elif kind == "keep":
        body, args, ins = keep_body, (*turned, expression), [flipped, flipped, near]
        outs, shapes = block, half
    else:
        body, args = functools.partial(both_body, kind == "across"), (logits, expression, expression)
        ins, scratch = [piece, near, far], [pltpu.VMEM((width, rows), BF16)] * 2
        outs, shapes = [block, block], [half, half]
        if kind == "across":
            mid = count // 2
            shapes = [shape_of(2, width, genes // 4)] * 2
            outs = [
                pl.BlockSpec((2, width, unit), lambda i, order: (0, 0, jnp.minimum(i, mid - 1))),
                pl.BlockSpec((2, width, unit), lambda i, order: (0, 0, jnp.maximum(i - mid, 0))),
            ]
    return pl.pallas_call(
        body,
        grid_spec=pltpu.PrefetchScalarGridSpec(
            num_scalar_prefetch=1, grid=(count,), in_specs=ins, out_specs=outs, scratch_shapes=scratch
        ),
        out_shape=shapes,
        compiler_params=params(56),
        cost_estimate=cost(3 * rows * genes * width, rows * genes * 4),
    )(order, *args)


def stats_body(turn, kept, came, sums, spatial, mask, onehot, pred, spots, genes):
    total = jnp.sum(sums[...], axis=0, keepdims=True)
    vals = kept[...] + came[...]
    if turn:
        vals = jnp.transpose(vals)
    vals = vals / total
    pred[...] = vals
    spat = spatial[...]
    seen = dot(mask[...].astype(BF16), onehot[...].astype(BF16), 0, 0)
    terms = (vals * spat, vals * vals, spat * spat)
    rows = [jnp.sum(seen * t, axis=0, keepdims=True) for t in terms]
    spots[...] = jnp.concatenate(rows + [jnp.zeros((5, rows[0].shape[1]), F32)], axis=0)
    genes[...] = jnp.concatenate([exact(onehot[...], t, 1, 1) for t in terms], axis=0)


def stats(kept, came, sums, spatial, mask, onehot, column):
    width, shard = kept.shape
    turn = shard % 128 == 0
    if not turn:
        kept, came = kept.T, came.T
    whole = pl.BlockSpec((shard, width), lambda i: (0, 0))
    given = pl.BlockSpec(kept.shape, lambda i: (0, 0))
    strip = pl.BlockSpec((8, width), lambda i: (0, column))
    return pl.pallas_call(
        functools.partial(stats_body, turn),
        grid=(1,),
        in_specs=[
            given,
            given,
            strip,
            pl.BlockSpec((shard, width), lambda i: (0, column)),
            pl.BlockSpec((8, shard), lambda i: (0, 0)),
            strip,
        ],
        out_specs=[
            whole,
            pl.BlockSpec((8, width), lambda i: (0, 0)),
            pl.BlockSpec((24, shard), lambda i: (0, 0)),
        ],
        out_shape=[shape_of(shard, width), shape_of(8, width), shape_of(24, shard)],
        compiler_params=params(32),
        cost_estimate=cost(shard * width * 40, shard * width * 16),
    )(kept, came, sums, spatial, mask, onehot)


def grad_body(slides, spots_total, parts, *refs):
    preds = refs[:parts]
    sums, spatial, mask, onehot, counts, gene_sums, spot_sums = refs[parts : parts + 7]
    outs = refs[parts + 7 : -2]
    inner, losses = refs[-2:]
    size = mask.shape[1]
    dot_g, pp_g, gg_g = (gene_sums[8 * i : 8 * i + 8, :] for i in range(3))
    norm_p, norm_s = jnp.sqrt(pp_g + eps), jnp.sqrt(gg_g + eps)
    weights = mask[...] / counts[...][:, :1]
    gene_part = jnp.sum(weights * (dot_g / (norm_p * norm_s))) / slides
    gene_weight = -weights / slides
    coef_s = gene_weight / (norm_p * norm_s)
    coef_p = gene_weight * dot_g / (norm_p * norm_p * norm_p * norm_s)
    a, b, c = (spot_sums[i : i + 1, :] for i in range(3))
    near_p, near_s = jnp.sqrt(b + eps), jnp.sqrt(c + eps)
    spot_part = jnp.sum(a / (near_p * near_s)) / spots_total
    edge_s = (-1.0 / spots_total) / (near_p * near_s)
    edge_p = (-1.0 / spots_total) * a / (near_p * near_p * near_p * near_s)
    total = jnp.sum(sums[...], axis=0, keepdims=True)
    hot = onehot[...]
    seen = dot(mask[...].astype(BF16), hot.astype(BF16), 0, 0)
    pred = jnp.concatenate([r[...] for r in preds], axis=1)
    grad = spatial[...] * (exact(coef_s, hot, 0, 0) + seen * edge_s) - pred * (
        exact(coef_p, hot, 0, 0) + seen * edge_p
    )
    row = jnp.sum(pred * grad, axis=0, keepdims=True)
    inner[...] = jnp.broadcast_to(row, inner.shape)
    grad = grad / total
    start = 0
    for out in outs:
        out[...] = grad[start : start + out.shape[0]]
        start += out.shape[0]
    lane = lax.broadcasted_iota(jnp.int32, losses.shape, 1)
    losses[...] = jnp.where(lane == 0, gene_part, jnp.where(lane == 1, spot_part, 0.0))


def gradient(preds, sums, spatial, mask, onehot, counts, gene_sums, spot_sums, heights, slides, spots_total):
    shard, cols = spatial.shape
    args = (*preds, sums, spatial, mask, onehot, counts, gene_sums, spot_sums)
    outs = [shape_of(h, cols) for h in heights] + [shape_of(8, cols), shape_of(8, 128)]
    return pl.pallas_call(
        functools.partial(grad_body, float(slides), float(spots_total), len(preds)),
        grid=(1,),
        in_specs=[pl.BlockSpec(a.shape, lambda i: (0, 0)) for a in args],
        out_specs=[pl.BlockSpec(o.shape, lambda i: (0, 0)) for o in outs],
        out_shape=outs,
        compiler_params=params(40),
        cost_estimate=cost(shard * cols * 60, shard * cols * 12),
    )(*args)


def pull_body(dens, sums, mh, ml, out):
    dh, dl = split(jnp.broadcast_to(dens[...][:1], dens.shape))

    @pl.when(pl.program_id(0) == 0)
    def _():
        out[...] = jnp.zeros_like(out)

    out[...] += dot3(dh, dl, mh[...], ml[...], 1, 0) / jnp.sum(sums[...], axis=0, keepdims=True)


def pull_cols(dens, sums, mparts):
    rows, cols = mparts[0].shape
    step = 512
    tile = pl.BlockSpec((step, cols), lambda i: (i, 0))
    strip = pl.BlockSpec((8, cols), lambda i: (0, 0))
    return pl.pallas_call(
        pull_body,
        grid=(rows // step,),
        in_specs=[pl.BlockSpec((8, step), lambda i: (0, i)), strip, tile, tile],
        out_specs=strip,
        out_shape=shape_of(8, cols),
        compiler_params=params(56),
        cost_estimate=cost(rows * cols * 48, rows * cols * 4),
    )(dens, sums, *mparts)


def expr_body(number, height, half, ids, near, far, across, mh, ml, ph, pls, *refs):
    outs, (oh, ol, ch, cl) = refs[:-4], refs[-4:]

    @pl.when(pl.program_id(0) == 0)
    def _():
        for n in range(number):
            at = ids[n]
            inside = pl.ds(pl.multiple_of((at % half) * height, 16), height)
            own = jnp.where(at < half, near[inside, :], far[inside, :])
            other = across[pl.ds(pl.multiple_of(ids[number + n] * height, 16), height), :]
            put = slice(n * height, (n + 1) * height)
            oh[put, :], ol[put, :] = split(own)
            ch[put, :], cl[put, :] = split(other)

    vals = dot3(mh[...], ml[...], oh[...], ol[...], 1, 1) + dot3(
        ph[...], pls[...], ch[...], cl[...], 1, 1
    )
    width = vals.shape[1] // len(outs)
    for n, out in enumerate(outs):
        out[...] = vals[:, n * width : (n + 1) * width]


def expr_part(ids, near, far, across, mparts, pparts, height, blocks, number):
    rows, cols = mparts[0].shape
    step = 512
    half = near.shape[0] // height
    tile = pl.BlockSpec((step, cols), lambda i, ids: (i, 0))
    width = number * height // blocks
    return pl.pallas_call(
        functools.partial(expr_body, number, height, half),
        grid_spec=pltpu.PrefetchScalarGridSpec(
            num_scalar_prefetch=1,
            grid=(rows // step,),
            in_specs=[pl.BlockSpec(a.shape, lambda i, ids: (0, 0)) for a in (near, far, across)]
            + [tile] * 4,
            out_specs=[pl.BlockSpec((step, width), lambda i, ids: (i, 0))] * blocks,
            scratch_shapes=[pltpu.VMEM((number * height, cols), BF16)] * 4,
        ),
        out_shape=[shape_of(rows, width)] * blocks,
        compiler_params=params(48),
        cost_estimate=cost(12 * rows * cols * number * height, rows * cols * 8),
    )(ids, near, far, across, *mparts, *pparts)


def logit_body(pieces, heights, unit, scale, order, dens, sums, inner, source, mh, ml, *refs):
    grads, (out, dh, dl) = refs[:-3], refs[-3:]

    @pl.when(pl.program_id(0) == 0)
    def _():
        shard = sum(heights)
        for p in range(pieces):
            base = order[p * shard // unit] * unit + p * shard % unit
            at = 0
            for q, height in enumerate(heights):
                grad = grads[2 * q + (p >= pieces // 2)]
                inside = p % (pieces // 2)
                rows = pl.ds(pl.multiple_of(base + at, 16), height)
                dh[rows, :], dl[rows, :] = split(grad[inside * height : (inside + 1) * height, :])
                at += height

    inv = 1.0 / jnp.sum(sums[...], axis=0, keepdims=True)
    column = jnp.transpose(dens[...])[:, :1]
    vals = dot3(*split(source[...]), dh[...], dl[...], 1, 0) + (column - inner[...][:1]) * inv
    out[...] = (mh[...].astype(F32) + ml[...].astype(F32)) * vals * scale


def logit_part(order, dens, sums, inner, expression, mparts, grads, heights, pieces, unit, scale):
    rows, cols = mparts[0].shape
    genes = expression.shape[1]
    step = 256
    strip = pl.BlockSpec((8, cols), lambda i, order: (0, 0))
    tile = pl.BlockSpec((step, cols), lambda i, order: (i, 0))
    return pl.pallas_call(
        functools.partial(logit_body, pieces, heights, unit, scale),
        grid_spec=pltpu.PrefetchScalarGridSpec(
            num_scalar_prefetch=1,
            grid=(rows // step,),
            in_specs=[pl.BlockSpec((8, step), lambda i, order: (0, i)), strip, strip]
            + [pl.BlockSpec((step, genes), lambda i, order: (i, 0))]
            + [tile] * 2
            + [
                pl.BlockSpec(g.shape, lambda i, order: (0, 0), pipeline_mode=pl.Buffered(1))
                for g in grads
            ],
            out_specs=tile,
            scratch_shapes=[pltpu.VMEM((genes, cols), BF16)] * 2,
        ),
        out_shape=shape_of(rows, cols),
        compiler_params=params(56),
        cost_estimate=cost(6 * rows * cols * genes, rows * genes * 4 + rows * cols * 8),
    )(order, dens, sums, inner, expression, *mparts, *grads)


def join_body(shards, heights, scale, *refs):
    out = refs[-1]
    shard = sum(heights)
    at = 0
    for q, height in enumerate(heights):
        vals = (refs[2 * q][...] + refs[2 * q + 1][...]) * scale
        for b in range(shards):
            out[:, b * shard + at : b * shard + at + height] = vals[:, b * height : (b + 1) * height]
        at += height


def join(pairs, heights, shards, scale):
    flat = [v for pair in pairs for v in pair]
    rows = flat[0].shape[0]
    step = 512
    genes = shards * sum(heights)
    return pl.pallas_call(
        functools.partial(join_body, shards, heights, scale),
        grid=(rows // step,),
        in_specs=[pl.BlockSpec((step, v.shape[1]), lambda i: (i, 0)) for v in flat],
        out_specs=pl.BlockSpec((step, genes), lambda i: (i, 0)),
        out_shape=shape_of(rows, genes),
        compiler_params=params(32),
        cost_estimate=cost(rows * genes * 2, rows * genes * 12),
    )(*flat)


class Line:
    def __init__(self):
        self.held = []

    def __call__(self, value):
        return after(value, *self.held) if self.held else value

    def mark(self, value):
        self.held = [value]

    def also(self, value):
        self.held = self.held + [value]


class Total:
    def __init__(self, line, value, axis, bits):
        self.line, self.value, self.axis, self.bits = line, value, axis, list(bits)
        self.come = swap(value, axis, self.bits.pop(0))

    def next(self):
        self.value = add(self.value, self.line(self.come))
        self.line.mark(self.value)
        self.come = swap(self.value, self.axis, self.bits.pop(0)) if self.bits else None

    def end(self):
        while self.come is not None:
            self.next()
        return self.value


def swap(v, axis, bit):
    size = lax.axis_size(axis)
    return lax.ppermute(v, axis, [(i, i ^ (1 << bit)) for i in range(size)])


def add_all(v, axis):
    for bit in range(lax.axis_size(axis).bit_length() - 1):
        v = add(v, swap(v, axis, bit))
    return v


def reverse(value, bits):
    return sum(((value >> b) & 1) << (bits - 1 - b) for b in range(bits))


def on_device(logits, expression, spatial, masks, slide_ids, counts):
    cells, spots_n = lax.axis_size("cell"), lax.axis_size("spot")
    me, mine = lax.axis_index("cell"), lax.axis_index("spot")
    rows, cols = logits.shape
    shard = spatial.shape[0]
    slides, genes = masks.shape
    cells_total, spots_total = rows * cells, cols * spots_n
    cell_bits = cells.bit_length() - 1
    per_block = cells // spots_n
    block_bits = per_block.bit_length() - 1
    scale = float(cells_total * spots_total)

    other_logits = swap(logits, "spot", 0)
    order = me ^ reverse(jnp.arange(cells, dtype=jnp.int32), cell_bits)
    unit = 256
    source = expression
    if shard != unit:
        source = source.reshape(rows, cells, shard)[:, order].reshape(rows, genes)
        order = jnp.arange(genes // unit, dtype=jnp.int32)

    mask8 = jnp.pad(masks.astype(F32), ((0, 8 - slides), (0, 0)))
    mask8 = lax.dynamic_slice_in_dim(mask8, me * shard, shard, 1)
    onehot = (slide_ids[None, :] == jnp.arange(8, dtype=jnp.int32)[:, None]).astype(F32)
    counts8 = jnp.broadcast_to(
        jnp.pad(counts.astype(F32), (0, 8 - slides), constant_values=1.0)[:, None], (8, 128)
    )

    line = Line()

    width = 256
    number = cols // width
    generic = not (cells == 8 and shard == unit and number == 4)
    cross = -1 if generic else 1
    keeps, sends, steps, found, turned, parts = {}, {}, {}, {}, {}, {}

    def make(kind, q):
        given = turned.get(q)
        if kind == "keep":
            given = line(given[0]), given[1]
        outs = predict(kind, order, source, unit, q, width, line(logits), given)
        if kind == "send":
            sends[q], *turned[q] = outs
        elif kind == "keep":
            keeps[q] = outs
        else:
            keeps[q], sends[q] = outs
        line.mark(keeps.get(q, sends.get(q)))
        if kind != "keep":
            found[q] = swap(sends[q], "cell", 1 if q == cross else 0)

    def step(q):
        bits = (1, 0, 2) if q == cross else tuple(range(cell_bits))
        at = steps.get(q, 0)
        steps[q] = at + 1
        if at < cell_bits - 1:
            kept, came = keeps[q], line(found[q])
            kept, out = add_split(kept, came)
            line.mark(out)
            keeps[q] = kept
            found[q] = swap(out, "cell", bits[at + 1])
        else:
            keeps[q] = stats(keeps[q], line(found[q]), parts["sums"].end(), spatial, mask8, onehot, q)
            line.mark(keeps[q][0])

    def own_exps():
        *parts["m"], sums = exp_split(line(logits), True)
        line.mark(sums)
        parts["sums"] = Total(line, sums, "cell", [*range(1, cell_bits), 0])

    def other_exps():
        parts["p"] = exp_split(line(other_logits), False)
        line.mark(parts["p"][0])

    def masses():
        parts["mass"] = mass_rows(line(parts["sums"].end()), parts["m"])
        line.mark(parts["mass"])

    if generic:
        own_exps()
        for q in range(number):
            make("both", q)
        masses(), other_exps()
        for _ in range(cell_bits):
            for q in range(number):
                step(q)
    else:
        make("send", 0), own_exps(), make("send", 2), parts["sums"].next(), make("keep", 0)
        parts["sums"].next(), step(0), make("across", 1), make("both", 3), make("keep", 2), step(2)
        step(0), step(1), other_exps(), step(2), step(3), step(0), masses()
        step(1), step(2), step(3), step(1), step(3)
    sums, mparts, pparts = parts["sums"].end(), parts["m"], parts["p"]
    preds = [keeps[q][0] for q in range(number)]
    spot_stats = [keeps[q][1] for q in range(number)]
    gene_stats = sum(keeps[q][2] for q in range(number))
    spot_stats = add_all(jnp.concatenate(spot_stats, axis=1), "cell")
    mass = parts["mass"][:1].reshape(-1, shard)
    joint = add_all(jnp.concatenate([gene_stats, mass], axis=0), "spot")
    gene_stats = joint[:24]
    mass = joint[24:].reshape(1, rows) / spots_total
    density_part = -jnp.sum(jnp.log(cells_total * mass)) / cells_total
    dens = jnp.broadcast_to(-1.0 / (cells_total * spots_total * mass), (8, rows))

    heights = (shard // 4,) * 4
    *grads, inner, losses = gradient(
        preds, sums, spatial, mask8, onehot, counts8, gene_stats, spot_stats, heights, slides, spots_total
    )

    blocks = spots_n // 2
    far_w = jnp.arange(blocks, dtype=jnp.int32)[:, None] << 1
    wanted = ((mine ^ far_w) * per_block + jnp.arange(per_block, dtype=jnp.int32)[None, :]) ^ me
    wanted = wanted.reshape(-1)
    place = reverse(wanted, cell_bits)
    low_bits = cell_bits - block_bits - 1
    short = ((place >> (low_bits + 1)) << low_bits) | (place & ((1 << low_bits) - 1))
    ids = jnp.concatenate([place, short]).astype(jnp.int32)
    core_bit = ((me >> block_bits) ^ mine) & 1

    line.mark(grads[0])
    number = len(heights)
    nears, fars, gots, acrosses, pairs, arrived = {}, {}, {}, {}, {}, {}

    def widen(q, bits):
        for bit in bits:
            if q in gots:
                nears[q] = glue(nears[q], line(gots[q]))
                line.mark(nears[q])
            else:
                nears[q] = line(nears[q])
            gots[q] = swap(nears[q], "cell", bit)

    def share(q):
        fars[q] = line(gots[q])
        size = heights[q] << low_bits
        out = pick(1 - core_bit.reshape(1), 1 << (block_bits - 1), size, nears[q], fars[q])
        line.mark(out)
        acrosses[q] = swap(out, "spot", 0)

    def multiply(q):
        outs = expr_part(
            ids, nears[q], fars[q], line(acrosses[q]), mparts, pparts, heights[q], blocks, wanted.size
        )
        outs = list(outs)
        line.mark(outs[0])
        bit = spots_n.bit_length() - 2
        while len(outs) > 2:
            half = len(outs) // 2
            came = swap(jnp.concatenate(outs[half:], axis=1), "spot", bit)
            came = jnp.split(came, half, axis=1)
            outs = [a + b for a, b in zip(outs[:half], came)]
            bit -= 1
        arrived[q] = swap(outs[1], "spot", bit)
        pairs[q] = (outs[0], arrived[q])

    nears.update(enumerate(grads))
    def first(q):
        widen(q, [cell_bits - 1])

    def second(q):
        widen(q, range(cell_bits - 2, 0, -1))

    def third(q):
        widen(q, [0])

    def pull():
        added = inner + pull_cols(line(dens), sums, mparts)
        added = jnp.concatenate(
            [added, jnp.broadcast_to(density_part - losses[0, 0], (8, 128))], axis=1
        )
        line.mark(added)
        parts["tail"] = Total(line, added, "cell", range(cell_bits - 1, -1, -1))

    spot_bits = range(spots_n.bit_length() - 1)
    parts["spots"] = Total(line, jnp.broadcast_to(losses[0, 1], (8, 128)), "spot", spot_bits)
    first(0), parts["spots"].next(), pull(), parts["spots"].next(), second(0), first(1), third(0)
    parts["tail"].next(), second(1), first(2), parts["tail"].next(), third(1), second(2), first(3)
    share(0), multiply(0), third(2), second(3), share(1), multiply(1), third(3), parts["tail"].next()
    line.also(arrived[0])
    share(2), multiply(2)
    line.also(arrived[1])
    share(3), multiply(3)
    tail = parts["tail"].end()
    loss = tail[0, cols] - parts["spots"].end()[0, 0]
    pairs = [pairs[q] for q in range(number)]
    gathered = [v for q in range(number) for v in (nears[q], fars[q])]

    logit_grad = logit_part(
        order, line(dens), sums, tail[:, :cols], source, mparts, gathered, heights, cells, unit, scale
    )
    expr_grad = join(pairs, heights, per_block, scale)
    return (loss, logit_grad, expr_grad)


def solution(mesh):
    placed = (P("cell", "spot"), P("cell", None), P("cell", "spot"), P(), P("spot"), P())
    return jax.shard_map(
        on_device,
        mesh=mesh,
        in_specs=placed,
        out_specs=(P(), P("cell", "spot"), P("cell", "spot")),
        check_vma=False,
    )
```

time: 459 us -> 384 us (0.84)
  waiting for transfers between devices: 167 us -> 120 us
  local copies, waits for them, and re-layouts: 43.8 us -> 15 us
  Pallas kernels: 173 us -> 192 us
  other arithmetic: 11 us -> 2.1 us
  starting transfers between devices: 56.8 us -> 48.7 us
    ppermute x46, waiting for transfers between devices: 167 us -> 120 us  [swap(): return lax.ppermute(v, axis, [(i, i ^ 1 << bit) for i in range(size)])]
    unnamed x84 -> x76, local copies, waits for them, and re-layouts: 40.8 us -> 10.4 us
    pallas_call x16 -> x46, Pallas kernels: 115 us -> 126 us  [the longest x6 61.9 us: predict(): pl.pallas_call(body, grid_spec=pltpu.PrefetchScalarGridSpec(num_scalar_pr...]
    ppermute x46, starting transfers between devices: 56.8 us -> 48.7 us  [swap(): return lax.ppermute(v, axis, [(i, i ^ 1 << bit) for i in range(size)])]
    concatenate x8 -> x0, other arithmetic: 4.94 us -> none  [the longest x4 3.8 us: on_device(): across = swap(jnp.concatenate([part(near), part(far)], axis=0), 'spot', 0)]
  transfers between devices with their start and end apart: 46 -> 46, of which waited for: 22 -> 21; matrix products, arithmetic and copies ran while one was open for 3% -> 2% of each run, Pallas kernels for 37% -> 47%
where the time goes in v2:
time: 384 us; the launch traced here: 383 us
  Pallas kernels  192 us (50%)
  waiting for transfers between devices  120 us (31%)
  starting transfers between devices  48.7 us (13%)
  local copies, waits for them, and re-layouts  15 us (4%)
  between operations  5.02 us (1%)
    ppermute x46, waiting for transfers between devices, swap(): return lax.ppermute(v, axis, [(i, i ^ 1 << bit) for i in range(size)])  120 us
    pallas_call x6, Pallas kernels, predict(): pl.pallas_call(body, grid_spec=pltpu.PrefetchScalarGridSpec(num_scalar_pr...  61.9 us
    ppermute x46, starting transfers between devices, swap(): return lax.ppermute(v, axis, [(i, i ^ 1 << bit) for i in range(size)])  48.7 us
    pallas_call x4, Pallas kernels, expr_part(): pl.pallas_call(functools.partial(expr_body, number, height, half), grid_s...  46.5 us
    pallas_call x1, Pallas kernels, logit_part(): pl.pallas_call(functools.partial(logit_body, pieces, heights, unit, scale...  35.9 us
    pallas_call x2, Pallas kernels, exp_split(): pl.pallas_call(functools.partial(exp_body, with_sums), grid=(rows // step...  12.7 us
    pallas_call x33, Pallas kernels, simple(): pl.pallas_call(body, grid_spec=pltpu.PrefetchScalarGridSpec(num_scalar_pr...  12.1 us
    unnamed x76, local copies, waits for them, and re-layouts  10.4 us
  transfers between devices with their start and end apart: 46, of which 21 were waited for; matrix products, arithmetic and copies ran while one was open for 2% of the time, Pallas kernels for 47%

profile of v2, /device:TPU:0, one launch (start us, length us, event | category | flops | bytes accessed | tf_op | source)
XLA Modules:
  0.0 383.1 jit_solution(10748172461367213936)
XLA Ops:
  1.7 9.1 %shard_map.85 = (f32[256,1024]{1,0:T(8,128)}, bf16[256,2048]{1,0:T(8,128)(2,1)}, bf16[256,2048]{1,0:T(8,128)(2,1)}) custom-call(s32[8]{0:T(128)} %fusion.7.order, f32[2048,1024]{1,0:T(8,128)} %logits.5, f32[2048,2048]{1,0:T(8,128)} %source.9), custom_call_target="tpu_custom_call" | custom-call | tf_op jit(solution)/shard_map/pallas_call | solution.py:237
  13.3 6.5 %shard_map.86 = (bf16[2048,1024]{1,0:T(8,128)(2,1)}, bf16[2048,1024]{1,0:T(8,128)(2,1)}, f32[8,1024]{1,0:T(8,128)}) custom-call(f32[2048,1024]{1,0:T(8,128)} %logits.5), custom_call_target="tpu_custom_call" | custom-call | tf_op jit(solution)/shard_map/pallas_call | solution.py:145
  19.8 9.3 %shard_map.87 = (f32[256,1024]{1,0:T(8,128)}, bf16[256,2048]{1,0:T(8,128)(2,1)}, bf16[256,2048]{1,0:T(8,128)(2,1)}) custom-call(s32[8]{0:T(128)} %fusion.7.order, f32[2048,1024]{1,0:T(8,128)} %logits.5, f32[2048,2048]{1,0:T(8,128)} %source.9), custom_call_target="tpu_custom_call" | custom-call | tf_op jit(solution)/shard_map/pallas_call | solution.py:237
  36.2 8.4 %shard_map.89.kept = f32[256,1024]{1,0:T(8,128)} custom-call(s32[8]{0:T(128)} %fusion.7.order, bf16[256,2048]{1,0:T(8,128)(2,1)} %get-tuple-element.117.th, bf16[256,2048]{1,0:T(8,128)(2,1)} %get-tuple-element.118.tl, f32[2048,2048]{1,0:T(8,128)} %source.9), custom_call_target="tpu_custom_call" | custom-call | tf_op jit(solution)/shard_map/pallas_call | solution.py:237
  46.0 13.3 %shard_map.92 = (f32[2,256,512]{2,1,0:T(8,128)}, f32[2,256,512]{2,1,0:T(8,128)}) custom-call(s32[8]{0:T(128)} %fusion.7.order, f32[2048,1024]{1,0:T(8,128)} %logits.5, f32[2048,2048]{1,0:T(8,128)} %source.9, f32[2048,2048]{1,0:T(8,128)} %source.9), custom_call_target="tpu_custom_call" | custom-call | tf_op jit(solution)/shard_map/pallas_call | solution.py:237
  60.8 13.2 %shard_map.93 = (f32[256,1024]{1,0:T(8,128)}, f32[256,1024]{1,0:T(8,128)}) custom-call(s32[8]{0:T(128)} %fusion.7.order, f32[2048,1024]{1,0:T(8,128)} %logits.5, f32[2048,2048]{1,0:T(8,128)} %source.9, f32[2048,2048]{1,0:T(8,128)} %source.9), custom_call_target="tpu_custom_call" | custom-call | tf_op jit(solution)/shard_map/pallas_call | solution.py:237
  76.0 8.6 %shard_map.94.kept = f32[256,1024]{1,0:T(8,128)} custom-call(s32[8]{0:T(128)} %fusion.7.order, bf16[256,2048]{1,0:T(8,128)(2,1)} %get-tuple-element.128.th, bf16[256,2048]{1,0:T(8,128)(2,1)} %get-tuple-element.129.tl, f32[2048,2048]{1,0:T(8,128)} %source.9), custom_call_target="tpu_custom_call" | custom-call | tf_op jit(solution)/shard_map/pallas_call | solution.py:237
  88.2 8.6 %collective-permute-done.3.came = f32[256,512]{1,0:T(8,128)S(1)} collective-permute-done((f32[256,512]{1,0:T(8,128)S(1)}, f32[256,512]{1,0:T(8,128)S(1)}, u32[]{:S(2)}, u32[]{:S(2)}) %collective-permute-start.3) | collective-permute-done | bytes 524320 | tf_op jit(solution)/shard_map/ppermute | solution.py:522
  99.4 6.2 %shard_map.98 = (bf16[2048,1024]{1,0:T(8,128)(2,1)}, bf16[2048,1024]{1,0:T(8,128)(2,1)}) custom-call(f32[2048,1024]{1,0:T(8,128)} %collective-permute-done.8.logits), custom_call_target="tpu_custom_call" | custom-call | tf_op jit(solution)/shard_map/pallas_call | solution.py:145
  113.0 13.4 %collective-permute-done.5.came = f32[256,256]{1,0:T(8,128)S(1)} collective-permute-done((f32[256,256]{1,0:T(8,128)}, f32[256,256]{1,0:T(8,128)S(1)}, u32[]{:S(2)}, u32[]{:S(2)}) %collective-permute-start.5) | collective-permute-done | bytes 262176 | tf_op jit(solution)/shard_map/ppermute | solution.py:522
  127.2 6.7 %shard_map.103 = f32[8,2048]{1,0:T(8,128)} custom-call(f32[8,1024]{1,0:T(8,128)} %copy-done.10, bf16[2048,1024]{1,0:T(8,128)(2,1)} %get-tuple-element.151.mh, bf16[2048,1024]{1,0:T(8,128)(2,1)} %get-tuple-element.152.ml), custom_call_target="tpu_custom_call" | custom-call | tf_op jit(solution)/shard_map/pallas_call | solution.py:166
  142.3 9.6 %collective-permute-done.12.came = f32[256,256]{1,0:T(8,128)S(1)} collective-permute-done((f32[256,256]{1,0:T(8,128)}, f32[256,256]{1,0:T(8,128)S(1)}, u32[]{:S(2)}, u32[]{:S(2)}) %collective-permute-start.12) | collective-permute-done | bytes 262176 | tf_op jit(solution)/shard_map/ppermute | solution.py:522
  179.0 5.8 %shard_map.116 = f32[8,1024]{1,0:T(8,128)} custom-call(f32[8,2048]{1,0:T(8,128)} %broadcast_in_dim.7.dens, f32[8,1024]{1,0:T(8,128)} %copy-done.10, bf16[2048,1024]{1,0:T(8,128)(2,1)} %get-tuple-element.151.mh, bf16[2048,1024]{1,0:T(8,128)(2,1)} %get-tuple-element.152.ml), custom_call_target="tpu_custom_call" | custom-call | tf_op jit(solution)/shard_map/pallas_call | solution.py:359
  187.6 12.0 %collective-permute-done.25.refs_1_ = f32[128,1024]{1,0:T(8,128)S(1)} collective-permute-done((f32[128,1024]{1,0:T(8,128)S(1)}, f32[128,1024]{1,0:T(8,128)S(1)}, u32[]{:S(2)}, u32[]{:S(2)}) %collective-permute-start.25) | collective-permute-done | bytes 524320 | tf_op jit(solution)/shard_map/ppermute | solution.py:522
  204.4 12.3 %collective-permute-done.22.b = f32[8,1152]{1,0:T(8,128)S(1)} collective-permute-done((f32[8,1152]{1,0:T(8,128)S(1)}, f32[8,1152]{1,0:T(8,128)S(1)}, u32[]{:S(2)}, u32[]{:S(2)}) %collective-permute-start.22) | collective-permute-done | bytes 36896 | tf_op jit(solution)/shard_map/ppermute | solution.py:522
  220.9 15.2 %collective-permute-done.26.b = f32[8,1152]{1,0:T(8,128)S(1)} collective-permute-done((f32[8,1152]{1,0:T(8,128)S(1)}, f32[8,1152]{1,0:T(8,128)S(1)}, u32[]{:S(2)}, u32[]{:S(2)}) %collective-permute-start.26) | collective-permute-done | bytes 36896 | tf_op jit(solution)/shard_map/ppermute | solution.py:522
  246.5 11.5 %shard_map.126 = (f32[2048,128]{1,0:T(8,128)S(1)}, f32[2048,128]{1,0:T(8,128)S(1)}) custom-call(s32[8]{0:T(128)S(1)} %pad_add_fusion.ids, f32[256,1024]{1,0:T(8,128)S(1)} %shard_map.119.refs_0_.near, f32[256,1024]{1,0:T(8,128)S(1)} %collective-permute-done.33.refs_1_.far, f32[256,1024]{1,0:T(8,128)} %collective-permute-done.34.across, ...), custom_call_target="tpu_custom_call" | custom-call | tf_op jit(solution)/shard_map/pallas_call | solution.py:398
  258.0 4.9 %collective-permute-done.32.refs_1_ = f32[128,1024]{1,0:T(8,128)} collective-permute-done((f32[128,1024]{1,0:T(8,128)}, f32[128,1024]{1,0:T(8,128)}, u32[]{:S(2)}, u32[]{:S(2)}) %collective-permute-start.32) | collective-permute-done | bytes 524320 | tf_op jit(solution)/shard_map/ppermute | solution.py:522
  272.5 11.7 %shard_map.130 = (f32[2048,128]{1,0:T(8,128)S(1)}, f32[2048,128]{1,0:T(8,128)S(1)}) custom-call(s32[8]{0:T(128)S(1)} %pad_add_fusion.ids, f32[256,1024]{1,0:T(8,128)S(1)} %shard_map.123.refs_0_.near.refs_2_, f32[256,1024]{1,0:T(8,128)} %collective-permute-done.36.refs_1_.far.refs_3_, f32[256,1024]{1,0:T(8,128)S(1)} %collective-permute-done.37.across, ...), custom_call_target="tpu_custom_call" | custom-call | tf_op jit(solution)/shard_map/pallas_call | solution.py:398
  284.9 11.0 %collective-permute-done.28.b = f32[8,1152]{1,0:T(8,128)S(1)} collective-permute-done((f32[8,1152]{1,0:T(8,128)S(1)}, f32[8,1152]{1,0:T(8,128)S(1)}, u32[]{:S(2)}, u32[]{:S(2)}) %collective-permute-start.28) | collective-permute-done | bytes 36896 | tf_op jit(solution)/shard_map/ppermute | solution.py:522
  298.8 11.7 %shard_map.134 = (f32[2048,128]{1,0:T(8,128)S(1)}, f32[2048,128]{1,0:T(8,128)}) custom-call(s32[8]{0:T(128)S(1)} %pad_add_fusion.ids, f32[256,1024]{1,0:T(8,128)S(1)} %shard_map.127.refs_0_.near.refs_4_, f32[256,1024]{1,0:T(8,128)S(1)} %collective-permute-done.39.refs_1_.far.refs_5_, f32[256,1024]{1,0:T(8,128)S(1)} %collective-permute-done.41.across, ...), custom_call_target="tpu_custom_call" | custom-call | tf_op jit(solution)/shard_map/pallas_call | solution.py:398
  311.4 10.2 %collective-permute-done.38.refs_1_.far.refs_7_ = f32[256,1024]{1,0:T(8,128)S(1)} collective-permute-done((f32[256,1024]{1,0:T(8,128)S(1)}, f32[256,1024]{1,0:T(8,128)S(1)}, u32[]{:S(2)}, u32[]{:S(2)}) %collective-permute-start.38) | collective-permute-done | bytes 1048608 | tf_op jit(solution)/shard_map/ppermute | solution.py:522
  325.1 11.7 %shard_map.136 = (f32[2048,128]{1,0:T(8,128)S(1)}, f32[2048,128]{1,0:T(8,128)}) custom-call(s32[8]{0:T(128)S(1)} %pad_add_fusion.ids, f32[256,1024]{1,0:T(8,128)S(1)} %shard_map.131.refs_0_.near.refs_6_, f32[256,1024]{1,0:T(8,128)S(1)} %collective-permute-done.38.refs_1_.far.refs_7_, f32[256,1024]{1,0:T(8,128)S(1)} %collective-permute-done.43.across, ...), custom_call_target="tpu_custom_call" | custom-call | tf_op jit(solution)/shard_map/pallas_call | solution.py:398
  341.3 35.9 %shard_map.137 = f32[2048,1024]{1,0:T(8,128)} custom-call(s32[8]{0:T(128)} %fusion.7.order, f32[8,2048]{1,0:T(8,128)} %broadcast_in_dim.7.dens, f32[8,1024]{1,0:T(8,128)} %copy-done.10, f32[8,1024]{1,0:T(8,128)} %slice.36.inner, f32[2048,2048]{1,0:T(8,128)} %source.9, bf16[2048,1024]{1,0:T(8,128)(2,1)} %get-tuple-element.151.mh, ...), custom_call_target="tpu_custom_call" | custom-call | tf_op jit(solution)/shard_map/pallas_call | solution.py:442
  (225 shorter events, 111.5 us)
Async XLA Ops:
  0.6 98.8 %collective-permute-start.8 = (f32[2048,1024]{1,0:T(8,128)}, f32[2048,1024]{1,0:T(8,128)}, u32[]{:S(2)}, u32[]{:S(2)}) collective-permute-start(f32[2048,1024]{1,0:T(8,128)} %logits.5), channel_id=1, source_target_pairs={{0,1},{1,0},{2,3},{3,2},{4,5},{5,4},{6,7},{7,6},{8,9},{9,8},{10,11... | collective-permute-start | bytes 25165832 | tf_op jit(solution)/shard_map/ppermute | solution.py:522
  10.8 33.8 %collective-permute-start.1 = (f32[256,1024]{1,0:T(8,128)}, f32[256,1024]{1,0:T(8,128)S(1)}, u32[]{:S(2)}, u32[]{:S(2)}) collective-permute-start(f32[256,1024]{1,0:T(8,128)} %get-tuple-element.111), channel_id=1, source_target_pairs={{0,4},{4,0},{8,12},{12,8},{16,20},{20,16},{24,28},{28,24},{1,5},{5... | collective-permute-start | bytes 3145736 | tf_op jit(solution)/shard_map/ppermute | solution.py:522
  29.1 55.4 %collective-permute-start.4 = (f32[256,1024]{1,0:T(8,128)}, f32[256,1024]{1,0:T(8,128)S(1)}, u32[]{:S(2)}, u32[]{:S(2)}) collective-permute-start(f32[256,1024]{1,0:T(8,128)} %get-tuple-element.115), channel_id=1, source_target_pairs={{0,4},{4,0},{8,12},{12,8},{16,20},{20,16},{24,28},{28,24},{1,5},{5... | collective-permute-start | bytes 3145736 | tf_op jit(solution)/shard_map/ppermute | solution.py:522
  59.2 37.6 %collective-permute-start.9 = (f32[2,256,512]{2,1,0:T(8,128)}, f32[2,256,512]{2,1,0:T(8,128)S(1)}, u32[]{:S(2)}, u32[]{:S(2)}) collective-permute-start(f32[2,256,512]{2,1,0:T(8,128)} %get-tuple-element.137), channel_id=1, source_target_pairs={{0,8},{4,12},{8,0},{12,4},{16,24},{20,28},{24,16},{28,20},{1,9},{5... | collective-permute-start | bytes 3145736 | tf_op jit(solution)/shard_map/ppermute | solution.py:522
  74.0 31.9 %collective-permute-start.6 = (f32[256,1024]{1,0:T(8,128)}, f32[256,1024]{1,0:T(8,128)S(1)}, u32[]{:S(2)}, u32[]{:S(2)}) collective-permute-start(f32[256,1024]{1,0:T(8,128)} %get-tuple-element.135), channel_id=1, source_target_pairs={{0,4},{4,0},{8,12},{12,8},{16,20},{20,16},{24,28},{28,24},{1,5},{5... | collective-permute-start | bytes 3145736 | tf_op jit(solution)/shard_map/ppermute | solution.py:522
  75.5 21.3 %collective-permute-start.3 = (f32[256,512]{1,0:T(8,128)S(1)}, f32[256,512]{1,0:T(8,128)S(1)}, u32[]{:S(2)}, u32[]{:S(2)}) collective-permute-start(f32[256,512]{1,0:T(8,128)S(1)} %get-tuple-element.122), channel_id=1, source_target_pairs={{0,8},{4,12},{8,0},{12,4},{16,24},{20,28},{24,16},{28,20},{1,9},{5... | collective-permute-start | bytes 1572872 | tf_op jit(solution)/shard_map/ppermute | solution.py:522
  86.7 19.1 %collective-permute-start.7 = (f32[256,512]{1,0:T(8,128)}, f32[256,512]{1,0:T(8,128)S(1)}, u32[]{:S(2)}, u32[]{:S(2)}) collective-permute-start(f32[256,512]{1,0:T(8,128)} %get-tuple-element.131), channel_id=1, source_target_pairs={{0,8},{4,12},{8,0},{12,4},{16,24},{20,28},{24,16},{28,20},{1,9},{5... | collective-permute-start | bytes 1572872 | tf_op jit(solution)/shard_map/ppermute | solution.py:522
  97.8 36.1 %collective-permute-start.11 = (f32[256,512]{1,0:T(8,128)}, f32[256,512]{1,0:T(8,128)S(1)}, u32[]{:S(2)}, u32[]{:S(2)}) collective-permute-start(f32[256,512]{1,0:T(8,128)} %get-tuple-element.139), channel_id=1, source_target_pairs={{0,4},{4,0},{8,12},{12,8},{16,20},{20,16},{24,28},{28,24},{1,5},{5... | collective-permute-start | bytes 1572872 | tf_op jit(solution)/shard_map/ppermute | solution.py:522
  106.8 33.6 %collective-permute-start.13 = (f32[256,512]{1,0:T(8,128)}, f32[256,512]{1,0:T(8,128)}, u32[]{:S(2)}, u32[]{:S(2)}) collective-permute-start(f32[256,512]{1,0:T(8,128)} %get-tuple-element.145), channel_id=1, source_target_pairs={{0,8},{4,12},{8,0},{12,4},{16,24},{20,28},{24,16},{28,20},{1,9},{5... | collective-permute-start | bytes 1572872 | tf_op jit(solution)/shard_map/ppermute | solution.py:522
  108.4 18.0 %collective-permute-start.5 = (f32[256,256]{1,0:T(8,128)}, f32[256,256]{1,0:T(8,128)S(1)}, u32[]{:S(2)}, u32[]{:S(2)}) collective-permute-start(f32[256,256]{1,0:T(8,128)} %copy-done.31), channel_id=1, source_target_pairs={{0,16},{4,20},{8,24},{12,28},{16,0},{20,4},{24,8},{28,12},{1,17},{... | collective-permute-start | bytes 786440 | tf_op jit(solution)/shard_map/ppermute | solution.py:522
  110.4 28.4 %collective-permute-start.14 = (f32[256,256]{1,0:T(8,128)}, f32[256,256]{1,0:T(8,128)S(1)}, u32[]{:S(2)}, u32[]{:S(2)}) collective-permute-start(f32[256,256]{1,0:T(8,128)} %copy-done.32), channel_id=1, source_target_pairs={{0,16},{4,20},{8,24},{12,28},{16,0},{20,4},{24,8},{28,12},{1,17},{... | collective-permute-start | bytes 786440 | tf_op jit(solution)/shard_map/ppermute | solution.py:522
  199.6 41.7 %collective-permute-start.33 = (f32[256,1024]{1,0:T(8,128)S(1)}, f32[256,1024]{1,0:T(8,128)S(1)}, u32[]{:S(2)}, u32[]{:S(2)}) collective-permute-start(f32[256,1024]{1,0:T(8,128)S(1)} %shard_map.119.refs_0_.near), channel_id=1, source_target_pairs={{0,4},{4,0},{8,12},{12,8},{16,20},{20,16},{24,28},{28,24},{1,5},{5... | collective-permute-start | bytes 3145736 | tf_op jit(solution)/shard_map/ppermute | solution.py:522
  216.8 19.3 %collective-permute-start.30 = (f32[128,1024]{1,0:T(8,128)S(1)}, f32[128,1024]{1,0:T(8,128)S(1)}, u32[]{:S(2)}, u32[]{:S(2)}) collective-permute-start(f32[128,1024]{1,0:T(8,128)S(1)} %shard_map.121.refs_0_), channel_id=1, source_target_pairs={{0,8},{4,12},{8,0},{12,4},{16,24},{20,28},{24,16},{28,20},{1,9},{5... | collective-permute-start | bytes 1572872 | tf_op jit(solution)/shard_map/ppermute | solution.py:522
  217.7 21.4 %collective-permute-start.29 = (f32[64,1024]{1,0:T(8,128)}, f32[64,1024]{1,0:T(8,128)}, u32[]{:S(2)}, u32[]{:S(2)}) collective-permute-start(f32[64,1024]{1,0:T(8,128)} %get-tuple-element.191.refs_0_), channel_id=1, source_target_pairs={{0,16},{4,20},{8,24},{12,28},{16,0},{20,4},{24,8},{28,12},{1,17},{... | collective-permute-start | bytes 786440 | tf_op jit(solution)/shard_map/ppermute | solution.py:522
  242.5 25.7 %collective-permute-start.36 = (f32[256,1024]{1,0:T(8,128)S(1)}, f32[256,1024]{1,0:T(8,128)}, u32[]{:S(2)}, u32[]{:S(2)}) collective-permute-start(f32[256,1024]{1,0:T(8,128)S(1)} %shard_map.123.refs_0_.near.refs_2_), channel_id=1, source_target_pairs={{0,4},{4,0},{8,12},{12,8},{16,20},{20,16},{24,28},{28,24},{1,5},{5... | collective-permute-start | bytes 3145736 | tf_op jit(solution)/shard_map/ppermute | solution.py:522
  242.9 20.0 %collective-permute-start.32 = (f32[128,1024]{1,0:T(8,128)}, f32[128,1024]{1,0:T(8,128)}, u32[]{:S(2)}, u32[]{:S(2)}) collective-permute-start(f32[128,1024]{1,0:T(8,128)} %shard_map.124.refs_0_), channel_id=1, source_target_pairs={{0,8},{4,12},{8,0},{12,4},{16,24},{20,28},{24,16},{28,20},{1,9},{5... | collective-permute-start | bytes 1572872 | tf_op jit(solution)/shard_map/ppermute | solution.py:522
  243.3 20.8 %collective-permute-start.31 = (f32[64,1024]{1,0:T(8,128)S(1)}, f32[64,1024]{1,0:T(8,128)S(1)}, u32[]{:S(2)}, u32[]{:S(2)}) collective-permute-start(f32[64,1024]{1,0:T(8,128)S(1)} %get-tuple-element.194.refs_0_), channel_id=1, source_target_pairs={{0,16},{4,20},{8,24},{12,28},{16,0},{20,4},{24,8},{28,12},{1,17},{... | collective-permute-start | bytes 786440 | tf_op jit(solution)/shard_map/ppermute | solution.py:522
  269.5 26.4 %collective-permute-start.39 = (f32[256,1024]{1,0:T(8,128)S(1)}, f32[256,1024]{1,0:T(8,128)S(1)}, u32[]{:S(2)}, u32[]{:S(2)}) collective-permute-start(f32[256,1024]{1,0:T(8,128)S(1)} %shard_map.127.refs_0_.near.refs_4_), channel_id=1, source_target_pairs={{0,4},{4,0},{8,12},{12,8},{16,20},{20,16},{24,28},{28,24},{1,5},{5... | collective-permute-start | bytes 3145736 | tf_op jit(solution)/shard_map/ppermute | solution.py:522
  270.0 25.9 %collective-permute-start.40 = (f32[2048,128]{1,0:T(8,128)S(1)}, f32[2048,128]{1,0:T(8,128)S(1)}, u32[]{:S(2)}, u32[]{:S(2)}) collective-permute-start(f32[2048,128]{1,0:T(8,128)S(1)} %get-tuple-element.206), channel_id=1, source_target_pairs={{0,2},{1,3},{2,0},{3,1},{4,6},{5,7},{6,4},{7,5},{8,10},{9,11},{10,... | collective-permute-start | bytes 3145736 | tf_op jit(solution)/shard_map/ppermute | solution.py:522
  271.4 24.5 %collective-permute-start.28 = (f32[8,1152]{1,0:T(8,128)S(1)}, f32[8,1152]{1,0:T(8,128)S(1)}, u32[]{:S(2)}, u32[]{:S(2)}) collective-permute-start(f32[8,1152]{1,0:T(8,128)S(1)} %shard_map.122.a), channel_id=1, source_target_pairs={{0,4},{4,0},{8,12},{12,8},{16,20},{20,16},{24,28},{28,24},{1,5},{5... | collective-permute-start | bytes 110600 | tf_op jit(solution)/shard_map/ppermute | solution.py:522
  296.1 25.6 %collective-permute-start.38 = (f32[256,1024]{1,0:T(8,128)S(1)}, f32[256,1024]{1,0:T(8,128)S(1)}, u32[]{:S(2)}, u32[]{:S(2)}) collective-permute-start(f32[256,1024]{1,0:T(8,128)S(1)} %shard_map.131.refs_0_.near.refs_6_), channel_id=1, source_target_pairs={{0,4},{4,0},{8,12},{12,8},{16,20},{20,16},{24,28},{28,24},{1,5},{5... | collective-permute-start | bytes 3145736 | tf_op jit(solution)/shard_map/ppermute | solution.py:522
  297.1 25.2 %collective-permute-start.42 = (f32[2048,128]{1,0:T(8,128)S(1)}, f32[2048,128]{1,0:T(8,128)S(1)}, u32[]{:S(2)}, u32[]{:S(2)}) collective-permute-start(f32[2048,128]{1,0:T(8,128)S(1)} %get-tuple-element.210), channel_id=1, source_target_pairs={{0,2},{1,3},{2,0},{3,1},{4,6},{5,7},{6,4},{7,5},{8,10},{9,11},{10,... | collective-permute-start | bytes 3145736 | tf_op jit(solution)/shard_map/ppermute | solution.py:522
  322.5 54.8 %collective-permute-start.44 = (f32[2048,128]{1,0:T(8,128)}, f32[2048,128]{1,0:T(8,128)S(1)}, u32[]{:S(2)}, u32[]{:S(2)}) collective-permute-start(f32[2048,128]{1,0:T(8,128)} %get-tuple-element.215), channel_id=1, source_target_pairs={{0,2},{1,3},{2,0},{3,1},{4,6},{5,7},{6,4},{7,5},{8,10},{9,11},{10,... | collective-permute-start | bytes 3145736 | tf_op jit(solution)/shard_map/ppermute | solution.py:522
  337.8 39.5 %collective-permute-start.45 = (f32[2048,128]{1,0:T(8,128)}, f32[2048,128]{1,0:T(8,128)}, u32[]{:S(2)}, u32[]{:S(2)}) collective-permute-start(f32[2048,128]{1,0:T(8,128)} %get-tuple-element.216), channel_id=1, source_target_pairs={{0,2},{1,3},{2,0},{3,1},{4,6},{5,7},{6,4},{7,5},{8,10},{9,11},{10,... | collective-permute-start | bytes 3145736 | tf_op jit(solution)/shard_map/ppermute | solution.py:522
  (58 other events, 725.1 us)

commit v3 on v2

--- a/solution.py
+++ b/solution.py
@@ -174,83 +174,110 @@
     )(sums, *mparts)
 
 
-def turn(logits, th, tl):
-    @pl.when(pl.program_id(0) == 0)
-    def _():
-        th[...], tl[...] = split(jnp.transpose(jnp.exp(logits[...])))
-
-
-def send_body(order, logits, source, out, th, tl):
-    turn(logits, th, tl)
-    out[...] = dot3(th[...], tl[...], *split(source[...]), 1, 0)
-
-
-def keep_body(order, th, tl, source, out):
-    out[...] = dot3(th[...], tl[...], *split(source[...]), 1, 0)
-
-
-def both_body(across, order, logits, near, far, keep, send, th, tl):
-    turn(logits, th, tl)
-    first = dot3(th[...], tl[...], *split(near[...]), 1, 0)
-    second = dot3(th[...], tl[...], *split(far[...]), 1, 0)
-    if not across:
-        keep[...], send[...] = first, second
-        return
-    number = pl.num_programs(0) // 2
-
-    @pl.when(pl.program_id(0) < number)
-    def _():
-        keep[0], keep[1] = first, second
-
-    @pl.when(pl.program_id(0) >= number)
-    def _():
-        send[0], send[1] = first, second
-
-
-def predict(kind, order, expression, unit, column, width, logits, turned=None):
+def below(total, shard, count):
+    if total.shape[1] < shard:
+        total = jnp.concatenate([total, jnp.zeros((1, shard - total.shape[1]), F32)], axis=1)
+    lines = [total[:, at : at + shard] for at in range(0, total.shape[1], shard)]
+    rows = jnp.concatenate(lines + [jnp.zeros((8 - len(lines), shard), F32)], axis=0)
+    return jnp.concatenate([rows] * count, axis=1)
+
+
+def predict_body(shard, given, widths, send_only, order, *refs):
+    refs = list(refs)
+    if given:
+        gh, gl, gtotal = refs[:3]
+        refs = refs[3:]
+    if widths:
+        logits, refs = refs[0], refs[1:]
+    near = None if send_only else refs.pop(0)
+    far = refs.pop(0) if widths else None
+    if widths:
+        total, refs = refs[-1], refs[:-1]
+        th, tl, refs = refs[-2], refs[-1], refs[:-2]
+
+        @pl.when(pl.program_id(0) == 0)
+        def _():
+            vals = jnp.exp(logits[...])
+            total[...] = jnp.broadcast_to(jnp.sum(vals, axis=0, keepdims=True), total.shape)
+            th[...], tl[...] = split(jnp.transpose(vals))
+
+    count = (far if near is None else near).shape[1] // shard
+    outs = iter(refs)
+    if not send_only:
+        near = split(near[...])
+    if widths:
+        far = split(far[...])
+    if given:
+        out, width = next(outs), gh.shape[0]
+        out[:width] = dot3(gh[...], gl[...], *near, 1, 0)
+        out[width:] = below(gtotal[:1], shard, count)
+    if widths:
+        kept = None if send_only else dot3(th[...], tl[...], *near, 1, 0)
+        sent = dot3(th[...], tl[...], *far, 1, 0)
+        at = 0
+        for width in widths:
+            rows = below(total[:1, at : at + width], shard, count)
+            for vals in (kept, sent):
+                if vals is not None:
+                    out = next(outs)
+                    out[:width] = vals[at : at + width]
+                    out[width:] = rows
+            at += width
+
+
+def predict(order, expression, unit, shard, given, logits, start, widths, send_only=False):
     rows, genes = expression.shape
     count = genes // 2 // unit
-    near = pl.BlockSpec((rows, unit), lambda i, order: (0, order[i]))
-    far = pl.BlockSpec((rows, unit), lambda i, order: (0, order[count + i]))
-    piece = pl.BlockSpec((rows, width), lambda i, order: (0, column))
-    flipped = pl.BlockSpec((width, rows), lambda i, order: (0, 0))
-    block = pl.BlockSpec((width, unit), lambda i, order: (0, i))
-    half = shape_of(width, genes // 2)
-    scratch = []
-    if kind == "send":
-        body, args, ins = send_body, (logits, expression), [piece, far]
-        outs, shapes = [block, flipped, flipped], [half] + [hbm(width, rows, BF16)] * 2
-    elif kind == "keep":
-        body, args, ins = keep_body, (*turned, expression), [flipped, flipped, near]
-        outs, shapes = block, half
-    else:
-        body, args = functools.partial(both_body, kind == "across"), (logits, expression, expression)
-        ins, scratch = [piece, near, far], [pltpu.VMEM((width, rows), BF16)] * 2
-        outs, shapes = [block, block], [half, half]
-        if kind == "across":
-            mid = count // 2
-            shapes = [shape_of(2, width, genes // 4)] * 2
-            outs = [
-                pl.BlockSpec((2, width, unit), lambda i, order: (0, 0, jnp.minimum(i, mid - 1))),
-                pl.BlockSpec((2, width, unit), lambda i, order: (0, 0, jnp.maximum(i - mid, 0))),
-            ]
-    return pl.pallas_call(
-        body,
+    args, ins = [], []
+    outs, shapes, scratch = [], [], []
+
+    def add_out(width):
+        outs.append(pl.BlockSpec((width + 8, unit), lambda i, order: (0, i)))
+        shapes.append(shape_of(width + 8, genes // 2))
+
+    if given is not None:
+        width = given[0].shape[0]
+        args += given
+        ins += [pl.BlockSpec((width, rows), lambda i, order: (0, 0))] * 2
+        ins += [pl.BlockSpec((8, width), lambda i, order: (0, 0))]
+        add_out(width)
+    wide = sum(widths)
+    if widths:
+        args.append(logits)
+        ins.append(pl.BlockSpec((rows, wide), lambda i, order: (0, start // wide)))
+        for width in widths:
+            for _ in range(1 if send_only else 2):
+                add_out(width)
+    if not send_only:
+        args.append(expression)
+        ins.append(pl.BlockSpec((rows, unit), lambda i, order: (0, order[i])))
+    if widths:
+        args.append(expression)
+        ins.append(pl.BlockSpec((rows, unit), lambda i, order: (0, order[count + i])))
+        if send_only:
+            outs += [pl.BlockSpec((wide, rows), lambda i, order: (0, 0))] * 2
+            outs += [pl.BlockSpec((8, wide), lambda i, order: (0, 0))]
+            shapes += [hbm(wide, rows, BF16)] * 2 + [shape_of(8, wide)]
+        else:
+            scratch = [pltpu.VMEM((wide, rows), BF16)] * 2 + [pltpu.VMEM((8, wide), F32)]
+    return pl.pallas_call(
+        functools.partial(predict_body, shard, given is not None, widths, send_only),
         grid_spec=pltpu.PrefetchScalarGridSpec(
             num_scalar_prefetch=1, grid=(count,), in_specs=ins, out_specs=outs, scratch_shapes=scratch
         ),
         out_shape=shapes,
-        compiler_params=params(56),
-        cost_estimate=cost(3 * rows * genes * width, rows * genes * 4),
+        compiler_params=params(60),
+        cost_estimate=cost(0, 0),
     )(order, *args)
 
 
-def stats_body(turn, kept, came, sums, spatial, mask, onehot, pred, spots, genes):
-    total = jnp.sum(sums[...], axis=0, keepdims=True)
+def stats_body(width, kept, came, spatial, mask, onehot, pred, spots, genes, totals):
     vals = kept[...] + came[...]
-    if turn:
-        vals = jnp.transpose(vals)
-    vals = vals / total
+    lines = max(1, width // vals.shape[1])
+    total = jnp.concatenate([vals[width + n : width + n + 1] for n in range(lines)], axis=1)
+    total = total[:, :width]
+    totals[...] = jnp.concatenate([total, jnp.zeros((7, width), F32)], axis=0)
+    vals = jnp.transpose(vals[:width]) / total
     pred[...] = vals
     spat = spatial[...]
     seen = dot(mask[...].astype(BF16), onehot[...].astype(BF16), 0, 0)
@@ -260,34 +287,31 @@
     genes[...] = jnp.concatenate([exact(onehot[...], t, 1, 1) for t in terms], axis=0)
 
 
-def stats(kept, came, sums, spatial, mask, onehot, column):
-    width, shard = kept.shape
-    turn = shard % 128 == 0
-    if not turn:
-        kept, came = kept.T, came.T
-    whole = pl.BlockSpec((shard, width), lambda i: (0, 0))
+def stats(kept, came, spatial, mask, onehot, column, width):
+    shard = kept.shape[1]
+    strip = pl.BlockSpec((8, width), lambda i: (0, column))
+    once = pl.BlockSpec((8, width), lambda i: (0, 0))
     given = pl.BlockSpec(kept.shape, lambda i: (0, 0))
-    strip = pl.BlockSpec((8, width), lambda i: (0, column))
-    return pl.pallas_call(
-        functools.partial(stats_body, turn),
+    return pl.pallas_call(
+        functools.partial(stats_body, width),
         grid=(1,),
         in_specs=[
             given,
             given,
-            strip,
             pl.BlockSpec((shard, width), lambda i: (0, column)),
             pl.BlockSpec((8, shard), lambda i: (0, 0)),
             strip,
         ],
         out_specs=[
-            whole,
-            pl.BlockSpec((8, width), lambda i: (0, 0)),
+            pl.BlockSpec((shard, width), lambda i: (0, 0)),
+            once,
             pl.BlockSpec((24, shard), lambda i: (0, 0)),
+            once,
         ],
-        out_shape=[shape_of(shard, width), shape_of(8, width), shape_of(24, shard)],
+        out_shape=[shape_of(shard, width), shape_of(8, width), shape_of(24, shard), shape_of(8, width)],
         compiler_params=params(32),
-        cost_estimate=cost(shard * width * 40, shard * width * 16),
-    )(kept, came, sums, spatial, mask, onehot)
+        cost_estimate=cost(0, 0),
+    )(kept, came, spatial, mask, onehot)
 
 
 def grad_body(slides, spots_total, parts, *refs):
@@ -411,14 +435,19 @@
     )(ids, near, far, across, *mparts, *pparts)
 
 
-def logit_body(pieces, heights, unit, scale, order, dens, sums, inner, source, mh, ml, *refs):
+def logit_body(pieces, heights, unit, offset, scale, final, added, order, *refs):
+    if final:
+        dens, sums, inner, *refs = refs
+    source, mh, ml, *refs = refs
+    if added:
+        part, *refs = refs
     grads, (out, dh, dl) = refs[:-3], refs[-3:]
+    high = sum(heights)
 
     @pl.when(pl.program_id(0) == 0)
     def _():
-        shard = sum(heights)
         for p in range(pieces):
-            base = order[p * shard // unit] * unit + p * shard % unit
+            base = order[p] * high
             at = 0
             for q, height in enumerate(heights):
                 grad = grads[2 * q + (p >= pieces // 2)]
@@ -427,37 +456,53 @@
                 dh[rows, :], dl[rows, :] = split(grad[inside * height : (inside + 1) * height, :])
                 at += height
 
-    inv = 1.0 / jnp.sum(sums[...], axis=0, keepdims=True)
-    column = jnp.transpose(dens[...])[:, :1]
-    vals = dot3(*split(source[...]), dh[...], dl[...], 1, 0) + (column - inner[...][:1]) * inv
-    out[...] = (mh[...].astype(F32) + ml[...].astype(F32)) * vals * scale
-
-
-def logit_part(order, dens, sums, inner, expression, mparts, grads, heights, pieces, unit, scale):
+    if offset is None:
+        vals = source[...]
+    else:
+        vals = jnp.concatenate(
+            [source[:, p * unit + offset : p * unit + offset + high] for p in range(pieces)], axis=1
+        )
+    vals = dot3(*split(vals), dh[...], dl[...], 1, 0)
+    if added:
+        vals = vals + part[...]
+    if final:
+        inv = 1.0 / jnp.sum(sums[...], axis=0, keepdims=True)
+        column = jnp.transpose(dens[...])[:, :1]
+        vals = vals + (column - inner[...][:1]) * inv
+        vals = (mh[...].astype(F32) + ml[...].astype(F32)) * vals * scale
+    out[...] = vals
+
+
+def logit_part(order, ends, expression, mparts, part, grads, heights, offset, pieces, unit, scale):
     rows, cols = mparts[0].shape
     genes = expression.shape[1]
     step = 256
     strip = pl.BlockSpec((8, cols), lambda i, order: (0, 0))
     tile = pl.BlockSpec((step, cols), lambda i, order: (i, 0))
-    return pl.pallas_call(
-        functools.partial(logit_body, pieces, heights, unit, scale),
+    added, final = part is not None, ends is not None
+    ins = [pl.BlockSpec((step, genes), lambda i, order: (i, 0)), tile, tile]
+    args = [expression, *mparts]
+    if final:
+        ins = [pl.BlockSpec((8, step), lambda i, order: (0, i)), strip, strip] + ins
+        args = [*ends, *args]
+    if added:
+        ins.append(tile)
+        args.append(part)
+    for g in grads:
+        ins.append(pl.BlockSpec(g.shape, lambda i, order: (0, 0), pipeline_mode=pl.Buffered(1)))
+    return pl.pallas_call(
+        functools.partial(logit_body, pieces, heights, unit, offset, scale, final, added),
         grid_spec=pltpu.PrefetchScalarGridSpec(
             num_scalar_prefetch=1,
             grid=(rows // step,),
-            in_specs=[pl.BlockSpec((8, step), lambda i, order: (0, i)), strip, strip]
-            + [pl.BlockSpec((step, genes), lambda i, order: (i, 0))]
-            + [tile] * 2
-            + [
-                pl.BlockSpec(g.shape, lambda i, order: (0, 0), pipeline_mode=pl.Buffered(1))
-                for g in grads
-            ],
+            in_specs=ins,
             out_specs=tile,
-            scratch_shapes=[pltpu.VMEM((genes, cols), BF16)] * 2,
+            scratch_shapes=[pltpu.VMEM((pieces * sum(heights), cols), BF16)] * 2,
         ),
         out_shape=shape_of(rows, cols),
         compiler_params=params(56),
-        cost_estimate=cost(6 * rows * cols * genes, rows * genes * 4 + rows * cols * 8),
-    )(order, dens, sums, inner, expression, *mparts, *grads)
+        cost_estimate=cost(0, 0),
+    )(order, *args, *grads)
 
 
 def join_body(shards, heights, scale, *refs):
@@ -547,10 +592,11 @@
     other_logits = swap(logits, "spot", 0)
     order = me ^ reverse(jnp.arange(cells, dtype=jnp.int32), cell_bits)
     unit = 256
-    source = expression
+    source, blocks_order = expression, order
     if shard != unit:
         source = source.reshape(rows, cells, shard)[:, order].reshape(rows, genes)
-        order = jnp.arange(genes // unit, dtype=jnp.int32)
+        blocks_order = jnp.arange(genes // unit, dtype=jnp.int32)
+        order = jnp.arange(cells, dtype=jnp.int32)
 
     mask8 = jnp.pad(masks.astype(F32), ((0, 8 - slides), (0, 0)))
     mask8 = lax.dynamic_slice_in_dim(mask8, me * shard, shard, 1)
@@ -561,78 +607,85 @@
 
     line = Line()
 
-    width = 256
-    number = cols // width
-    generic = not (cells == 8 and shard == unit and number == 4)
-    cross = -1 if generic else 1
-    keeps, sends, steps, found, turned, parts = {}, {}, {}, {}, {}, {}
-
-    def make(kind, q):
-        given = turned.get(q)
-        if kind == "keep":
-            given = line(given[0]), given[1]
-        outs = predict(kind, order, source, unit, q, width, line(logits), given)
-        if kind == "send":
-            sends[q], *turned[q] = outs
-        elif kind == "keep":
-            keeps[q] = outs
-        else:
-            keeps[q], sends[q] = outs
-        line.mark(keeps.get(q, sends.get(q)))
-        if kind != "keep":
-            found[q] = swap(sends[q], "cell", 1 if q == cross else 0)
+    widths = (256, 256, 256, 128, 128)
+    starts = [sum(widths[:q]) for q in range(len(widths))]
+    generic = cell_bits != 3
+    piece = min(shard, unit)
+    keeps, steps, found, parts = {}, {}, {}, {}
+
+    def make(*chunks, given=None):
+        outs = predict(
+            blocks_order,
+            source,
+            unit,
+            piece,
+            given,
+            line(logits),
+            starts[chunks[0]],
+            tuple(widths[q] for q in chunks),
+        )
+        line.mark(outs[0])
+        if given is not None:
+            keeps[chunks[0] - 1], *outs = outs
+        for n, q in enumerate(chunks):
+            keeps[q] = outs[2 * n]
+            found[q] = swap(outs[2 * n + 1], "cell", 0)
 
     def step(q):
-        bits = (1, 0, 2) if q == cross else tuple(range(cell_bits))
         at = steps.get(q, 0)
         steps[q] = at + 1
+        came = line(found[q])
         if at < cell_bits - 1:
-            kept, came = keeps[q], line(found[q])
-            kept, out = add_split(kept, came)
+            keeps[q], out = add_split(keeps[q], came)
             line.mark(out)
-            keeps[q] = kept
-            found[q] = swap(out, "cell", bits[at + 1])
+            found[q] = swap(out, "cell", at + 1)
         else:
-            keeps[q] = stats(keeps[q], line(found[q]), parts["sums"].end(), spatial, mask8, onehot, q)
+            keeps[q] = stats(
+                keeps[q], came, spatial, mask8, onehot, starts[q] // widths[q], widths[q]
+            )
             line.mark(keeps[q][0])
 
     def own_exps():
-        *parts["m"], sums = exp_split(line(logits), True)
-        line.mark(sums)
-        parts["sums"] = Total(line, sums, "cell", [*range(1, cell_bits), 0])
+        parts["m"] = exp_split(line(logits), False)
+        line.mark(parts["m"][0])
 
     def other_exps():
         parts["p"] = exp_split(line(other_logits), False)
         line.mark(parts["p"][0])
 
     def masses():
-        parts["mass"] = mass_rows(line(parts["sums"].end()), parts["m"])
-        line.mark(parts["mass"])
-
+        mass = mass_rows(line(sums), parts["m"])
+        mass = jnp.concatenate([mass, jnp.broadcast_to(losses[0, 1], (8, 128))], axis=1)
+        line.mark(mass)
+        parts["mass"] = Total(line, mass, "spot", range(spots_n.bit_length() - 1))
+
+    out, *first = predict(
+        blocks_order, source, unit, piece, None, logits, 0, widths[:1], send_only=True
+    )
+    line.mark(out)
+    found[0] = swap(out, "cell", 0)
+    make(1, given=first)
+    own_exps()
     if generic:
-        own_exps()
-        for q in range(number):
-            make("both", q)
-        masses(), other_exps()
+        make(2), make(3, 4), other_exps()
         for _ in range(cell_bits):
-            for q in range(number):
+            for q in range(len(widths)):
                 step(q)
     else:
-        make("send", 0), own_exps(), make("send", 2), parts["sums"].next(), make("keep", 0)
-        parts["sums"].next(), step(0), make("across", 1), make("both", 3), make("keep", 2), step(2)
-        step(0), step(1), other_exps(), step(2), step(3), step(0), masses()
-        step(1), step(2), step(3), step(1), step(3)
-    sums, mparts, pparts = parts["sums"].end(), parts["m"], parts["p"]
+        step(0), make(2), step(0), step(1), make(3, 4), step(0), step(1), step(2)
+        other_exps(), step(2), step(3), step(1), step(4), step(3), step(2), step(4)
+        step(3), step(4)
+    number = len(widths)
+    sums = jnp.concatenate([keeps[q][3] for q in range(number)], axis=1)
+    mparts, pparts = parts["m"], parts["p"]
     preds = [keeps[q][0] for q in range(number)]
     spot_stats = [keeps[q][1] for q in range(number)]
     gene_stats = sum(keeps[q][2] for q in range(number))
-    spot_stats = add_all(jnp.concatenate(spot_stats, axis=1), "cell")
-    mass = parts["mass"][:1].reshape(-1, shard)
-    joint = add_all(jnp.concatenate([gene_stats, mass], axis=0), "spot")
-    gene_stats = joint[:24]
-    mass = joint[24:].reshape(1, rows) / spots_total
-    density_part = -jnp.sum(jnp.log(cells_total * mass)) / cells_total
-    dens = jnp.broadcast_to(-1.0 / (cells_total * spots_total * mass), (8, rows))
+    spot_stats = Total(line, jnp.concatenate(spot_stats, axis=1), "cell", range(cell_bits))
+    gene_stats = Total(line, gene_stats, "spot", range(spots_n.bit_length() - 1))
+    for _ in range(2):
+        gene_stats.next(), spot_stats.next()
+    gene_stats, spot_stats = gene_stats.end(), spot_stats.end()
 
     heights = (shard // 4,) * 4
     *grads, inner, losses = gradient(
@@ -696,30 +749,38 @@
         widen(q, [0])
 
     def pull():
-        added = inner + pull_cols(line(dens), sums, mparts)
+        joint = parts["mass"].end()[:1]
+        mass, parts["spots"] = joint[:, :rows] / spots_total, joint[0, rows]
+        density_part = -jnp.sum(jnp.log(cells_total * mass)) / cells_total
+        parts["dens"] = jnp.broadcast_to(-1.0 / (cells_total * spots_total * mass), (8, rows))
+        added = inner + pull_cols(line(parts["dens"]), sums, mparts)
         added = jnp.concatenate(
             [added, jnp.broadcast_to(density_part - losses[0, 0], (8, 128))], axis=1
         )
         line.mark(added)
         parts["tail"] = Total(line, added, "cell", range(cell_bits - 1, -1, -1))
 
-    spot_bits = range(spots_n.bit_length() - 1)
-    parts["spots"] = Total(line, jnp.broadcast_to(losses[0, 1], (8, 128)), "spot", spot_bits)
-    first(0), parts["spots"].next(), pull(), parts["spots"].next(), second(0), first(1), third(0)
-    parts["tail"].next(), second(1), first(2), parts["tail"].next(), third(1), second(2), first(3)
-    share(0), multiply(0), third(2), second(3), share(1), multiply(1), third(3), parts["tail"].next()
+    def logits_of(chunks, ends, part, offset):
+        grads_of = [v for q in chunks for v in (nears[q], fars[q])]
+        size = [heights[q] for q in chunks]
+        out = logit_part(
+            order, ends, line(source), mparts, part, grads_of, size, offset, cells, unit, scale
+        )
+        line.mark(out)
+        return out
+
+    first(0), masses(), second(0), parts["mass"].next(), first(1), second(1), third(0), first(2)
+    pull(), third(1), second(2), first(3), share(0), multiply(0), third(2), second(3)
+    share(1), multiply(1), third(3), parts["tail"].next()
     line.also(arrived[0])
-    share(2), multiply(2)
+    share(2), multiply(2), parts["tail"].next()
     line.also(arrived[1])
     share(3), multiply(3)
     tail = parts["tail"].end()
-    loss = tail[0, cols] - parts["spots"].end()[0, 0]
+    loss = tail[0, cols] - parts["spots"]
     pairs = [pairs[q] for q in range(number)]
-    gathered = [v for q in range(number) for v in (nears[q], fars[q])]
-
-    logit_grad = logit_part(
-        order, line(dens), sums, tail[:, :cols], source, mparts, gathered, heights, cells, unit, scale
-    )
+    ends = parts["dens"], sums, tail[:, :cols]
+    logit_grad = logits_of(range(number), ends, None, None)
     expr_grad = join(pairs, heights, per_block, scale)
     return (loss, logit_grad, expr_grad)
 

time: 384 us -> 356 us (0.927)
  waiting for transfers between devices: 120 us -> 106 us
  Pallas kernels: 192 us -> 183 us
    ppermute x46, waiting for transfers between devices: 120 us -> 106 us  [swap(): return lax.ppermute(v, axis, [(i, i ^ 1 << bit) for i in range(size)])]
    pallas_call x11 -> x10, Pallas kernels: 101 us -> 92.3 us  [the longest x4 51.9 us: predict(): pl.pallas_call(functools.partial(predict_body, shard, given is not None,...]
    unnamed x76 -> x73, local copies, waits for them, and re-layouts: 10.4 us -> 7.09 us
    pallas_call x33 -> x32, Pallas kernels: 12.1 us -> 11.8 us  [simple(): pl.pallas_call(body, grid_spec=pltpu.PrefetchScalarGridSpec(num_scalar_pr...]
  transfers between devices with their start and end apart: 46 -> 46, of which waited for: 21 -> 29; matrix products, arithmetic and copies ran while one was open for 2% -> 2% of each run, Pallas kernels for 47% -> 49%
where the time goes in v3:
time: 356 us; the launch traced here: 355 us
  Pallas kernels  183 us (51%)
  waiting for transfers between devices  106 us (30%)
  starting transfers between devices  47.7 us (13%)
  local copies, waits for them, and re-layouts  11.7 us (3%)
  between operations  4.89 us (1%)
    ppermute x46, waiting for transfers between devices, swap(): return lax.ppermute(v, axis, [(i, i ^ 1 << bit) for i in range(size)])  106 us
    pallas_call x4, Pallas kernels, predict(): pl.pallas_call(functools.partial(predict_body, shard, given is not None,...  51.9 us
    ppermute x46, starting transfers between devices, swap(): return lax.ppermute(v, axis, [(i, i ^ 1 << bit) for i in range(size)])  47.7 us
    pallas_call x4, Pallas kernels, expr_part(): pl.pallas_call(functools.partial(expr_body, number, height, half), grid_s...  46.5 us
    pallas_call x1, Pallas kernels, logit_part(): pl.pallas_call(functools.partial(logit_body, pieces, heights, unit, offse...  36 us
    pallas_call x2, Pallas kernels, exp_split(): pl.pallas_call(functools.partial(exp_body, with_sums), grid=(rows // step...  12.5 us
    pallas_call x32, Pallas kernels, simple(): pl.pallas_call(body, grid_spec=pltpu.PrefetchScalarGridSpec(num_scalar_pr...  11.8 us
  transfers between devices with their start and end apart: 46, of which 29 were waited for; matrix products, arithmetic and copies ran while one was open for 2% of the time, Pallas kernels for 49%

profile of v3, /device:TPU:0, one launch (start us, length us, event | category | flops | bytes accessed | tf_op | source)
XLA Modules:
  0.0 355.3 jit_solution(2886697829786016285)
XLA Ops:
  1.7 9.2 %shard_map.85 = (f32[264,1024]{1,0:T(8,128)}, bf16[256,2048]{1,0:T(8,128)(2,1)}, bf16[256,2048]{1,0:T(8,128)(2,1)}, f32[8,256]{1,0:T(8,128)}) custom-call(s32[8]{0:T(128)} %fusion.7.order, f32[2048,1024]{1,0:T(8,128)} %refs_0_.3, f32[2048,2048]{1,0:T(8,128)} %refs_3_.1), custom_call_target="tpu_custom_call" | custom-call | tf_op jit(solution)/shard_map/pallas_call | solution.py:263
  13.4 16.3 %shard_map.86 = (f32[264,1024]{1,0:T(8,128)}, f32[264,1024]{1,0:T(8,128)}, f32[264,1024]{1,0:T(8,128)}) custom-call(s32[8]{0:T(128)} %fusion.7.order, bf16[256,2048]{1,0:T(8,128)(2,1)} %get-tuple-element.127.refs_0_, bf16[256,2048]{1,0:T(8,128)(2,1)} %get-tuple-element.128.refs_1_, f32[8,256]{1,0:T(8,128)} %get-tuple-element.129.refs_2_, ...), custom_call_target="tpu_custom_call" | custom-call | tf_op jit(solution)/shard_map/pallas_call | solution.py:263
  29.7 6.2 %shard_map.87 = (bf16[2048,1024]{1,0:T(8,128)(2,1)}, bf16[2048,1024]{1,0:T(8,128)(2,1)}) custom-call(f32[2048,1024]{1,0:T(8,128)} %refs_0_.3), custom_call_target="tpu_custom_call" | custom-call | tf_op jit(solution)/shard_map/pallas_call | solution.py:145
  41.3 13.2 %shard_map.89 = (f32[264,1024]{1,0:T(8,128)}, f32[264,1024]{1,0:T(8,128)}) custom-call(s32[8]{0:T(128)} %fusion.7.order, f32[2048,1024]{1,0:T(8,128)} %refs_0_.3, f32[2048,2048]{1,0:T(8,128)} %refs_3_.1, f32[2048,2048]{1,0:T(8,128)} %refs_3_.1), custom_call_target="tpu_custom_call" | custom-call | tf_op jit(solution)/shard_map/pallas_call | solution.py:263
  57.7 3.7 %collective-permute-done.3.came = f32[264,1024]{1,0:T(8,128)S(1)} collective-permute-done((f32[264,1024]{1,0:T(8,128)}, f32[264,1024]{1,0:T(8,128)S(1)}, u32[]{:S(2)}, u32[]{:S(2)}) %collective-permute-start.3) | collective-permute-done | bytes 1081376 | tf_op jit(solution)/shard_map/ppermute | solution.py:567
  67.1 13.2 %shard_map.92 = (f32[136,1024]{1,0:T(8,128)}, f32[136,1024]{1,0:T(8,128)}, f32[136,1024]{1,0:T(8,128)}, f32[136,1024]{1,0:T(8,128)}) custom-call(s32[8]{0:T(128)} %fusion.7.order, f32[2048,1024]{1,0:T(8,128)} %refs_0_.3, f32[2048,2048]{1,0:T(8,128)} %refs_3_.1, f32[2048,2048]{1,0:T(8,128)} %refs_3_.1), custom_call_target="tpu_custom_call" | custom-call | tf_op jit(solution)/shard_map/pallas_call | solution.py:263
  89.8 6.3 %shard_map.96 = (bf16[2048,1024]{1,0:T(8,128)(2,1)}, bf16[2048,1024]{1,0:T(8,128)(2,1)}) custom-call(f32[2048,1024]{1,0:T(8,128)} %collective-permute-done.9.logits), custom_call_target="tpu_custom_call" | custom-call | tf_op jit(solution)/shard_map/pallas_call | solution.py:145
  96.1 10.0 %collective-permute-done.8.came = f32[264,512]{1,0:T(8,128)S(1)} collective-permute-done((f32[264,512]{1,0:T(8,128)S(1)}, f32[264,512]{1,0:T(8,128)S(1)}, u32[]{:S(2)}, u32[]{:S(2)}) %collective-permute-start.8) | collective-permute-done | bytes 540704 | tf_op jit(solution)/shard_map/ppermute | solution.py:567
  112.9 8.3 %collective-permute-done.11.came = f32[136,512]{1,0:T(8,128)S(1)} collective-permute-done((f32[136,512]{1,0:T(8,128)S(1)}, f32[136,512]{1,0:T(8,128)S(1)}, u32[]{:S(2)}, u32[]{:S(2)}) %collective-permute-start.11) | collective-permute-done | bytes 278560 | tf_op jit(solution)/shard_map/ppermute | solution.py:567
  121.3 9.5 %collective-permute-done.10.came = f32[264,256]{1,0:T(8,128)S(1)} collective-permute-done((f32[264,256]{1,0:T(8,128)S(1)}, f32[264,256]{1,0:T(8,128)S(1)}, u32[]{:S(2)}, u32[]{:S(2)}) %collective-permute-start.10) | collective-permute-done | bytes 270368 | tf_op jit(solution)/shard_map/ppermute | solution.py:567
  134.3 4.5 %collective-permute-done.15.came = f32[136,256]{1,0:T(8,128)S(1)} collective-permute-done((f32[136,256]{1,0:T(8,128)S(1)}, f32[136,256]{1,0:T(8,128)S(1)}, u32[]{:S(2)}, u32[]{:S(2)}) %collective-permute-start.15) | collective-permute-done | bytes 139296 | tf_op jit(solution)/shard_map/ppermute | solution.py:567
  147.4 4.8 %collective-permute-done.20.b = f32[8,1024]{1,0:T(8,128)S(1)} collective-permute-done((f32[8,1024]{1,0:T(8,128)S(1)}, f32[8,1024]{1,0:T(8,128)S(1)}, u32[]{:S(2)}, u32[]{:S(2)}) %collective-permute-start.20) | collective-permute-done | bytes 32800 | tf_op jit(solution)/shard_map/ppermute | solution.py:567
  155.8 6.6 %shard_map.112 = f32[8,2048]{1,0:T(8,128)} custom-call(f32[8,1024]{1,0:T(8,128)} %copy-done.19, bf16[2048,1024]{1,0:T(8,128)(2,1)} %get-tuple-element.134.mh.refs_4_, bf16[2048,1024]{1,0:T(8,128)(2,1)} %get-tuple-element.210.ml.refs_5_), custom_call_target="tpu_custom_call" | custom-call | tf_op jit(solution)/shard_map/pallas_call | solution.py:166
  170.7 12.9 %collective-permute-done.25.refs_1_ = f32[64,1024]{1,0:T(8,128)S(1)} collective-permute-done((f32[64,1024]{1,0:T(8,128)S(1)}, f32[64,1024]{1,0:T(8,128)S(1)}, u32[]{:S(2)}, u32[]{:S(2)}) %collective-permute-start.25) | collective-permute-done | bytes 262176 | tf_op jit(solution)/shard_map/ppermute | solution.py:567
  195.4 5.7 %shard_map.118 = f32[8,1024]{1,0:T(8,128)} custom-call(f32[8,2048]{1,0:T(8,128)} %broadcast_in_dim.8.dens.refs_0_, f32[8,1024]{1,0:T(8,128)} %copy-done.19, bf16[2048,1024]{1,0:T(8,128)(2,1)} %get-tuple-element.134.mh.refs_4_, bf16[2048,1024]{1,0:T(8,128)(2,1)} %get-tuple-element.210.ml.refs_5_), custom_call_target="tpu_custom_call" | custom-call | tf_op jit(solution)/shard_map/pallas_call | solution.py:383
  214.1 11.5 %shard_map.122 = (f32[2048,128]{1,0:T(8,128)S(1)}, f32[2048,128]{1,0:T(8,128)S(1)}) custom-call(s32[8]{0:T(128)S(1)} %pad_add_fusion.ids, f32[256,1024]{1,0:T(8,128)S(1)} %shard_map.116.refs_0_.near.refs_6_, f32[256,1024]{1,0:T(8,128)S(1)} %collective-permute-done.31.refs_1_.far.refs_7_, f32[256,1024]{1,0:T(8,128)} %collective-permute-done.32.across, ...), custom_call_target="tpu_custom_call" | custom-call | tf_op jit(solution)/shard_map/pallas_call | solution.py:422
  225.7 6.0 %collective-permute-done.30.refs_1_ = f32[128,1024]{1,0:T(8,128)} collective-permute-done((f32[128,1024]{1,0:T(8,128)}, f32[128,1024]{1,0:T(8,128)}, u32[]{:S(2)}, u32[]{:S(2)}) %collective-permute-start.30) | collective-permute-done | bytes 524320 | tf_op jit(solution)/shard_map/ppermute | solution.py:567
  242.5 11.7 %shard_map.126 = (f32[2048,128]{1,0:T(8,128)S(1)}, f32[2048,128]{1,0:T(8,128)S(1)}) custom-call(s32[8]{0:T(128)S(1)} %pad_add_fusion.ids, f32[256,1024]{1,0:T(8,128)S(1)} %shard_map.119.refs_0_.near.refs_8_, f32[256,1024]{1,0:T(8,128)} %collective-permute-done.34.refs_1_.far.refs_9_, f32[256,1024]{1,0:T(8,128)S(1)} %collective-permute-done.35.across, ...), custom_call_target="tpu_custom_call" | custom-call | tf_op jit(solution)/shard_map/pallas_call | solution.py:422
  254.9 8.0 %collective-permute-done.37.refs_1_.far.refs_11_ = f32[256,1024]{1,0:T(8,128)S(1)} collective-permute-done((f32[256,1024]{1,0:T(8,128)S(1)}, f32[256,1024]{1,0:T(8,128)S(1)}, u32[]{:S(2)}, u32[]{:S(2)}) %collective-permute-start.37) | collective-permute-done | bytes 1048608 | tf_op jit(solution)/shard_map/ppermute | solution.py:567
  267.0 11.7 %shard_map.130 = (f32[2048,128]{1,0:T(8,128)S(1)}, f32[2048,128]{1,0:T(8,128)}) custom-call(s32[8]{0:T(128)S(1)} %pad_add_fusion.ids, f32[256,1024]{1,0:T(8,128)S(1)} %shard_map.123.refs_0_.near.refs_10_, f32[256,1024]{1,0:T(8,128)S(1)} %collective-permute-done.37.refs_1_.far.refs_11_, f32[256,1024]{1,0:T(8,128)S(1)} %collective-permute-done.39.across, ...), custom_call_target="tpu_custom_call" | custom-call | tf_op jit(solution)/shard_map/pallas_call | solution.py:422
  279.6 10.1 %collective-permute-done.41.refs_1_.far.refs_13_ = f32[256,1024]{1,0:T(8,128)S(1)} collective-permute-done((f32[256,1024]{1,0:T(8,128)S(1)}, f32[256,1024]{1,0:T(8,128)S(1)}, u32[]{:S(2)}, u32[]{:S(2)}) %collective-permute-start.41) | collective-permute-done | bytes 1048608 | tf_op jit(solution)/shard_map/ppermute | solution.py:567
  292.9 11.7 %shard_map.133 = (f32[2048,128]{1,0:T(8,128)S(1)}, f32[2048,128]{1,0:T(8,128)}) custom-call(s32[8]{0:T(128)S(1)} %pad_add_fusion.ids, f32[256,1024]{1,0:T(8,128)S(1)} %shard_map.127.refs_0_.near.refs_12_, f32[256,1024]{1,0:T(8,128)S(1)} %collective-permute-done.41.refs_1_.far.refs_13_, f32[256,1024]{1,0:T(8,128)S(1)} %collective-permute-done.43.across, ...), custom_call_target="tpu_custom_call" | custom-call | tf_op jit(solution)/shard_map/pallas_call | solution.py:422
  313.5 36.0 %shard_map.135 = f32[2048,1024]{1,0:T(8,128)} custom-call(s32[8]{0:T(128)} %fusion.7.order, f32[8,2048]{1,0:T(8,128)} %broadcast_in_dim.8.dens.refs_0_, f32[8,1024]{1,0:T(8,128)} %copy-done.19, f32[8,1024]{1,0:T(8,128)} %slice.30.refs_2_, f32[2048,2048]{1,0:T(8,128)} %refs_3_.1, bf16[2048,1024]{1,0:T(8,128)(2,1)} %get-tuple-element.134.mh.refs_4_, ...), custom_call_target="tpu_custom_call" | custom-call | tf_op jit(solution)/shard_map/pallas_call | solution.py:493
  349.5 4.6 %shard_map.136 = f32[2048,512]{1,0:T(8,128)} custom-call(f32[2048,128]{1,0:T(8,128)S(1)} %copy-done.14, f32[2048,128]{1,0:T(8,128)S(1)} %collective-permute-done.38.refs_1_, f32[2048,128]{1,0:T(8,128)S(1)} %get-tuple-element.235.refs_2_, f32[2048,128]{1,0:T(8,128)S(1)} %collective-permute-done.42.refs_3_, f32[2048,128]{1,0:T(8,128)S(1)} %copy-done.16, ...), custom_call_target="tpu_custom_call" | custom-call | tf_op jit(solution)/shard_map/pallas_call | solution.py:524
  (217 shorter events, 108.5 us)
Async XLA Ops:
  0.6 89.2 %collective-permute-start.9 = (f32[2048,1024]{1,0:T(8,128)}, f32[2048,1024]{1,0:T(8,128)}, u32[]{:S(2)}, u32[]{:S(2)}) collective-permute-start(f32[2048,1024]{1,0:T(8,128)} %refs_0_.3), channel_id=1, source_target_pairs={{0,1},{1,0},{2,3},{3,2},{4,5},{5,4},{6,7},{7,6},{8,9},{9,8},{10,11... | collective-permute-start | bytes 25165832 | tf_op jit(solution)/shard_map/ppermute | solution.py:567
  10.9 27.4 %collective-permute-start = (f32[264,1024]{1,0:T(8,128)}, f32[264,1024]{1,0:T(8,128)S(1)}, u32[]{:S(2)}, u32[]{:S(2)}) collective-permute-start(f32[264,1024]{1,0:T(8,128)} %get-tuple-element.130), channel_id=1, source_target_pairs={{0,4},{4,0},{8,12},{12,8},{16,20},{20,16},{24,28},{28,24},{1,5},{5... | collective-permute-start | bytes 3244040 | tf_op jit(solution)/shard_map/ppermute | solution.py:567
  29.7 31.8 %collective-permute-start.3 = (f32[264,1024]{1,0:T(8,128)}, f32[264,1024]{1,0:T(8,128)S(1)}, u32[]{:S(2)}, u32[]{:S(2)}) collective-permute-start(f32[264,1024]{1,0:T(8,128)} %get-tuple-element.144), channel_id=1, source_target_pairs={{0,4},{4,0},{8,12},{12,8},{16,20},{20,16},{24,28},{28,24},{1,5},{5... | collective-permute-start | bytes 3244040 | tf_op jit(solution)/shard_map/ppermute | solution.py:567
  54.4 31.6 %collective-permute-start.7 = (f32[264,1024]{1,0:T(8,128)}, f32[264,1024]{1,0:T(8,128)S(1)}, u32[]{:S(2)}, u32[]{:S(2)}) collective-permute-start(f32[264,1024]{1,0:T(8,128)} %get-tuple-element.156), channel_id=1, source_target_pairs={{0,4},{4,0},{8,12},{12,8},{16,20},{20,16},{24,28},{28,24},{1,5},{5... | collective-permute-start | bytes 3244040 | tf_op jit(solution)/shard_map/ppermute | solution.py:567
  62.4 22.4 %collective-permute-start.4 = (f32[264,512]{1,0:T(8,128)}, f32[264,512]{1,0:T(8,128)}, u32[]{:S(2)}, u32[]{:S(2)}) collective-permute-start(f32[264,512]{1,0:T(8,128)} %get-tuple-element.146), channel_id=1, source_target_pairs={{0,8},{4,12},{8,0},{12,4},{16,24},{20,28},{24,16},{28,20},{1,9},{5... | collective-permute-start | bytes 1622024 | tf_op jit(solution)/shard_map/ppermute | solution.py:567
  64.4 17.4 %collective-permute-start.2 = (f32[264,256]{1,0:T(8,128)}, f32[264,256]{1,0:T(8,128)}, u32[]{:S(2)}, u32[]{:S(2)}) collective-permute-start(f32[264,256]{1,0:T(8,128)} %get-tuple-element.142), channel_id=1, source_target_pairs={{0,16},{4,20},{8,24},{12,28},{16,0},{20,4},{24,8},{28,12},{1,17},{... | collective-permute-start | bytes 811016 | tf_op jit(solution)/shard_map/ppermute | solution.py:567
  80.3 25.9 %collective-permute-start.6 = (f32[136,1024]{1,0:T(8,128)}, f32[136,1024]{1,0:T(8,128)S(1)}, u32[]{:S(2)}, u32[]{:S(2)}) collective-permute-start(f32[136,1024]{1,0:T(8,128)} %get-tuple-element.155), channel_id=1, source_target_pairs={{0,4},{4,0},{8,12},{12,8},{16,20},{20,16},{24,28},{28,24},{1,5},{5... | collective-permute-start | bytes 1671176 | tf_op jit(solution)/shard_map/ppermute | solution.py:567
  81.8 26.5 %collective-permute-start.12 = (f32[136,1024]{1,0:T(8,128)}, f32[136,1024]{1,0:T(8,128)S(1)}, u32[]{:S(2)}, u32[]{:S(2)}) collective-permute-start(f32[136,1024]{1,0:T(8,128)} %get-tuple-element.171), channel_id=1, source_target_pairs={{0,4},{4,0},{8,12},{12,8},{16,20},{20,16},{24,28},{28,24},{1,5},{5... | collective-permute-start | bytes 1671176 | tf_op jit(solution)/shard_map/ppermute | solution.py:567
  86.2 19.9 %collective-permute-start.8 = (f32[264,512]{1,0:T(8,128)S(1)}, f32[264,512]{1,0:T(8,128)S(1)}, u32[]{:S(2)}, u32[]{:S(2)}) collective-permute-start(f32[264,512]{1,0:T(8,128)S(1)} %get-tuple-element.159), channel_id=1, source_target_pairs={{0,8},{4,12},{8,0},{12,4},{16,24},{20,28},{24,16},{28,20},{1,9},{5... | collective-permute-start | bytes 1622024 | tf_op jit(solution)/shard_map/ppermute | solution.py:567
  108.4 23.3 %collective-permute-start.14 = (f32[136,512]{1,0:T(8,128)S(1)}, f32[136,512]{1,0:T(8,128)S(1)}, u32[]{:S(2)}, u32[]{:S(2)}) collective-permute-start(f32[136,512]{1,0:T(8,128)S(1)} %get-tuple-element.173), channel_id=1, source_target_pairs={{0,8},{4,12},{8,0},{12,4},{16,24},{20,28},{24,16},{28,20},{1,9},{5... | collective-permute-start | bytes 835592 | tf_op jit(solution)/shard_map/ppermute | solution.py:567
  110.3 20.6 %collective-permute-start.10 = (f32[264,256]{1,0:T(8,128)S(1)}, f32[264,256]{1,0:T(8,128)S(1)}, u32[]{:S(2)}, u32[]{:S(2)}) collective-permute-start(f32[264,256]{1,0:T(8,128)S(1)} %get-tuple-element.163), channel_id=1, source_target_pairs={{0,16},{4,20},{8,24},{12,28},{16,0},{20,4},{24,8},{28,12},{1,17},{... | collective-permute-start | bytes 811016 | tf_op jit(solution)/shard_map/ppermute | solution.py:567
  167.2 18.6 %collective-permute-start.24 = (f32[128,1024]{1,0:T(8,128)S(1)}, f32[128,1024]{1,0:T(8,128)S(1)}, u32[]{:S(2)}, u32[]{:S(2)}) collective-permute-start(f32[128,1024]{1,0:T(8,128)S(1)} %shard_map.113.refs_0_), channel_id=1, source_target_pairs={{0,8},{4,12},{8,0},{12,4},{16,24},{20,28},{24,16},{28,20},{1,9},{5... | collective-permute-start | bytes 1572872 | tf_op jit(solution)/shard_map/ppermute | solution.py:567
  185.9 23.3 %collective-permute-start.31 = (f32[256,1024]{1,0:T(8,128)S(1)}, f32[256,1024]{1,0:T(8,128)S(1)}, u32[]{:S(2)}, u32[]{:S(2)}) collective-permute-start(f32[256,1024]{1,0:T(8,128)S(1)} %shard_map.116.refs_0_.near.refs_6_), channel_id=1, source_target_pairs={{0,4},{4,0},{8,12},{12,8},{16,20},{20,16},{24,28},{28,24},{1,5},{5... | collective-permute-start | bytes 3145736 | tf_op jit(solution)/shard_map/ppermute | solution.py:567
  186.5 17.3 %collective-permute-start.28 = (f32[128,1024]{1,0:T(8,128)S(1)}, f32[128,1024]{1,0:T(8,128)S(1)}, u32[]{:S(2)}, u32[]{:S(2)}) collective-permute-start(f32[128,1024]{1,0:T(8,128)S(1)} %shard_map.115.refs_0_), channel_id=1, source_target_pairs={{0,8},{4,12},{8,0},{12,4},{16,24},{20,28},{24,16},{28,20},{1,9},{5... | collective-permute-start | bytes 1572872 | tf_op jit(solution)/shard_map/ppermute | solution.py:567
  189.3 17.5 %collective-permute-start.27 = (f32[64,1024]{1,0:T(8,128)}, f32[64,1024]{1,0:T(8,128)}, u32[]{:S(2)}, u32[]{:S(2)}) collective-permute-start(f32[64,1024]{1,0:T(8,128)} %get-tuple-element.223.refs_0_), channel_id=1, source_target_pairs={{0,16},{4,20},{8,24},{12,28},{16,0},{20,4},{24,8},{28,12},{1,17},{... | collective-permute-start | bytes 786440 | tf_op jit(solution)/shard_map/ppermute | solution.py:567
  210.3 25.7 %collective-permute-start.34 = (f32[256,1024]{1,0:T(8,128)S(1)}, f32[256,1024]{1,0:T(8,128)}, u32[]{:S(2)}, u32[]{:S(2)}) collective-permute-start(f32[256,1024]{1,0:T(8,128)S(1)} %shard_map.119.refs_0_.near.refs_8_), channel_id=1, source_target_pairs={{0,4},{4,0},{8,12},{12,8},{16,20},{20,16},{24,28},{28,24},{1,5},{5... | collective-permute-start | bytes 3145736 | tf_op jit(solution)/shard_map/ppermute | solution.py:567
  211.7 20.0 %collective-permute-start.30 = (f32[128,1024]{1,0:T(8,128)}, f32[128,1024]{1,0:T(8,128)}, u32[]{:S(2)}, u32[]{:S(2)}) collective-permute-start(f32[128,1024]{1,0:T(8,128)} %shard_map.120.refs_0_), channel_id=1, source_target_pairs={{0,8},{4,12},{8,0},{12,4},{16,24},{20,28},{24,16},{28,20},{1,9},{5... | collective-permute-start | bytes 1572872 | tf_op jit(solution)/shard_map/ppermute | solution.py:567
  212.5 20.4 %collective-permute-start.29 = (f32[64,1024]{1,0:T(8,128)S(1)}, f32[64,1024]{1,0:T(8,128)S(1)}, u32[]{:S(2)}, u32[]{:S(2)}) collective-permute-start(f32[64,1024]{1,0:T(8,128)S(1)} %get-tuple-element.226.refs_0_), channel_id=1, source_target_pairs={{0,16},{4,20},{8,24},{12,28},{16,0},{20,4},{24,8},{28,12},{1,17},{... | collective-permute-start | bytes 786440 | tf_op jit(solution)/shard_map/ppermute | solution.py:567
  237.4 25.6 %collective-permute-start.37 = (f32[256,1024]{1,0:T(8,128)S(1)}, f32[256,1024]{1,0:T(8,128)S(1)}, u32[]{:S(2)}, u32[]{:S(2)}) collective-permute-start(f32[256,1024]{1,0:T(8,128)S(1)} %shard_map.123.refs_0_.near.refs_10_), channel_id=1, source_target_pairs={{0,4},{4,0},{8,12},{12,8},{16,20},{20,16},{24,28},{28,24},{1,5},{5... | collective-permute-start | bytes 3145736 | tf_op jit(solution)/shard_map/ppermute | solution.py:567
  238.8 25.2 %collective-permute-start.38 = (f32[2048,128]{1,0:T(8,128)S(1)}, f32[2048,128]{1,0:T(8,128)S(1)}, u32[]{:S(2)}, u32[]{:S(2)}) collective-permute-start(f32[2048,128]{1,0:T(8,128)S(1)} %get-tuple-element.238), channel_id=1, source_target_pairs={{0,2},{1,3},{2,0},{3,1},{4,6},{5,7},{6,4},{7,5},{8,10},{9,11},{10,... | collective-permute-start | bytes 3145736 | tf_op jit(solution)/shard_map/ppermute | solution.py:567
  264.2 25.6 %collective-permute-start.41 = (f32[256,1024]{1,0:T(8,128)S(1)}, f32[256,1024]{1,0:T(8,128)S(1)}, u32[]{:S(2)}, u32[]{:S(2)}) collective-permute-start(f32[256,1024]{1,0:T(8,128)S(1)} %shard_map.127.refs_0_.near.refs_12_), channel_id=1, source_target_pairs={{0,4},{4,0},{8,12},{12,8},{16,20},{20,16},{24,28},{28,24},{1,5},{5... | collective-permute-start | bytes 3145736 | tf_op jit(solution)/shard_map/ppermute | solution.py:567
  264.9 25.2 %collective-permute-start.42 = (f32[2048,128]{1,0:T(8,128)S(1)}, f32[2048,128]{1,0:T(8,128)S(1)}, u32[]{:S(2)}, u32[]{:S(2)}) collective-permute-start(f32[2048,128]{1,0:T(8,128)S(1)} %get-tuple-element.243), channel_id=1, source_target_pairs={{0,2},{1,3},{2,0},{3,1},{4,6},{5,7},{6,4},{7,5},{8,10},{9,11},{10,... | collective-permute-start | bytes 3145736 | tf_op jit(solution)/shard_map/ppermute | solution.py:567
  290.3 59.2 %collective-permute-start.44 = (f32[2048,128]{1,0:T(8,128)}, f32[2048,128]{1,0:T(8,128)S(1)}, u32[]{:S(2)}, u32[]{:S(2)}) collective-permute-start(f32[2048,128]{1,0:T(8,128)} %get-tuple-element.249), channel_id=1, source_target_pairs={{0,2},{1,3},{2,0},{3,1},{4,6},{5,7},{6,4},{7,5},{8,10},{9,11},{10,... | collective-permute-start | bytes 3145736 | tf_op jit(solution)/shard_map/ppermute | solution.py:567
  305.6 43.9 %collective-permute-start.45 = (f32[2048,128]{1,0:T(8,128)}, f32[2048,128]{1,0:T(8,128)}, u32[]{:S(2)}, u32[]{:S(2)}) collective-permute-start(f32[2048,128]{1,0:T(8,128)} %get-tuple-element.250), channel_id=1, source_target_pairs={{0,2},{1,3},{2,0},{3,1},{4,6},{5,7},{6,4},{7,5},{8,10},{9,11},{10,... | collective-permute-start | bytes 3145736 | tf_op jit(solution)/shard_map/ppermute | solution.py:567
  (55 other events, 749.0 us)

commit v4 on v3

--- a/solution.py
+++ b/solution.py
@@ -672,7 +672,7 @@
             for q in range(len(widths)):
                 step(q)
     else:
-        step(0), make(2), step(0), step(1), make(3, 4), step(0), step(1), step(2)
+        step(0), make(2), step(0), step(1), make(3, 4), step(0), step(2), step(1)
         other_exps(), step(2), step(3), step(1), step(4), step(3), step(2), step(4)
         step(3), step(4)
     number = len(widths)
@@ -775,8 +775,9 @@
     line.also(arrived[0])
     share(2), multiply(2), parts["tail"].next()
     line.also(arrived[1])
-    share(3), multiply(3)
+    share(3)
     tail = parts["tail"].end()
+    multiply(3)
     loss = tail[0, cols] - parts["spots"]
     pairs = [pairs[q] for q in range(number)]
     ends = parts["dens"], sums, tail[:, :cols]

time: 356 us -> 354 us (level)
    unnamed x73 -> x77, local copies, waits for them, and re-layouts: 7.09 us -> 7.9 us
  transfers between devices with their start and end apart: 46 -> 46, of which waited for: 29 -> 28; matrix products, arithmetic and copies ran while one was open for 2% -> 2% of each run, Pallas kernels for 49% -> 49%
where the time goes in v4:
time: 354 us; the launch traced here: 353 us
  Pallas kernels  183 us (52%)
  waiting for transfers between devices  103 us (29%)
  starting transfers between devices  47.2 us (13%)
  local copies, waits for them, and re-layouts  12.4 us (4%)
  between operations  4.98 us (1%)
    ppermute x46, waiting for transfers between devices, swap(): return lax.ppermute(v, axis, [(i, i ^ 1 << bit) for i in range(size)])  103 us
    pallas_call x4, Pallas kernels, predict(): pl.pallas_call(functools.partial(predict_body, shard, given is not None,...  52.1 us
    ppermute x46, starting transfers between devices, swap(): return lax.ppermute(v, axis, [(i, i ^ 1 << bit) for i in range(size)])  47.2 us
    pallas_call x4, Pallas kernels, expr_part(): pl.pallas_call(functools.partial(expr_body, number, height, half), grid_s...  46.6 us
    pallas_call x1, Pallas kernels, logit_part(): pl.pallas_call(functools.partial(logit_body, pieces, heights, unit, offse...  35.9 us
    pallas_call x2, Pallas kernels, exp_split(): pl.pallas_call(functools.partial(exp_body, with_sums), grid=(rows // step...  12.3 us
    pallas_call x32, Pallas kernels, simple(): pl.pallas_call(body, grid_spec=pltpu.PrefetchScalarGridSpec(num_scalar_pr...  11.8 us
    unnamed x77, local copies, waits for them, and re-layouts  7.9 us
  transfers between devices with their start and end apart: 46, of which 28 were waited for; matrix products, arithmetic and copies ran while one was open for 2% of the time, Pallas kernels for 49%

profile of v4, /device:TPU:0, one launch (start us, length us, event | category | flops | bytes accessed | tf_op | source)
XLA Modules:
  0.0 353.1 jit_solution(5167252182621441062)
XLA Ops:
  1.7 9.2 %shard_map.85 = (f32[264,1024]{1,0:T(8,128)}, bf16[256,2048]{1,0:T(8,128)(2,1)}, bf16[256,2048]{1,0:T(8,128)(2,1)}, f32[8,256]{1,0:T(8,128)}) custom-call(s32[8]{0:T(128)} %fusion.7.order, f32[2048,1024]{1,0:T(8,128)} %refs_0_.3, f32[2048,2048]{1,0:T(8,128)} %refs_3_.1), custom_call_target="tpu_custom_call" | custom-call | tf_op jit(solution)/shard_map/pallas_call | solution.py:263
  13.4 16.3 %shard_map.86 = (f32[264,1024]{1,0:T(8,128)}, f32[264,1024]{1,0:T(8,128)}, f32[264,1024]{1,0:T(8,128)}) custom-call(s32[8]{0:T(128)} %fusion.7.order, bf16[256,2048]{1,0:T(8,128)(2,1)} %get-tuple-element.127.refs_0_, bf16[256,2048]{1,0:T(8,128)(2,1)} %get-tuple-element.128.refs_1_, f32[8,256]{1,0:T(8,128)} %get-tuple-element.129.refs_2_, ...), custom_call_target="tpu_custom_call" | custom-call | tf_op jit(solution)/shard_map/pallas_call | solution.py:263
  29.8 6.2 %shard_map.87 = (bf16[2048,1024]{1,0:T(8,128)(2,1)}, bf16[2048,1024]{1,0:T(8,128)(2,1)}) custom-call(f32[2048,1024]{1,0:T(8,128)} %refs_0_.3), custom_call_target="tpu_custom_call" | custom-call | tf_op jit(solution)/shard_map/pallas_call | solution.py:145
  39.3 13.3 %shard_map.89 = (f32[264,1024]{1,0:T(8,128)}, f32[264,1024]{1,0:T(8,128)}) custom-call(s32[8]{0:T(128)} %fusion.7.order, f32[2048,1024]{1,0:T(8,128)} %refs_0_.3, f32[2048,2048]{1,0:T(8,128)} %refs_3_.1, f32[2048,2048]{1,0:T(8,128)} %refs_3_.1), custom_call_target="tpu_custom_call" | custom-call | tf_op jit(solution)/shard_map/pallas_call | solution.py:263
  56.1 11.6 %collective-permute-done.1.came = f32[264,512]{1,0:T(8,128)S(1)} collective-permute-done((f32[264,512]{1,0:T(8,128)S(1)}, f32[264,512]{1,0:T(8,128)S(1)}, u32[]{:S(2)}, u32[]{:S(2)}) %collective-permute-start.1) | collective-permute-done | bytes 540704 | tf_op jit(solution)/shard_map/ppermute | solution.py:567
  74.9 13.3 %shard_map.92 = (f32[136,1024]{1,0:T(8,128)}, f32[136,1024]{1,0:T(8,128)}, f32[136,1024]{1,0:T(8,128)}, f32[136,1024]{1,0:T(8,128)}) custom-call(s32[8]{0:T(128)} %fusion.7.order, f32[2048,1024]{1,0:T(8,128)} %refs_0_.3, f32[2048,2048]{1,0:T(8,128)} %refs_3_.1, f32[2048,2048]{1,0:T(8,128)} %refs_3_.1), custom_call_target="tpu_custom_call" | custom-call | tf_op jit(solution)/shard_map/pallas_call | solution.py:263
  94.9 6.1 %shard_map.96 = (bf16[2048,1024]{1,0:T(8,128)(2,1)}, bf16[2048,1024]{1,0:T(8,128)(2,1)}) custom-call(f32[2048,1024]{1,0:T(8,128)} %collective-permute-done.9.logits), custom_call_target="tpu_custom_call" | custom-call | tf_op jit(solution)/shard_map/pallas_call | solution.py:145
  101.0 9.0 %collective-permute-done.8.came = f32[264,512]{1,0:T(8,128)S(1)} collective-permute-done((f32[264,512]{1,0:T(8,128)}, f32[264,512]{1,0:T(8,128)S(1)}, u32[]{:S(2)}, u32[]{:S(2)}) %collective-permute-start.8) | collective-permute-done | bytes 540704 | tf_op jit(solution)/shard_map/ppermute | solution.py:567
  113.4 13.6 %collective-permute-done.11.came = f32[136,512]{1,0:T(8,128)S(1)} collective-permute-done((f32[136,512]{1,0:T(8,128)S(1)}, f32[136,512]{1,0:T(8,128)S(1)}, u32[]{:S(2)}, u32[]{:S(2)}) %collective-permute-start.11) | collective-permute-done | bytes 278560 | tf_op jit(solution)/shard_map/ppermute | solution.py:567
  132.3 4.7 %collective-permute-done.13.came = f32[136,256]{1,0:T(8,128)S(1)} collective-permute-done((f32[136,256]{1,0:T(8,128)S(1)}, f32[136,256]{1,0:T(8,128)S(1)}, u32[]{:S(2)}, u32[]{:S(2)}) %collective-permute-start.13) | collective-permute-done | bytes 139296 | tf_op jit(solution)/shard_map/ppermute | solution.py:567
  148.2 3.7 %collective-permute-done.20.b = f32[8,1024]{1,0:T(8,128)S(1)} collective-permute-done((f32[8,1024]{1,0:T(8,128)S(1)}, f32[8,1024]{1,0:T(8,128)S(1)}, u32[]{:S(2)}, u32[]{:S(2)}) %collective-permute-start.20) | collective-permute-done | bytes 32800 | tf_op jit(solution)/shard_map/ppermute | solution.py:567
  156.5 6.6 %shard_map.112 = f32[8,2048]{1,0:T(8,128)} custom-call(f32[8,1024]{1,0:T(8,128)} %copy-done.19, bf16[2048,1024]{1,0:T(8,128)(2,1)} %get-tuple-element.134.mh.refs_4_, bf16[2048,1024]{1,0:T(8,128)(2,1)} %get-tuple-element.210.ml.refs_5_), custom_call_target="tpu_custom_call" | custom-call | tf_op jit(solution)/shard_map/pallas_call | solution.py:166
  171.4 12.2 %collective-permute-done.25.refs_1_ = f32[64,1024]{1,0:T(8,128)S(1)} collective-permute-done((f32[64,1024]{1,0:T(8,128)S(1)}, f32[64,1024]{1,0:T(8,128)S(1)}, u32[]{:S(2)}, u32[]{:S(2)}) %collective-permute-start.25) | collective-permute-done | bytes 262176 | tf_op jit(solution)/shard_map/ppermute | solution.py:567
  195.4 5.7 %shard_map.118 = f32[8,1024]{1,0:T(8,128)} custom-call(f32[8,2048]{1,0:T(8,128)} %broadcast_in_dim.8.dens.refs_0_, f32[8,1024]{1,0:T(8,128)} %copy-done.19, bf16[2048,1024]{1,0:T(8,128)(2,1)} %get-tuple-element.134.mh.refs_4_, bf16[2048,1024]{1,0:T(8,128)(2,1)} %get-tuple-element.210.ml.refs_5_), custom_call_target="tpu_custom_call" | custom-call | tf_op jit(solution)/shard_map/pallas_call | solution.py:383
  214.7 11.5 %shard_map.122 = (f32[2048,128]{1,0:T(8,128)S(1)}, f32[2048,128]{1,0:T(8,128)S(1)}) custom-call(s32[8]{0:T(128)S(1)} %pad_add_fusion.ids, f32[256,1024]{1,0:T(8,128)S(1)} %shard_map.116.refs_0_.near.refs_6_, f32[256,1024]{1,0:T(8,128)S(1)} %collective-permute-done.31.refs_1_.far.refs_7_, f32[256,1024]{1,0:T(8,128)} %collective-permute-done.32.across, ...), custom_call_target="tpu_custom_call" | custom-call | tf_op jit(solution)/shard_map/pallas_call | solution.py:422
  226.2 5.5 %collective-permute-done.30.refs_1_ = f32[128,1024]{1,0:T(8,128)} collective-permute-done((f32[128,1024]{1,0:T(8,128)}, f32[128,1024]{1,0:T(8,128)}, u32[]{:S(2)}, u32[]{:S(2)}) %collective-permute-start.30) | collective-permute-done | bytes 524320 | tf_op jit(solution)/shard_map/ppermute | solution.py:567
  233.1 2.9 collective-permute-done.34.refs_1_.far.refs_9_
  243.1 11.7 %shard_map.126 = (f32[2048,128]{1,0:T(8,128)S(1)}, f32[2048,128]{1,0:T(8,128)S(1)}) custom-call(s32[8]{0:T(128)S(1)} %pad_add_fusion.ids, f32[256,1024]{1,0:T(8,128)S(1)} %shard_map.119.refs_0_.near.refs_8_, f32[256,1024]{1,0:T(8,128)} %collective-permute-done.34.refs_1_.far.refs_9_, f32[256,1024]{1,0:T(8,128)S(1)} %collective-permute-done.35.across, ...), custom_call_target="tpu_custom_call" | custom-call | tf_op jit(solution)/shard_map/pallas_call | solution.py:422
  254.9 8.0 %collective-permute-done.37.refs_1_.far.refs_11_ = f32[256,1024]{1,0:T(8,128)S(1)} collective-permute-done((f32[256,1024]{1,0:T(8,128)S(1)}, f32[256,1024]{1,0:T(8,128)S(1)}, u32[]{:S(2)}, u32[]{:S(2)}) %collective-permute-start.37) | collective-permute-done | bytes 1048608 | tf_op jit(solution)/shard_map/ppermute | solution.py:567
  267.7 11.7 %shard_map.130 = (f32[2048,128]{1,0:T(8,128)S(1)}, f32[2048,128]{1,0:T(8,128)}) custom-call(s32[8]{0:T(128)S(1)} %pad_add_fusion.ids, f32[256,1024]{1,0:T(8,128)S(1)} %shard_map.123.refs_0_.near.refs_10_, f32[256,1024]{1,0:T(8,128)S(1)} %collective-permute-done.37.refs_1_.far.refs_11_, f32[256,1024]{1,0:T(8,128)S(1)} %collective-permute-done.39.across, ...), custom_call_target="tpu_custom_call" | custom-call | tf_op jit(solution)/shard_map/pallas_call | solution.py:422
  280.4 9.4 %collective-permute-done.41.refs_1_.far.refs_13_ = f32[256,1024]{1,0:T(8,128)S(1)} collective-permute-done((f32[256,1024]{1,0:T(8,128)S(1)}, f32[256,1024]{1,0:T(8,128)S(1)}, u32[]{:S(2)}, u32[]{:S(2)}) %collective-permute-start.41) | collective-permute-done | bytes 1048608 | tf_op jit(solution)/shard_map/ppermute | solution.py:567
  294.3 11.7 %shard_map.134 = (f32[2048,128]{1,0:T(8,128)S(1)}, f32[2048,128]{1,0:T(8,128)}) custom-call(s32[8]{0:T(128)S(1)} %pad_add_fusion.ids, f32[256,1024]{1,0:T(8,128)S(1)} %shard_map.127.refs_0_.near.refs_12_, f32[256,1024]{1,0:T(8,128)S(1)} %collective-permute-done.41.refs_1_.far.refs_13_, f32[256,1024]{1,0:T(8,128)S(1)} %collective-permute-done.43.across, ...), custom_call_target="tpu_custom_call" | custom-call | tf_op jit(solution)/shard_map/pallas_call | solution.py:422
  311.4 35.9 %shard_map.135 = f32[2048,1024]{1,0:T(8,128)} custom-call(s32[8]{0:T(128)} %fusion.7.order, f32[8,2048]{1,0:T(8,128)} %broadcast_in_dim.8.dens.refs_0_, f32[8,1024]{1,0:T(8,128)} %copy-done.19, f32[8,1024]{1,0:T(8,128)} %slice.30.refs_2_, f32[2048,2048]{1,0:T(8,128)} %refs_3_.1, bf16[2048,1024]{1,0:T(8,128)(2,1)} %get-tuple-element.134.mh.refs_4_, ...), custom_call_target="tpu_custom_call" | custom-call | tf_op jit(solution)/shard_map/pallas_call | solution.py:493
  347.4 4.6 %shard_map.136 = f32[2048,512]{1,0:T(8,128)} custom-call(f32[2048,128]{1,0:T(8,128)S(1)} %copy-done.14, f32[2048,128]{1,0:T(8,128)S(1)} %collective-permute-done.38.refs_1_, f32[2048,128]{1,0:T(8,128)S(1)} %get-tuple-element.235.refs_2_, f32[2048,128]{1,0:T(8,128)S(1)} %collective-permute-done.42.refs_3_, f32[2048,128]{1,0:T(8,128)S(1)} %copy-done.16, ...), custom_call_target="tpu_custom_call" | custom-call | tf_op jit(solution)/shard_map/pallas_call | solution.py:524
  (221 shorter events, 103.6 us)
Async XLA Ops:
  0.6 94.3 %collective-permute-start.9 = (f32[2048,1024]{1,0:T(8,128)}, f32[2048,1024]{1,0:T(8,128)}, u32[]{:S(2)}, u32[]{:S(2)}) collective-permute-start(f32[2048,1024]{1,0:T(8,128)} %refs_0_.3), channel_id=1, source_target_pairs={{0,1},{1,0},{2,3},{3,2},{4,5},{5,4},{6,7},{7,6},{8,9},{9,8},{10,11... | collective-permute-start | bytes 25165832 | tf_op jit(solution)/shard_map/ppermute | solution.py:567
  10.9 27.4 %collective-permute-start = (f32[264,1024]{1,0:T(8,128)}, f32[264,1024]{1,0:T(8,128)S(1)}, u32[]{:S(2)}, u32[]{:S(2)}) collective-permute-start(f32[264,1024]{1,0:T(8,128)} %get-tuple-element.130), channel_id=1, source_target_pairs={{0,4},{4,0},{8,12},{12,8},{16,20},{20,16},{24,28},{28,24},{1,5},{5... | collective-permute-start | bytes 3244040 | tf_op jit(solution)/shard_map/ppermute | solution.py:567
  29.8 41.4 %collective-permute-start.3 = (f32[264,1024]{1,0:T(8,128)}, f32[264,1024]{1,0:T(8,128)}, u32[]{:S(2)}, u32[]{:S(2)}) collective-permute-start(f32[264,1024]{1,0:T(8,128)} %get-tuple-element.144), channel_id=1, source_target_pairs={{0,4},{4,0},{8,12},{12,8},{16,20},{20,16},{24,28},{28,24},{1,5},{5... | collective-permute-start | bytes 3244040 | tf_op jit(solution)/shard_map/ppermute | solution.py:567
  52.6 39.4 %collective-permute-start.5 = (f32[264,1024]{1,0:T(8,128)}, f32[264,1024]{1,0:T(8,128)S(1)}, u32[]{:S(2)}, u32[]{:S(2)}) collective-permute-start(f32[264,1024]{1,0:T(8,128)} %get-tuple-element.152), channel_id=1, source_target_pairs={{0,4},{4,0},{8,12},{12,8},{16,20},{20,16},{24,28},{28,24},{1,5},{5... | collective-permute-start | bytes 3244040 | tf_op jit(solution)/shard_map/ppermute | solution.py:567
  68.5 20.2 %collective-permute-start.2 = (f32[264,256]{1,0:T(8,128)}, f32[264,256]{1,0:T(8,128)}, u32[]{:S(2)}, u32[]{:S(2)}) collective-permute-start(f32[264,256]{1,0:T(8,128)} %get-tuple-element.142), channel_id=1, source_target_pairs={{0,16},{4,20},{8,24},{12,28},{16,0},{20,4},{24,8},{28,12},{1,17},{... | collective-permute-start | bytes 811016 | tf_op jit(solution)/shard_map/ppermute | solution.py:567
  73.3 20.1 %collective-permute-start.4 = (f32[264,512]{1,0:T(8,128)}, f32[264,512]{1,0:T(8,128)}, u32[]{:S(2)}, u32[]{:S(2)}) collective-permute-start(f32[264,512]{1,0:T(8,128)} %get-tuple-element.146), channel_id=1, source_target_pairs={{0,8},{4,12},{8,0},{12,4},{16,24},{20,28},{24,16},{28,20},{1,9},{5... | collective-permute-start | bytes 1622024 | tf_op jit(solution)/shard_map/ppermute | solution.py:567
  88.2 22.0 %collective-permute-start.7 = (f32[136,1024]{1,0:T(8,128)}, f32[136,1024]{1,0:T(8,128)S(1)}, u32[]{:S(2)}, u32[]{:S(2)}) collective-permute-start(f32[136,1024]{1,0:T(8,128)} %get-tuple-element.158), channel_id=1, source_target_pairs={{0,4},{4,0},{8,12},{12,8},{16,20},{20,16},{24,28},{28,24},{1,5},{5... | collective-permute-start | bytes 1671176 | tf_op jit(solution)/shard_map/ppermute | solution.py:567
  88.7 23.7 %collective-permute-start.12 = (f32[136,1024]{1,0:T(8,128)}, f32[136,1024]{1,0:T(8,128)S(1)}, u32[]{:S(2)}, u32[]{:S(2)}) collective-permute-start(f32[136,1024]{1,0:T(8,128)} %get-tuple-element.171), channel_id=1, source_target_pairs={{0,4},{4,0},{8,12},{12,8},{16,20},{20,16},{24,28},{28,24},{1,5},{5... | collective-permute-start | bytes 1671176 | tf_op jit(solution)/shard_map/ppermute | solution.py:567
  92.9 17.2 %collective-permute-start.8 = (f32[264,512]{1,0:T(8,128)}, f32[264,512]{1,0:T(8,128)S(1)}, u32[]{:S(2)}, u32[]{:S(2)}) collective-permute-start(f32[264,512]{1,0:T(8,128)} %get-tuple-element.154), channel_id=1, source_target_pairs={{0,8},{4,12},{8,0},{12,4},{16,24},{20,28},{24,16},{28,20},{1,9},{5... | collective-permute-start | bytes 1622024 | tf_op jit(solution)/shard_map/ppermute | solution.py:567
  110.3 16.8 %collective-permute-start.11 = (f32[136,512]{1,0:T(8,128)S(1)}, f32[136,512]{1,0:T(8,128)S(1)}, u32[]{:S(2)}, u32[]{:S(2)}) collective-permute-start(f32[136,512]{1,0:T(8,128)S(1)} %get-tuple-element.165), channel_id=1, source_target_pairs={{0,8},{4,12},{8,0},{12,4},{16,24},{20,28},{24,16},{28,20},{1,9},{5... | collective-permute-start | bytes 835592 | tf_op jit(solution)/shard_map/ppermute | solution.py:567
  112.5 17.6 %collective-permute-start.14 = (f32[136,512]{1,0:T(8,128)S(1)}, f32[136,512]{1,0:T(8,128)S(1)}, u32[]{:S(2)}, u32[]{:S(2)}) collective-permute-start(f32[136,512]{1,0:T(8,128)S(1)} %get-tuple-element.173), channel_id=1, source_target_pairs={{0,8},{4,12},{8,0},{12,4},{16,24},{20,28},{24,16},{28,20},{1,9},{5... | collective-permute-start | bytes 835592 | tf_op jit(solution)/shard_map/ppermute | solution.py:567
  167.1 18.6 %collective-permute-start.24 = (f32[128,1024]{1,0:T(8,128)S(1)}, f32[128,1024]{1,0:T(8,128)S(1)}, u32[]{:S(2)}, u32[]{:S(2)}) collective-permute-start(f32[128,1024]{1,0:T(8,128)S(1)} %shard_map.113.refs_0_), channel_id=1, source_target_pairs={{0,8},{4,12},{8,0},{12,4},{16,24},{20,28},{24,16},{28,20},{1,9},{5... | collective-permute-start | bytes 1572872 | tf_op jit(solution)/shard_map/ppermute | solution.py:567
  185.8 23.3 %collective-permute-start.31 = (f32[256,1024]{1,0:T(8,128)S(1)}, f32[256,1024]{1,0:T(8,128)S(1)}, u32[]{:S(2)}, u32[]{:S(2)}) collective-permute-start(f32[256,1024]{1,0:T(8,128)S(1)} %shard_map.116.refs_0_.near.refs_6_), channel_id=1, source_target_pairs={{0,4},{4,0},{8,12},{12,8},{16,20},{20,16},{24,28},{28,24},{1,5},{5... | collective-permute-start | bytes 3145736 | tf_op jit(solution)/shard_map/ppermute | solution.py:567
  186.5 17.4 %collective-permute-start.28 = (f32[128,1024]{1,0:T(8,128)S(1)}, f32[128,1024]{1,0:T(8,128)S(1)}, u32[]{:S(2)}, u32[]{:S(2)}) collective-permute-start(f32[128,1024]{1,0:T(8,128)S(1)} %shard_map.115.refs_0_), channel_id=1, source_target_pairs={{0,8},{4,12},{8,0},{12,4},{16,24},{20,28},{24,16},{28,20},{1,9},{5... | collective-permute-start | bytes 1572872 | tf_op jit(solution)/shard_map/ppermute | solution.py:567
  189.1 17.7 %collective-permute-start.27 = (f32[64,1024]{1,0:T(8,128)}, f32[64,1024]{1,0:T(8,128)}, u32[]{:S(2)}, u32[]{:S(2)}) collective-permute-start(f32[64,1024]{1,0:T(8,128)} %get-tuple-element.223.refs_0_), channel_id=1, source_target_pairs={{0,16},{4,20},{8,24},{12,28},{16,0},{20,4},{24,8},{28,12},{1,17},{... | collective-permute-start | bytes 786440 | tf_op jit(solution)/shard_map/ppermute | solution.py:567
  210.3 25.7 %collective-permute-start.34 = (f32[256,1024]{1,0:T(8,128)S(1)}, f32[256,1024]{1,0:T(8,128)}, u32[]{:S(2)}, u32[]{:S(2)}) collective-permute-start(f32[256,1024]{1,0:T(8,128)S(1)} %shard_map.119.refs_0_.near.refs_8_), channel_id=1, source_target_pairs={{0,4},{4,0},{8,12},{12,8},{16,20},{20,16},{24,28},{28,24},{1,5},{5... | collective-permute-start | bytes 3145736 | tf_op jit(solution)/shard_map/ppermute | solution.py:567
  211.7 20.0 %collective-permute-start.30 = (f32[128,1024]{1,0:T(8,128)}, f32[128,1024]{1,0:T(8,128)}, u32[]{:S(2)}, u32[]{:S(2)}) collective-permute-start(f32[128,1024]{1,0:T(8,128)} %shard_map.120.refs_0_), channel_id=1, source_target_pairs={{0,8},{4,12},{8,0},{12,4},{16,24},{20,28},{24,16},{28,20},{1,9},{5... | collective-permute-start | bytes 1572872 | tf_op jit(solution)/shard_map/ppermute | solution.py:567
  212.4 20.6 %collective-permute-start.29 = (f32[64,1024]{1,0:T(8,128)S(1)}, f32[64,1024]{1,0:T(8,128)S(1)}, u32[]{:S(2)}, u32[]{:S(2)}) collective-permute-start(f32[64,1024]{1,0:T(8,128)S(1)} %get-tuple-element.226.refs_0_), channel_id=1, source_target_pairs={{0,16},{4,20},{8,24},{12,28},{16,0},{20,4},{24,8},{28,12},{1,17},{... | collective-permute-start | bytes 786440 | tf_op jit(solution)/shard_map/ppermute | solution.py:567
  237.4 25.6 %collective-permute-start.37 = (f32[256,1024]{1,0:T(8,128)S(1)}, f32[256,1024]{1,0:T(8,128)S(1)}, u32[]{:S(2)}, u32[]{:S(2)}) collective-permute-start(f32[256,1024]{1,0:T(8,128)S(1)} %shard_map.123.refs_0_.near.refs_10_), channel_id=1, source_target_pairs={{0,4},{4,0},{8,12},{12,8},{16,20},{20,16},{24,28},{28,24},{1,5},{5... | collective-permute-start | bytes 3145736 | tf_op jit(solution)/shard_map/ppermute | solution.py:567
  238.9 25.2 %collective-permute-start.38 = (f32[2048,128]{1,0:T(8,128)S(1)}, f32[2048,128]{1,0:T(8,128)S(1)}, u32[]{:S(2)}, u32[]{:S(2)}) collective-permute-start(f32[2048,128]{1,0:T(8,128)S(1)} %get-tuple-element.238), channel_id=1, source_target_pairs={{0,2},{1,3},{2,0},{3,1},{4,6},{5,7},{6,4},{7,5},{8,10},{9,11},{10,... | collective-permute-start | bytes 3145736 | tf_op jit(solution)/shard_map/ppermute | solution.py:567
  264.2 25.6 %collective-permute-start.41 = (f32[256,1024]{1,0:T(8,128)S(1)}, f32[256,1024]{1,0:T(8,128)S(1)}, u32[]{:S(2)}, u32[]{:S(2)}) collective-permute-start(f32[256,1024]{1,0:T(8,128)S(1)} %shard_map.127.refs_0_.near.refs_12_), channel_id=1, source_target_pairs={{0,4},{4,0},{8,12},{12,8},{16,20},{20,16},{24,28},{28,24},{1,5},{5... | collective-permute-start | bytes 3145736 | tf_op jit(solution)/shard_map/ppermute | solution.py:567
  264.9 25.2 %collective-permute-start.42 = (f32[2048,128]{1,0:T(8,128)S(1)}, f32[2048,128]{1,0:T(8,128)S(1)}, u32[]{:S(2)}, u32[]{:S(2)}) collective-permute-start(f32[2048,128]{1,0:T(8,128)S(1)} %get-tuple-element.243), channel_id=1, source_target_pairs={{0,2},{1,3},{2,0},{3,1},{4,6},{5,7},{6,4},{7,5},{8,10},{9,11},{10,... | collective-permute-start | bytes 3145736 | tf_op jit(solution)/shard_map/ppermute | solution.py:567
  291.8 55.5 %collective-permute-start.44 = (f32[2048,128]{1,0:T(8,128)}, f32[2048,128]{1,0:T(8,128)S(1)}, u32[]{:S(2)}, u32[]{:S(2)}) collective-permute-start(f32[2048,128]{1,0:T(8,128)} %get-tuple-element.249), channel_id=1, source_target_pairs={{0,2},{1,3},{2,0},{3,1},{4,6},{5,7},{6,4},{7,5},{8,10},{9,11},{10,... | collective-permute-start | bytes 3145736 | tf_op jit(solution)/shard_map/ppermute | solution.py:567
  307.0 40.3 %collective-permute-start.45 = (f32[2048,128]{1,0:T(8,128)}, f32[2048,128]{1,0:T(8,128)}, u32[]{:S(2)}, u32[]{:S(2)}) collective-permute-start(f32[2048,128]{1,0:T(8,128)} %get-tuple-element.250), channel_id=1, source_target_pairs={{0,2},{1,3},{2,0},{3,1},{4,6},{5,7},{6,4},{7,5},{8,10},{9,11},{10,... | collective-permute-start | bytes 3145736 | tf_op jit(solution)/shard_map/ppermute | solution.py:567
  (57 other events, 771.6 us)

commit v5 on v4

--- a/solution.py
+++ b/solution.py
@@ -161,7 +161,7 @@
 
 def mass_rows(sums, mparts):
     rows, cols = mparts[0].shape
-    step = 512
+    step = 1024
     tile = pl.BlockSpec((step, cols), lambda i: (i, 0))
     return pl.pallas_call(
         mass_body,
@@ -377,7 +377,7 @@
 
 def pull_cols(dens, sums, mparts):
     rows, cols = mparts[0].shape
-    step = 512
+    step = 1024
     tile = pl.BlockSpec((step, cols), lambda i: (i, 0))
     strip = pl.BlockSpec((8, cols), lambda i: (0, 0))
     return pl.pallas_call(
@@ -519,7 +519,7 @@
 def join(pairs, heights, shards, scale):
     flat = [v for pair in pairs for v in pair]
     rows = flat[0].shape[0]
-    step = 512
+    step = 1024
     genes = shards * sum(heights)
     return pl.pallas_call(
         functools.partial(join_body, shards, heights, scale),

time: 354 us -> 353 us (level)
  no operation moved by 1% of the time
where the time goes in v5:
time: 353 us; the launch traced here: 352 us
  Pallas kernels  181 us (51%)
  waiting for transfers between devices  104 us (29%)
  starting transfers between devices  47.2 us (13%)
  local copies, waits for them, and re-layouts  12.4 us (4%)
  between operations  4.99 us (1%)
    ppermute x46, waiting for transfers between devices, swap(): return lax.ppermute(v, axis, [(i, i ^ 1 << bit) for i in range(size)])  104 us
    pallas_call x4, Pallas kernels, predict(): pl.pallas_call(functools.partial(predict_body, shard, given is not None,...  52.1 us
    ppermute x46, starting transfers between devices, swap(): return lax.ppermute(v, axis, [(i, i ^ 1 << bit) for i in range(size)])  47.2 us
    pallas_call x4, Pallas kernels, expr_part(): pl.pallas_call(functools.partial(expr_body, number, height, half), grid_s...  46.6 us
    pallas_call x1, Pallas kernels, logit_part(): pl.pallas_call(functools.partial(logit_body, pieces, heights, unit, offse...  35.9 us
    pallas_call x2, Pallas kernels, exp_split(): pl.pallas_call(functools.partial(exp_body, with_sums), grid=(rows // step...  12.3 us
    pallas_call x32, Pallas kernels, simple(): pl.pallas_call(body, grid_spec=pltpu.PrefetchScalarGridSpec(num_scalar_pr...  11.8 us
    unnamed x77, local copies, waits for them, and re-layouts  7.9 us
  transfers between devices with their start and end apart: 46, of which 28 were waited for; matrix products, arithmetic and copies ran while one was open for 2% of the time, Pallas kernels for 49%

profile of v5, /device:TPU:0, one launch (start us, length us, event | category | flops | bytes accessed | tf_op | source)
XLA Modules:
  0.0 352.3 jit_solution(4256431684849886007)
XLA Ops:
  1.7 9.2 %shard_map.85 = (f32[264,1024]{1,0:T(8,128)}, bf16[256,2048]{1,0:T(8,128)(2,1)}, bf16[256,2048]{1,0:T(8,128)(2,1)}, f32[8,256]{1,0:T(8,128)}) custom-call(s32[8]{0:T(128)} %fusion.7.order, f32[2048,1024]{1,0:T(8,128)} %refs_0_.3, f32[2048,2048]{1,0:T(8,128)} %refs_3_.1), custom_call_target="tpu_custom_call" | custom-call | tf_op jit(solution)/shard_map/pallas_call | solution.py:263
  13.4 16.3 %shard_map.86 = (f32[264,1024]{1,0:T(8,128)}, f32[264,1024]{1,0:T(8,128)}, f32[264,1024]{1,0:T(8,128)}) custom-call(s32[8]{0:T(128)} %fusion.7.order, bf16[256,2048]{1,0:T(8,128)(2,1)} %get-tuple-element.127.refs_0_, bf16[256,2048]{1,0:T(8,128)(2,1)} %get-tuple-element.128.refs_1_, f32[8,256]{1,0:T(8,128)} %get-tuple-element.129.refs_2_, ...), custom_call_target="tpu_custom_call" | custom-call | tf_op jit(solution)/shard_map/pallas_call | solution.py:263
  29.8 6.2 %shard_map.87 = (bf16[2048,1024]{1,0:T(8,128)(2,1)}, bf16[2048,1024]{1,0:T(8,128)(2,1)}) custom-call(f32[2048,1024]{1,0:T(8,128)} %refs_0_.3), custom_call_target="tpu_custom_call" | custom-call | tf_op jit(solution)/shard_map/pallas_call | solution.py:145
  39.3 13.3 %shard_map.89 = (f32[264,1024]{1,0:T(8,128)}, f32[264,1024]{1,0:T(8,128)}) custom-call(s32[8]{0:T(128)} %fusion.7.order, f32[2048,1024]{1,0:T(8,128)} %refs_0_.3, f32[2048,2048]{1,0:T(8,128)} %refs_3_.1, f32[2048,2048]{1,0:T(8,128)} %refs_3_.1), custom_call_target="tpu_custom_call" | custom-call | tf_op jit(solution)/shard_map/pallas_call | solution.py:263
  56.1 11.6 %collective-permute-done.1.came = f32[264,512]{1,0:T(8,128)S(1)} collective-permute-done((f32[264,512]{1,0:T(8,128)S(1)}, f32[264,512]{1,0:T(8,128)S(1)}, u32[]{:S(2)}, u32[]{:S(2)}) %collective-permute-start.1) | collective-permute-done | bytes 540704 | tf_op jit(solution)/shard_map/ppermute | solution.py:567
  74.9 13.3 %shard_map.92 = (f32[136,1024]{1,0:T(8,128)}, f32[136,1024]{1,0:T(8,128)}, f32[136,1024]{1,0:T(8,128)}, f32[136,1024]{1,0:T(8,128)}) custom-call(s32[8]{0:T(128)} %fusion.7.order, f32[2048,1024]{1,0:T(8,128)} %refs_0_.3, f32[2048,2048]{1,0:T(8,128)} %refs_3_.1, f32[2048,2048]{1,0:T(8,128)} %refs_3_.1), custom_call_target="tpu_custom_call" | custom-call | tf_op jit(solution)/shard_map/pallas_call | solution.py:263
  94.9 6.1 %shard_map.96 = (bf16[2048,1024]{1,0:T(8,128)(2,1)}, bf16[2048,1024]{1,0:T(8,128)(2,1)}) custom-call(f32[2048,1024]{1,0:T(8,128)} %collective-permute-done.9.logits), custom_call_target="tpu_custom_call" | custom-call | tf_op jit(solution)/shard_map/pallas_call | solution.py:145
  101.0 9.0 %collective-permute-done.8.came = f32[264,512]{1,0:T(8,128)S(1)} collective-permute-done((f32[264,512]{1,0:T(8,128)}, f32[264,512]{1,0:T(8,128)S(1)}, u32[]{:S(2)}, u32[]{:S(2)}) %collective-permute-start.8) | collective-permute-done | bytes 540704 | tf_op jit(solution)/shard_map/ppermute | solution.py:567
  113.4 13.6 %collective-permute-done.11.came = f32[136,512]{1,0:T(8,128)S(1)} collective-permute-done((f32[136,512]{1,0:T(8,128)S(1)}, f32[136,512]{1,0:T(8,128)S(1)}, u32[]{:S(2)}, u32[]{:S(2)}) %collective-permute-start.11) | collective-permute-done | bytes 278560 | tf_op jit(solution)/shard_map/ppermute | solution.py:567
  132.3 4.7 %collective-permute-done.13.came = f32[136,256]{1,0:T(8,128)S(1)} collective-permute-done((f32[136,256]{1,0:T(8,128)S(1)}, f32[136,256]{1,0:T(8,128)S(1)}, u32[]{:S(2)}, u32[]{:S(2)}) %collective-permute-start.13) | collective-permute-done | bytes 139296 | tf_op jit(solution)/shard_map/ppermute | solution.py:567
  148.2 3.7 %collective-permute-done.20.b = f32[8,1024]{1,0:T(8,128)S(1)} collective-permute-done((f32[8,1024]{1,0:T(8,128)S(1)}, f32[8,1024]{1,0:T(8,128)S(1)}, u32[]{:S(2)}, u32[]{:S(2)}) %collective-permute-start.20) | collective-permute-done | bytes 32800 | tf_op jit(solution)/shard_map/ppermute | solution.py:567
  156.5 6.3 %shard_map.112 = f32[8,2048]{1,0:T(8,128)} custom-call(f32[8,1024]{1,0:T(8,128)} %copy-done.19, bf16[2048,1024]{1,0:T(8,128)(2,1)} %get-tuple-element.134.mh.refs_4_, bf16[2048,1024]{1,0:T(8,128)(2,1)} %get-tuple-element.210.ml.refs_5_), custom_call_target="tpu_custom_call" | custom-call | tf_op jit(solution)/shard_map/pallas_call | solution.py:166
  171.4 12.2 %collective-permute-done.25.refs_1_ = f32[64,1024]{1,0:T(8,128)S(1)} collective-permute-done((f32[64,1024]{1,0:T(8,128)S(1)}, f32[64,1024]{1,0:T(8,128)S(1)}, u32[]{:S(2)}, u32[]{:S(2)}) %collective-permute-start.25) | collective-permute-done | bytes 262176 | tf_op jit(solution)/shard_map/ppermute | solution.py:567
  195.4 5.1 %shard_map.118 = f32[8,1024]{1,0:T(8,128)} custom-call(f32[8,2048]{1,0:T(8,128)} %broadcast_in_dim.8.dens.refs_0_, f32[8,1024]{1,0:T(8,128)} %copy-done.19, bf16[2048,1024]{1,0:T(8,128)(2,1)} %get-tuple-element.134.mh.refs_4_, bf16[2048,1024]{1,0:T(8,128)(2,1)} %get-tuple-element.210.ml.refs_5_), custom_call_target="tpu_custom_call" | custom-call | tf_op jit(solution)/shard_map/pallas_call | solution.py:383
  214.7 11.5 %shard_map.122 = (f32[2048,128]{1,0:T(8,128)S(1)}, f32[2048,128]{1,0:T(8,128)S(1)}) custom-call(s32[8]{0:T(128)S(1)} %pad_add_fusion.ids, f32[256,1024]{1,0:T(8,128)S(1)} %shard_map.116.refs_0_.near.refs_6_, f32[256,1024]{1,0:T(8,128)S(1)} %collective-permute-done.31.refs_1_.far.refs_7_, f32[256,1024]{1,0:T(8,128)} %collective-permute-done.32.across, ...), custom_call_target="tpu_custom_call" | custom-call | tf_op jit(solution)/shard_map/pallas_call | solution.py:422
  226.2 5.5 %collective-permute-done.30.refs_1_ = f32[128,1024]{1,0:T(8,128)} collective-permute-done((f32[128,1024]{1,0:T(8,128)}, f32[128,1024]{1,0:T(8,128)}, u32[]{:S(2)}, u32[]{:S(2)}) %collective-permute-start.30) | collective-permute-done | bytes 524320 | tf_op jit(solution)/shard_map/ppermute | solution.py:567
  233.1 2.9 collective-permute-done.34.refs_1_.far.refs_9_
  243.1 11.7 %shard_map.126 = (f32[2048,128]{1,0:T(8,128)S(1)}, f32[2048,128]{1,0:T(8,128)S(1)}) custom-call(s32[8]{0:T(128)S(1)} %pad_add_fusion.ids, f32[256,1024]{1,0:T(8,128)S(1)} %shard_map.119.refs_0_.near.refs_8_, f32[256,1024]{1,0:T(8,128)} %collective-permute-done.34.refs_1_.far.refs_9_, f32[256,1024]{1,0:T(8,128)S(1)} %collective-permute-done.35.across, ...), custom_call_target="tpu_custom_call" | custom-call | tf_op jit(solution)/shard_map/pallas_call | solution.py:422
  254.9 8.0 %collective-permute-done.37.refs_1_.far.refs_11_ = f32[256,1024]{1,0:T(8,128)S(1)} collective-permute-done((f32[256,1024]{1,0:T(8,128)S(1)}, f32[256,1024]{1,0:T(8,128)S(1)}, u32[]{:S(2)}, u32[]{:S(2)}) %collective-permute-start.37) | collective-permute-done | bytes 1048608 | tf_op jit(solution)/shard_map/ppermute | solution.py:567
  267.7 11.7 %shard_map.130 = (f32[2048,128]{1,0:T(8,128)S(1)}, f32[2048,128]{1,0:T(8,128)}) custom-call(s32[8]{0:T(128)S(1)} %pad_add_fusion.ids, f32[256,1024]{1,0:T(8,128)S(1)} %shard_map.123.refs_0_.near.refs_10_, f32[256,1024]{1,0:T(8,128)S(1)} %collective-permute-done.37.refs_1_.far.refs_11_, f32[256,1024]{1,0:T(8,128)S(1)} %collective-permute-done.39.across, ...), custom_call_target="tpu_custom_call" | custom-call | tf_op jit(solution)/shard_map/pallas_call | solution.py:422
  280.4 9.4 %collective-permute-done.41.refs_1_.far.refs_13_ = f32[256,1024]{1,0:T(8,128)S(1)} collective-permute-done((f32[256,1024]{1,0:T(8,128)S(1)}, f32[256,1024]{1,0:T(8,128)S(1)}, u32[]{:S(2)}, u32[]{:S(2)}) %collective-permute-start.41) | collective-permute-done | bytes 1048608 | tf_op jit(solution)/shard_map/ppermute | solution.py:567
  294.3 11.7 %shard_map.134 = (f32[2048,128]{1,0:T(8,128)S(1)}, f32[2048,128]{1,0:T(8,128)}) custom-call(s32[8]{0:T(128)S(1)} %pad_add_fusion.ids, f32[256,1024]{1,0:T(8,128)S(1)} %shard_map.127.refs_0_.near.refs_12_, f32[256,1024]{1,0:T(8,128)S(1)} %collective-permute-done.41.refs_1_.far.refs_13_, f32[256,1024]{1,0:T(8,128)S(1)} %collective-permute-done.43.across, ...), custom_call_target="tpu_custom_call" | custom-call | tf_op jit(solution)/shard_map/pallas_call | solution.py:422
  311.4 35.9 %shard_map.135 = f32[2048,1024]{1,0:T(8,128)} custom-call(s32[8]{0:T(128)} %fusion.7.order, f32[8,2048]{1,0:T(8,128)} %broadcast_in_dim.8.dens.refs_0_, f32[8,1024]{1,0:T(8,128)} %copy-done.19, f32[8,1024]{1,0:T(8,128)} %slice.30.refs_2_, f32[2048,2048]{1,0:T(8,128)} %refs_3_.1, bf16[2048,1024]{1,0:T(8,128)(2,1)} %get-tuple-element.134.mh.refs_4_, ...), custom_call_target="tpu_custom_call" | custom-call | tf_op jit(solution)/shard_map/pallas_call | solution.py:493
  347.4 3.8 %shard_map.136 = f32[2048,512]{1,0:T(8,128)} custom-call(f32[2048,128]{1,0:T(8,128)S(1)} %copy-done.14, f32[2048,128]{1,0:T(8,128)S(1)} %collective-permute-done.38.refs_1_, f32[2048,128]{1,0:T(8,128)S(1)} %get-tuple-element.235.refs_2_, f32[2048,128]{1,0:T(8,128)S(1)} %collective-permute-done.42.refs_3_, f32[2048,128]{1,0:T(8,128)S(1)} %copy-done.16, ...), custom_call_target="tpu_custom_call" | custom-call | tf_op jit(solution)/shard_map/pallas_call | solution.py:524
  (221 shorter events, 104.5 us)
Async XLA Ops:
  0.6 94.3 %collective-permute-start.9 = (f32[2048,1024]{1,0:T(8,128)}, f32[2048,1024]{1,0:T(8,128)}, u32[]{:S(2)}, u32[]{:S(2)}) collective-permute-start(f32[2048,1024]{1,0:T(8,128)} %refs_0_.3), channel_id=1, source_target_pairs={{0,1},{1,0},{2,3},{3,2},{4,5},{5,4},{6,7},{7,6},{8,9},{9,8},{10,11... | collective-permute-start | bytes 25165832 | tf_op jit(solution)/shard_map/ppermute | solution.py:567
  10.9 27.4 %collective-permute-start = (f32[264,1024]{1,0:T(8,128)}, f32[264,1024]{1,0:T(8,128)S(1)}, u32[]{:S(2)}, u32[]{:S(2)}) collective-permute-start(f32[264,1024]{1,0:T(8,128)} %get-tuple-element.130), channel_id=1, source_target_pairs={{0,4},{4,0},{8,12},{12,8},{16,20},{20,16},{24,28},{28,24},{1,5},{5... | collective-permute-start | bytes 3244040 | tf_op jit(solution)/shard_map/ppermute | solution.py:567
  29.8 41.4 %collective-permute-start.3 = (f32[264,1024]{1,0:T(8,128)}, f32[264,1024]{1,0:T(8,128)}, u32[]{:S(2)}, u32[]{:S(2)}) collective-permute-start(f32[264,1024]{1,0:T(8,128)} %get-tuple-element.144), channel_id=1, source_target_pairs={{0,4},{4,0},{8,12},{12,8},{16,20},{20,16},{24,28},{28,24},{1,5},{5... | collective-permute-start | bytes 3244040 | tf_op jit(solution)/shard_map/ppermute | solution.py:567
  52.6 39.4 %collective-permute-start.5 = (f32[264,1024]{1,0:T(8,128)}, f32[264,1024]{1,0:T(8,128)S(1)}, u32[]{:S(2)}, u32[]{:S(2)}) collective-permute-start(f32[264,1024]{1,0:T(8,128)} %get-tuple-element.152), channel_id=1, source_target_pairs={{0,4},{4,0},{8,12},{12,8},{16,20},{20,16},{24,28},{28,24},{1,5},{5... | collective-permute-start | bytes 3244040 | tf_op jit(solution)/shard_map/ppermute | solution.py:567
  68.5 20.2 %collective-permute-start.2 = (f32[264,256]{1,0:T(8,128)}, f32[264,256]{1,0:T(8,128)}, u32[]{:S(2)}, u32[]{:S(2)}) collective-permute-start(f32[264,256]{1,0:T(8,128)} %get-tuple-element.142), channel_id=1, source_target_pairs={{0,16},{4,20},{8,24},{12,28},{16,0},{20,4},{24,8},{28,12},{1,17},{... | collective-permute-start | bytes 811016 | tf_op jit(solution)/shard_map/ppermute | solution.py:567
  73.3 20.1 %collective-permute-start.4 = (f32[264,512]{1,0:T(8,128)}, f32[264,512]{1,0:T(8,128)}, u32[]{:S(2)}, u32[]{:S(2)}) collective-permute-start(f32[264,512]{1,0:T(8,128)} %get-tuple-element.146), channel_id=1, source_target_pairs={{0,8},{4,12},{8,0},{12,4},{16,24},{20,28},{24,16},{28,20},{1,9},{5... | collective-permute-start | bytes 1622024 | tf_op jit(solution)/shard_map/ppermute | solution.py:567
  88.2 22.0 %collective-permute-start.7 = (f32[136,1024]{1,0:T(8,128)}, f32[136,1024]{1,0:T(8,128)S(1)}, u32[]{:S(2)}, u32[]{:S(2)}) collective-permute-start(f32[136,1024]{1,0:T(8,128)} %get-tuple-element.158), channel_id=1, source_target_pairs={{0,4},{4,0},{8,12},{12,8},{16,20},{20,16},{24,28},{28,24},{1,5},{5... | collective-permute-start | bytes 1671176 | tf_op jit(solution)/shard_map/ppermute | solution.py:567
  88.7 23.7 %collective-permute-start.12 = (f32[136,1024]{1,0:T(8,128)}, f32[136,1024]{1,0:T(8,128)S(1)}, u32[]{:S(2)}, u32[]{:S(2)}) collective-permute-start(f32[136,1024]{1,0:T(8,128)} %get-tuple-element.171), channel_id=1, source_target_pairs={{0,4},{4,0},{8,12},{12,8},{16,20},{20,16},{24,28},{28,24},{1,5},{5... | collective-permute-start | bytes 1671176 | tf_op jit(solution)/shard_map/ppermute | solution.py:567
  92.9 17.2 %collective-permute-start.8 = (f32[264,512]{1,0:T(8,128)}, f32[264,512]{1,0:T(8,128)S(1)}, u32[]{:S(2)}, u32[]{:S(2)}) collective-permute-start(f32[264,512]{1,0:T(8,128)} %get-tuple-element.154), channel_id=1, source_target_pairs={{0,8},{4,12},{8,0},{12,4},{16,24},{20,28},{24,16},{28,20},{1,9},{5... | collective-permute-start | bytes 1622024 | tf_op jit(solution)/shard_map/ppermute | solution.py:567
  110.3 16.8 %collective-permute-start.11 = (f32[136,512]{1,0:T(8,128)S(1)}, f32[136,512]{1,0:T(8,128)S(1)}, u32[]{:S(2)}, u32[]{:S(2)}) collective-permute-start(f32[136,512]{1,0:T(8,128)S(1)} %get-tuple-element.165), channel_id=1, source_target_pairs={{0,8},{4,12},{8,0},{12,4},{16,24},{20,28},{24,16},{28,20},{1,9},{5... | collective-permute-start | bytes 835592 | tf_op jit(solution)/shard_map/ppermute | solution.py:567
  112.5 17.6 %collective-permute-start.14 = (f32[136,512]{1,0:T(8,128)S(1)}, f32[136,512]{1,0:T(8,128)S(1)}, u32[]{:S(2)}, u32[]{:S(2)}) collective-permute-start(f32[136,512]{1,0:T(8,128)S(1)} %get-tuple-element.173), channel_id=1, source_target_pairs={{0,8},{4,12},{8,0},{12,4},{16,24},{20,28},{24,16},{28,20},{1,9},{5... | collective-permute-start | bytes 835592 | tf_op jit(solution)/shard_map/ppermute | solution.py:567
  167.1 18.6 %collective-permute-start.24 = (f32[128,1024]{1,0:T(8,128)S(1)}, f32[128,1024]{1,0:T(8,128)S(1)}, u32[]{:S(2)}, u32[]{:S(2)}) collective-permute-start(f32[128,1024]{1,0:T(8,128)S(1)} %shard_map.113.refs_0_), channel_id=1, source_target_pairs={{0,8},{4,12},{8,0},{12,4},{16,24},{20,28},{24,16},{28,20},{1,9},{5... | collective-permute-start | bytes 1572872 | tf_op jit(solution)/shard_map/ppermute | solution.py:567
  185.8 23.3 %collective-permute-start.31 = (f32[256,1024]{1,0:T(8,128)S(1)}, f32[256,1024]{1,0:T(8,128)S(1)}, u32[]{:S(2)}, u32[]{:S(2)}) collective-permute-start(f32[256,1024]{1,0:T(8,128)S(1)} %shard_map.116.refs_0_.near.refs_6_), channel_id=1, source_target_pairs={{0,4},{4,0},{8,12},{12,8},{16,20},{20,16},{24,28},{28,24},{1,5},{5... | collective-permute-start | bytes 3145736 | tf_op jit(solution)/shard_map/ppermute | solution.py:567
  186.5 17.4 %collective-permute-start.28 = (f32[128,1024]{1,0:T(8,128)S(1)}, f32[128,1024]{1,0:T(8,128)S(1)}, u32[]{:S(2)}, u32[]{:S(2)}) collective-permute-start(f32[128,1024]{1,0:T(8,128)S(1)} %shard_map.115.refs_0_), channel_id=1, source_target_pairs={{0,8},{4,12},{8,0},{12,4},{16,24},{20,28},{24,16},{28,20},{1,9},{5... | collective-permute-start | bytes 1572872 | tf_op jit(solution)/shard_map/ppermute | solution.py:567
  189.1 17.7 %collective-permute-start.27 = (f32[64,1024]{1,0:T(8,128)}, f32[64,1024]{1,0:T(8,128)}, u32[]{:S(2)}, u32[]{:S(2)}) collective-permute-start(f32[64,1024]{1,0:T(8,128)} %get-tuple-element.223.refs_0_), channel_id=1, source_target_pairs={{0,16},{4,20},{8,24},{12,28},{16,0},{20,4},{24,8},{28,12},{1,17},{... | collective-permute-start | bytes 786440 | tf_op jit(solution)/shard_map/ppermute | solution.py:567
  210.3 25.7 %collective-permute-start.34 = (f32[256,1024]{1,0:T(8,128)S(1)}, f32[256,1024]{1,0:T(8,128)}, u32[]{:S(2)}, u32[]{:S(2)}) collective-permute-start(f32[256,1024]{1,0:T(8,128)S(1)} %shard_map.119.refs_0_.near.refs_8_), channel_id=1, source_target_pairs={{0,4},{4,0},{8,12},{12,8},{16,20},{20,16},{24,28},{28,24},{1,5},{5... | collective-permute-start | bytes 3145736 | tf_op jit(solution)/shard_map/ppermute | solution.py:567
  211.7 20.0 %collective-permute-start.30 = (f32[128,1024]{1,0:T(8,128)}, f32[128,1024]{1,0:T(8,128)}, u32[]{:S(2)}, u32[]{:S(2)}) collective-permute-start(f32[128,1024]{1,0:T(8,128)} %shard_map.120.refs_0_), channel_id=1, source_target_pairs={{0,8},{4,12},{8,0},{12,4},{16,24},{20,28},{24,16},{28,20},{1,9},{5... | collective-permute-start | bytes 1572872 | tf_op jit(solution)/shard_map/ppermute | solution.py:567
  212.4 20.6 %collective-permute-start.29 = (f32[64,1024]{1,0:T(8,128)S(1)}, f32[64,1024]{1,0:T(8,128)S(1)}, u32[]{:S(2)}, u32[]{:S(2)}) collective-permute-start(f32[64,1024]{1,0:T(8,128)S(1)} %get-tuple-element.226.refs_0_), channel_id=1, source_target_pairs={{0,16},{4,20},{8,24},{12,28},{16,0},{20,4},{24,8},{28,12},{1,17},{... | collective-permute-start | bytes 786440 | tf_op jit(solution)/shard_map/ppermute | solution.py:567
  237.4 25.6 %collective-permute-start.37 = (f32[256,1024]{1,0:T(8,128)S(1)}, f32[256,1024]{1,0:T(8,128)S(1)}, u32[]{:S(2)}, u32[]{:S(2)}) collective-permute-start(f32[256,1024]{1,0:T(8,128)S(1)} %shard_map.123.refs_0_.near.refs_10_), channel_id=1, source_target_pairs={{0,4},{4,0},{8,12},{12,8},{16,20},{20,16},{24,28},{28,24},{1,5},{5... | collective-permute-start | bytes 3145736 | tf_op jit(solution)/shard_map/ppermute | solution.py:567
  238.9 25.2 %collective-permute-start.38 = (f32[2048,128]{1,0:T(8,128)S(1)}, f32[2048,128]{1,0:T(8,128)S(1)}, u32[]{:S(2)}, u32[]{:S(2)}) collective-permute-start(f32[2048,128]{1,0:T(8,128)S(1)} %get-tuple-element.238), channel_id=1, source_target_pairs={{0,2},{1,3},{2,0},{3,1},{4,6},{5,7},{6,4},{7,5},{8,10},{9,11},{10,... | collective-permute-start | bytes 3145736 | tf_op jit(solution)/shard_map/ppermute | solution.py:567
  264.2 25.6 %collective-permute-start.41 = (f32[256,1024]{1,0:T(8,128)S(1)}, f32[256,1024]{1,0:T(8,128)S(1)}, u32[]{:S(2)}, u32[]{:S(2)}) collective-permute-start(f32[256,1024]{1,0:T(8,128)S(1)} %shard_map.127.refs_0_.near.refs_12_), channel_id=1, source_target_pairs={{0,4},{4,0},{8,12},{12,8},{16,20},{20,16},{24,28},{28,24},{1,5},{5... | collective-permute-start | bytes 3145736 | tf_op jit(solution)/shard_map/ppermute | solution.py:567
  264.9 25.2 %collective-permute-start.42 = (f32[2048,128]{1,0:T(8,128)S(1)}, f32[2048,128]{1,0:T(8,128)S(1)}, u32[]{:S(2)}, u32[]{:S(2)}) collective-permute-start(f32[2048,128]{1,0:T(8,128)S(1)} %get-tuple-element.243), channel_id=1, source_target_pairs={{0,2},{1,3},{2,0},{3,1},{4,6},{5,7},{6,4},{7,5},{8,10},{9,11},{10,... | collective-permute-start | bytes 3145736 | tf_op jit(solution)/shard_map/ppermute | solution.py:567
  291.8 55.5 %collective-permute-start.44 = (f32[2048,128]{1,0:T(8,128)}, f32[2048,128]{1,0:T(8,128)S(1)}, u32[]{:S(2)}, u32[]{:S(2)}) collective-permute-start(f32[2048,128]{1,0:T(8,128)} %get-tuple-element.249), channel_id=1, source_target_pairs={{0,2},{1,3},{2,0},{3,1},{4,6},{5,7},{6,4},{7,5},{8,10},{9,11},{10,... | collective-permute-start | bytes 3145736 | tf_op jit(solution)/shard_map/ppermute | solution.py:567
  307.0 40.3 %collective-permute-start.45 = (f32[2048,128]{1,0:T(8,128)}, f32[2048,128]{1,0:T(8,128)}, u32[]{:S(2)}, u32[]{:S(2)}) collective-permute-start(f32[2048,128]{1,0:T(8,128)} %get-tuple-element.250), channel_id=1, source_target_pairs={{0,2},{1,3},{2,0},{3,1},{4,6},{5,7},{6,4},{7,5},{8,10},{9,11},{10,... | collective-permute-start | bytes 3145736 | tf_op jit(solution)/shard_map/ppermute | solution.py:567
  (57 other events, 770.6 us)

commit v6 on v5

--- a/solution.py
+++ b/solution.py
@@ -429,7 +429,7 @@
             out_specs=[pl.BlockSpec((step, width), lambda i, ids: (i, 0))] * blocks,
             scratch_shapes=[pltpu.VMEM((number * height, cols), BF16)] * 4,
         ),
-        out_shape=[shape_of(rows, width)] * blocks,
+        out_shape=[hbm(rows, width, F32)] * blocks,
         compiler_params=params(48),
         cost_estimate=cost(12 * rows * cols * number * height, rows * cols * 8),
     )(ids, near, far, across, *mparts, *pparts)

time: 353 us -> 353 us (level)
  transfers between devices with their start and end apart: 46 -> 46, of which waited for: 28 -> 28; matrix products, arithmetic and copies ran while one was open for 2% -> 2% of each run, Pallas kernels for 49% -> 50%
where the time goes in v6:
time: 353 us; the launch traced here: 352 us
  Pallas kernels  184 us (52%)
  waiting for transfers between devices  103 us (29%)
  starting transfers between devices  47 us (13%)
  local copies, waits for them, and re-layouts  10.3 us (3%)
  between operations  4.95 us (1%)
    ppermute x46, waiting for transfers between devices, swap(): return lax.ppermute(v, axis, [(i, i ^ 1 << bit) for i in range(size)])  103 us
    pallas_call x4, Pallas kernels, predict(): pl.pallas_call(functools.partial(predict_body, shard, given is not None,...  52.1 us
    pallas_call x4, Pallas kernels, expr_part(): pl.pallas_call(functools.partial(expr_body, number, height, half), grid_s...  49.1 us
    ppermute x46, starting transfers between devices, swap(): return lax.ppermute(v, axis, [(i, i ^ 1 << bit) for i in range(size)])  47 us
    pallas_call x1, Pallas kernels, logit_part(): pl.pallas_call(functools.partial(logit_body, pieces, heights, unit, offse...  36.2 us
    pallas_call x2, Pallas kernels, exp_split(): pl.pallas_call(functools.partial(exp_body, with_sums), grid=(rows // step...  12.3 us
    pallas_call x32, Pallas kernels, simple(): pl.pallas_call(body, grid_spec=pltpu.PrefetchScalarGridSpec(num_scalar_pr...  11.8 us
  transfers between devices with their start and end apart: 46, of which 28 were waited for; matrix products, arithmetic and copies ran while one was open for 2% of the time, Pallas kernels for 50%

profile of v6, /device:TPU:0, one launch (start us, length us, event | category | flops | bytes accessed | tf_op | source)
XLA Modules:
  0.0 351.8 jit_solution(14515641408692132027)
XLA Ops:
  1.7 9.2 %shard_map.85 = (f32[264,1024]{1,0:T(8,128)}, bf16[256,2048]{1,0:T(8,128)(2,1)}, bf16[256,2048]{1,0:T(8,128)(2,1)}, f32[8,256]{1,0:T(8,128)}) custom-call(s32[8]{0:T(128)} %fusion.7.order, f32[2048,1024]{1,0:T(8,128)} %refs_0_.3, f32[2048,2048]{1,0:T(8,128)} %refs_3_.1), custom_call_target="tpu_custom_call" | custom-call | tf_op jit(solution)/shard_map/pallas_call | solution.py:263
  13.3 16.3 %shard_map.86 = (f32[264,1024]{1,0:T(8,128)}, f32[264,1024]{1,0:T(8,128)}, f32[264,1024]{1,0:T(8,128)}) custom-call(s32[8]{0:T(128)} %fusion.7.order, bf16[256,2048]{1,0:T(8,128)(2,1)} %get-tuple-element.127.refs_0_, bf16[256,2048]{1,0:T(8,128)(2,1)} %get-tuple-element.128.refs_1_, f32[8,256]{1,0:T(8,128)} %get-tuple-element.129.refs_2_, ...), custom_call_target="tpu_custom_call" | custom-call | tf_op jit(solution)/shard_map/pallas_call | solution.py:263
  29.7 6.2 %shard_map.87 = (bf16[2048,1024]{1,0:T(8,128)(2,1)}, bf16[2048,1024]{1,0:T(8,128)(2,1)}) custom-call(f32[2048,1024]{1,0:T(8,128)} %refs_0_.3), custom_call_target="tpu_custom_call" | custom-call | tf_op jit(solution)/shard_map/pallas_call | solution.py:145
  39.2 13.3 %shard_map.89 = (f32[264,1024]{1,0:T(8,128)}, f32[264,1024]{1,0:T(8,128)}) custom-call(s32[8]{0:T(128)} %fusion.7.order, f32[2048,1024]{1,0:T(8,128)} %refs_0_.3, f32[2048,2048]{1,0:T(8,128)} %refs_3_.1, f32[2048,2048]{1,0:T(8,128)} %refs_3_.1), custom_call_target="tpu_custom_call" | custom-call | tf_op jit(solution)/shard_map/pallas_call | solution.py:263
  56.0 11.6 %collective-permute-done.1.came = f32[264,512]{1,0:T(8,128)S(1)} collective-permute-done((f32[264,512]{1,0:T(8,128)S(1)}, f32[264,512]{1,0:T(8,128)S(1)}, u32[]{:S(2)}, u32[]{:S(2)}) %collective-permute-start.1) | collective-permute-done | bytes 540704 | tf_op jit(solution)/shard_map/ppermute | solution.py:567
  74.8 13.3 %shard_map.92 = (f32[136,1024]{1,0:T(8,128)}, f32[136,1024]{1,0:T(8,128)}, f32[136,1024]{1,0:T(8,128)}, f32[136,1024]{1,0:T(8,128)}) custom-call(s32[8]{0:T(128)} %fusion.7.order, f32[2048,1024]{1,0:T(8,128)} %refs_0_.3, f32[2048,2048]{1,0:T(8,128)} %refs_3_.1, f32[2048,2048]{1,0:T(8,128)} %refs_3_.1), custom_call_target="tpu_custom_call" | custom-call | tf_op jit(solution)/shard_map/pallas_call | solution.py:263
  94.8 6.1 %shard_map.96 = (bf16[2048,1024]{1,0:T(8,128)(2,1)}, bf16[2048,1024]{1,0:T(8,128)(2,1)}) custom-call(f32[2048,1024]{1,0:T(8,128)} %collective-permute-done.9.logits), custom_call_target="tpu_custom_call" | custom-call | tf_op jit(solution)/shard_map/pallas_call | solution.py:145
  101.0 9.1 %collective-permute-done.8.came = f32[264,512]{1,0:T(8,128)S(1)} collective-permute-done((f32[264,512]{1,0:T(8,128)}, f32[264,512]{1,0:T(8,128)S(1)}, u32[]{:S(2)}, u32[]{:S(2)}) %collective-permute-start.8) | collective-permute-done | bytes 540704 | tf_op jit(solution)/shard_map/ppermute | solution.py:567
  113.3 13.6 %collective-permute-done.11.came = f32[136,512]{1,0:T(8,128)S(1)} collective-permute-done((f32[136,512]{1,0:T(8,128)S(1)}, f32[136,512]{1,0:T(8,128)S(1)}, u32[]{:S(2)}, u32[]{:S(2)}) %collective-permute-start.11) | collective-permute-done | bytes 278560 | tf_op jit(solution)/shard_map/ppermute | solution.py:567
  132.2 4.7 %collective-permute-done.13.came = f32[136,256]{1,0:T(8,128)S(1)} collective-permute-done((f32[136,256]{1,0:T(8,128)S(1)}, f32[136,256]{1,0:T(8,128)S(1)}, u32[]{:S(2)}, u32[]{:S(2)}) %collective-permute-start.13) | collective-permute-done | bytes 139296 | tf_op jit(solution)/shard_map/ppermute | solution.py:567
  148.1 3.7 %collective-permute-done.20.b = f32[8,1024]{1,0:T(8,128)S(1)} collective-permute-done((f32[8,1024]{1,0:T(8,128)S(1)}, f32[8,1024]{1,0:T(8,128)S(1)}, u32[]{:S(2)}, u32[]{:S(2)}) %collective-permute-start.20) | collective-permute-done | bytes 32800 | tf_op jit(solution)/shard_map/ppermute | solution.py:567
  156.4 6.3 %shard_map.112 = f32[8,2048]{1,0:T(8,128)} custom-call(f32[8,1024]{1,0:T(8,128)} %copy-done.17, bf16[2048,1024]{1,0:T(8,128)(2,1)} %get-tuple-element.134.mh.refs_4_, bf16[2048,1024]{1,0:T(8,128)(2,1)} %get-tuple-element.210.ml.refs_5_), custom_call_target="tpu_custom_call" | custom-call | tf_op jit(solution)/shard_map/pallas_call | solution.py:166
  171.3 12.2 %collective-permute-done.25.refs_1_ = f32[64,1024]{1,0:T(8,128)S(1)} collective-permute-done((f32[64,1024]{1,0:T(8,128)S(1)}, f32[64,1024]{1,0:T(8,128)S(1)}, u32[]{:S(2)}, u32[]{:S(2)}) %collective-permute-start.25) | collective-permute-done | bytes 262176 | tf_op jit(solution)/shard_map/ppermute | solution.py:567
  195.2 5.1 %shard_map.118 = f32[8,1024]{1,0:T(8,128)} custom-call(f32[8,2048]{1,0:T(8,128)} %broadcast_in_dim.8.dens.refs_0_, f32[8,1024]{1,0:T(8,128)} %copy-done.17, bf16[2048,1024]{1,0:T(8,128)(2,1)} %get-tuple-element.134.mh.refs_4_, bf16[2048,1024]{1,0:T(8,128)(2,1)} %get-tuple-element.210.ml.refs_5_), custom_call_target="tpu_custom_call" | custom-call | tf_op jit(solution)/shard_map/pallas_call | solution.py:383
  214.6 12.5 %shard_map.122 = (f32[2048,128]{1,0:T(8,128)}, f32[2048,128]{1,0:T(8,128)}) custom-call(s32[8]{0:T(128)S(1)} %pad_add_fusion.ids, f32[256,1024]{1,0:T(8,128)S(1)} %shard_map.116.refs_0_.near.refs_6_, f32[256,1024]{1,0:T(8,128)S(1)} %collective-permute-done.31.refs_1_.far.refs_7_, f32[256,1024]{1,0:T(8,128)} %collective-permute-done.32.across, ...), custom_call_target="tpu_custom_call" | custom-call | tf_op jit(solution)/shard_map/pallas_call | solution.py:422
  227.2 4.5 %collective-permute-done.30.refs_1_ = f32[128,1024]{1,0:T(8,128)} collective-permute-done((f32[128,1024]{1,0:T(8,128)}, f32[128,1024]{1,0:T(8,128)}, u32[]{:S(2)}, u32[]{:S(2)}) %collective-permute-start.30) | collective-permute-done | bytes 524320 | tf_op jit(solution)/shard_map/ppermute | solution.py:567
  233.0 2.9 collective-permute-done.34.refs_1_.far.refs_9_
  243.0 12.8 %shard_map.126 = (f32[2048,128]{1,0:T(8,128)}, f32[2048,128]{1,0:T(8,128)}) custom-call(s32[8]{0:T(128)S(1)} %pad_add_fusion.ids, f32[256,1024]{1,0:T(8,128)S(1)} %shard_map.119.refs_0_.near.refs_8_, f32[256,1024]{1,0:T(8,128)} %collective-permute-done.34.refs_1_.far.refs_9_, f32[256,1024]{1,0:T(8,128)S(1)} %collective-permute-done.35.across, ...), custom_call_target="tpu_custom_call" | custom-call | tf_op jit(solution)/shard_map/pallas_call | solution.py:422
  255.9 7.0 %collective-permute-done.37.refs_1_.far.refs_11_ = f32[256,1024]{1,0:T(8,128)S(1)} collective-permute-done((f32[256,1024]{1,0:T(8,128)S(1)}, f32[256,1024]{1,0:T(8,128)S(1)}, u32[]{:S(2)}, u32[]{:S(2)}) %collective-permute-start.37) | collective-permute-done | bytes 1048608 | tf_op jit(solution)/shard_map/ppermute | solution.py:567
  267.7 11.9 %shard_map.130 = (f32[2048,128]{1,0:T(8,128)}, f32[2048,128]{1,0:T(8,128)}) custom-call(s32[8]{0:T(128)S(1)} %pad_add_fusion.ids, f32[256,1024]{1,0:T(8,128)S(1)} %shard_map.123.refs_0_.near.refs_10_, f32[256,1024]{1,0:T(8,128)S(1)} %collective-permute-done.37.refs_1_.far.refs_11_, f32[256,1024]{1,0:T(8,128)S(1)} %collective-permute-done.39.across, ...), custom_call_target="tpu_custom_call" | custom-call | tf_op jit(solution)/shard_map/pallas_call | solution.py:422
  279.6 10.2 %collective-permute-done.41.refs_1_.far.refs_13_ = f32[256,1024]{1,0:T(8,128)S(1)} collective-permute-done((f32[256,1024]{1,0:T(8,128)S(1)}, f32[256,1024]{1,0:T(8,128)S(1)}, u32[]{:S(2)}, u32[]{:S(2)}) %collective-permute-start.41) | collective-permute-done | bytes 1048608 | tf_op jit(solution)/shard_map/ppermute | solution.py:567
  294.3 11.9 %shard_map.134 = (f32[2048,128]{1,0:T(8,128)}, f32[2048,128]{1,0:T(8,128)}) custom-call(s32[8]{0:T(128)S(1)} %pad_add_fusion.ids, f32[256,1024]{1,0:T(8,128)S(1)} %shard_map.127.refs_0_.near.refs_12_, f32[256,1024]{1,0:T(8,128)S(1)} %collective-permute-done.41.refs_1_.far.refs_13_, f32[256,1024]{1,0:T(8,128)S(1)} %collective-permute-done.43.across, ...), custom_call_target="tpu_custom_call" | custom-call | tf_op jit(solution)/shard_map/pallas_call | solution.py:422
  310.6 36.2 %shard_map.135 = f32[2048,1024]{1,0:T(8,128)} custom-call(s32[8]{0:T(128)} %fusion.7.order, f32[8,2048]{1,0:T(8,128)} %broadcast_in_dim.8.dens.refs_0_, f32[8,1024]{1,0:T(8,128)} %copy-done.17, f32[8,1024]{1,0:T(8,128)} %slice.30.refs_2_, f32[2048,2048]{1,0:T(8,128)} %refs_3_.1, bf16[2048,1024]{1,0:T(8,128)(2,1)} %get-tuple-element.134.mh.refs_4_, ...), custom_call_target="tpu_custom_call" | custom-call | tf_op jit(solution)/shard_map/pallas_call | solution.py:493
  346.9 3.8 %shard_map.136 = f32[2048,512]{1,0:T(8,128)} custom-call(f32[2048,128]{1,0:T(8,128)S(1)} %copy-done.13, f32[2048,128]{1,0:T(8,128)S(1)} %collective-permute-done.38.refs_1_, f32[2048,128]{1,0:T(8,128)S(1)} %copy-done.14, f32[2048,128]{1,0:T(8,128)S(1)} %collective-permute-done.42.refs_3_, f32[2048,128]{1,0:T(8,128)S(1)} %copy-done.15, ...), custom_call_target="tpu_custom_call" | custom-call | tf_op jit(solution)/shard_map/pallas_call | solution.py:524
  (221 shorter events, 102.4 us)
Async XLA Ops:
  0.6 94.2 %collective-permute-start.9 = (f32[2048,1024]{1,0:T(8,128)}, f32[2048,1024]{1,0:T(8,128)}, u32[]{:S(2)}, u32[]{:S(2)}) collective-permute-start(f32[2048,1024]{1,0:T(8,128)} %refs_0_.3), channel_id=1, source_target_pairs={{0,1},{1,0},{2,3},{3,2},{4,5},{5,4},{6,7},{7,6},{8,9},{9,8},{10,11... | collective-permute-start | bytes 25165832 | tf_op jit(solution)/shard_map/ppermute | solution.py:567
  10.8 27.4 %collective-permute-start = (f32[264,1024]{1,0:T(8,128)}, f32[264,1024]{1,0:T(8,128)S(1)}, u32[]{:S(2)}, u32[]{:S(2)}) collective-permute-start(f32[264,1024]{1,0:T(8,128)} %get-tuple-element.130), channel_id=1, source_target_pairs={{0,4},{4,0},{8,12},{12,8},{16,20},{20,16},{24,28},{28,24},{1,5},{5... | collective-permute-start | bytes 3244040 | tf_op jit(solution)/shard_map/ppermute | solution.py:567
  29.7 41.4 %collective-permute-start.3 = (f32[264,1024]{1,0:T(8,128)}, f32[264,1024]{1,0:T(8,128)}, u32[]{:S(2)}, u32[]{:S(2)}) collective-permute-start(f32[264,1024]{1,0:T(8,128)} %get-tuple-element.144), channel_id=1, source_target_pairs={{0,4},{4,0},{8,12},{12,8},{16,20},{20,16},{24,28},{28,24},{1,5},{5... | collective-permute-start | bytes 3244040 | tf_op jit(solution)/shard_map/ppermute | solution.py:567
  52.5 39.4 %collective-permute-start.5 = (f32[264,1024]{1,0:T(8,128)}, f32[264,1024]{1,0:T(8,128)S(1)}, u32[]{:S(2)}, u32[]{:S(2)}) collective-permute-start(f32[264,1024]{1,0:T(8,128)} %get-tuple-element.152), channel_id=1, source_target_pairs={{0,4},{4,0},{8,12},{12,8},{16,20},{20,16},{24,28},{28,24},{1,5},{5... | collective-permute-start | bytes 3244040 | tf_op jit(solution)/shard_map/ppermute | solution.py:567
  68.4 20.2 %collective-permute-start.2 = (f32[264,256]{1,0:T(8,128)}, f32[264,256]{1,0:T(8,128)}, u32[]{:S(2)}, u32[]{:S(2)}) collective-permute-start(f32[264,256]{1,0:T(8,128)} %get-tuple-element.142), channel_id=1, source_target_pairs={{0,16},{4,20},{8,24},{12,28},{16,0},{20,4},{24,8},{28,12},{1,17},{... | collective-permute-start | bytes 811016 | tf_op jit(solution)/shard_map/ppermute | solution.py:567
  73.2 20.1 %collective-permute-start.4 = (f32[264,512]{1,0:T(8,128)}, f32[264,512]{1,0:T(8,128)}, u32[]{:S(2)}, u32[]{:S(2)}) collective-permute-start(f32[264,512]{1,0:T(8,128)} %get-tuple-element.146), channel_id=1, source_target_pairs={{0,8},{4,12},{8,0},{12,4},{16,24},{20,28},{24,16},{28,20},{1,9},{5... | collective-permute-start | bytes 1622024 | tf_op jit(solution)/shard_map/ppermute | solution.py:567
  88.1 22.0 %collective-permute-start.7 = (f32[136,1024]{1,0:T(8,128)}, f32[136,1024]{1,0:T(8,128)S(1)}, u32[]{:S(2)}, u32[]{:S(2)}) collective-permute-start(f32[136,1024]{1,0:T(8,128)} %get-tuple-element.158), channel_id=1, source_target_pairs={{0,4},{4,0},{8,12},{12,8},{16,20},{20,16},{24,28},{28,24},{1,5},{5... | collective-permute-start | bytes 1671176 | tf_op jit(solution)/shard_map/ppermute | solution.py:567
  88.6 23.7 %collective-permute-start.12 = (f32[136,1024]{1,0:T(8,128)}, f32[136,1024]{1,0:T(8,128)S(1)}, u32[]{:S(2)}, u32[]{:S(2)}) collective-permute-start(f32[136,1024]{1,0:T(8,128)} %get-tuple-element.171), channel_id=1, source_target_pairs={{0,4},{4,0},{8,12},{12,8},{16,20},{20,16},{24,28},{28,24},{1,5},{5... | collective-permute-start | bytes 1671176 | tf_op jit(solution)/shard_map/ppermute | solution.py:567
  92.8 17.2 %collective-permute-start.8 = (f32[264,512]{1,0:T(8,128)}, f32[264,512]{1,0:T(8,128)S(1)}, u32[]{:S(2)}, u32[]{:S(2)}) collective-permute-start(f32[264,512]{1,0:T(8,128)} %get-tuple-element.154), channel_id=1, source_target_pairs={{0,8},{4,12},{8,0},{12,4},{16,24},{20,28},{24,16},{28,20},{1,9},{5... | collective-permute-start | bytes 1622024 | tf_op jit(solution)/shard_map/ppermute | solution.py:567
  110.2 16.8 %collective-permute-start.11 = (f32[136,512]{1,0:T(8,128)S(1)}, f32[136,512]{1,0:T(8,128)S(1)}, u32[]{:S(2)}, u32[]{:S(2)}) collective-permute-start(f32[136,512]{1,0:T(8,128)S(1)} %get-tuple-element.165), channel_id=1, source_target_pairs={{0,8},{4,12},{8,0},{12,4},{16,24},{20,28},{24,16},{28,20},{1,9},{5... | collective-permute-start | bytes 835592 | tf_op jit(solution)/shard_map/ppermute | solution.py:567
  112.4 17.6 %collective-permute-start.14 = (f32[136,512]{1,0:T(8,128)S(1)}, f32[136,512]{1,0:T(8,128)S(1)}, u32[]{:S(2)}, u32[]{:S(2)}) collective-permute-start(f32[136,512]{1,0:T(8,128)S(1)} %get-tuple-element.173), channel_id=1, source_target_pairs={{0,8},{4,12},{8,0},{12,4},{16,24},{20,28},{24,16},{28,20},{1,9},{5... | collective-permute-start | bytes 835592 | tf_op jit(solution)/shard_map/ppermute | solution.py:567
  167.0 18.6 %collective-permute-start.24 = (f32[128,1024]{1,0:T(8,128)S(1)}, f32[128,1024]{1,0:T(8,128)S(1)}, u32[]{:S(2)}, u32[]{:S(2)}) collective-permute-start(f32[128,1024]{1,0:T(8,128)S(1)} %shard_map.113.refs_0_), channel_id=1, source_target_pairs={{0,8},{4,12},{8,0},{12,4},{16,24},{20,28},{24,16},{28,20},{1,9},{5... | collective-permute-start | bytes 1572872 | tf_op jit(solution)/shard_map/ppermute | solution.py:567
  185.8 23.3 %collective-permute-start.31 = (f32[256,1024]{1,0:T(8,128)S(1)}, f32[256,1024]{1,0:T(8,128)S(1)}, u32[]{:S(2)}, u32[]{:S(2)}) collective-permute-start(f32[256,1024]{1,0:T(8,128)S(1)} %shard_map.116.refs_0_.near.refs_6_), channel_id=1, source_target_pairs={{0,4},{4,0},{8,12},{12,8},{16,20},{20,16},{24,28},{28,24},{1,5},{5... | collective-permute-start | bytes 3145736 | tf_op jit(solution)/shard_map/ppermute | solution.py:567
  186.3 17.4 %collective-permute-start.28 = (f32[128,1024]{1,0:T(8,128)S(1)}, f32[128,1024]{1,0:T(8,128)S(1)}, u32[]{:S(2)}, u32[]{:S(2)}) collective-permute-start(f32[128,1024]{1,0:T(8,128)S(1)} %shard_map.115.refs_0_), channel_id=1, source_target_pairs={{0,8},{4,12},{8,0},{12,4},{16,24},{20,28},{24,16},{28,20},{1,9},{5... | collective-permute-start | bytes 1572872 | tf_op jit(solution)/shard_map/ppermute | solution.py:567
  189.0 17.7 %collective-permute-start.27 = (f32[64,1024]{1,0:T(8,128)}, f32[64,1024]{1,0:T(8,128)}, u32[]{:S(2)}, u32[]{:S(2)}) collective-permute-start(f32[64,1024]{1,0:T(8,128)} %get-tuple-element.223.refs_0_), channel_id=1, source_target_pairs={{0,16},{4,20},{8,24},{12,28},{16,0},{20,4},{24,8},{28,12},{1,17},{... | collective-permute-start | bytes 786440 | tf_op jit(solution)/shard_map/ppermute | solution.py:567
  210.2 25.7 %collective-permute-start.34 = (f32[256,1024]{1,0:T(8,128)S(1)}, f32[256,1024]{1,0:T(8,128)}, u32[]{:S(2)}, u32[]{:S(2)}) collective-permute-start(f32[256,1024]{1,0:T(8,128)S(1)} %shard_map.119.refs_0_.near.refs_8_), channel_id=1, source_target_pairs={{0,4},{4,0},{8,12},{12,8},{16,20},{20,16},{24,28},{28,24},{1,5},{5... | collective-permute-start | bytes 3145736 | tf_op jit(solution)/shard_map/ppermute | solution.py:567
  211.6 20.0 %collective-permute-start.30 = (f32[128,1024]{1,0:T(8,128)}, f32[128,1024]{1,0:T(8,128)}, u32[]{:S(2)}, u32[]{:S(2)}) collective-permute-start(f32[128,1024]{1,0:T(8,128)} %shard_map.120.refs_0_), channel_id=1, source_target_pairs={{0,8},{4,12},{8,0},{12,4},{16,24},{20,28},{24,16},{28,20},{1,9},{5... | collective-permute-start | bytes 1572872 | tf_op jit(solution)/shard_map/ppermute | solution.py:567
  212.2 20.7 %collective-permute-start.29 = (f32[64,1024]{1,0:T(8,128)S(1)}, f32[64,1024]{1,0:T(8,128)S(1)}, u32[]{:S(2)}, u32[]{:S(2)}) collective-permute-start(f32[64,1024]{1,0:T(8,128)S(1)} %get-tuple-element.226.refs_0_), channel_id=1, source_target_pairs={{0,16},{4,20},{8,24},{12,28},{16,0},{20,4},{24,8},{28,12},{1,17},{... | collective-permute-start | bytes 786440 | tf_op jit(solution)/shard_map/ppermute | solution.py:567
  237.3 25.6 %collective-permute-start.37 = (f32[256,1024]{1,0:T(8,128)S(1)}, f32[256,1024]{1,0:T(8,128)S(1)}, u32[]{:S(2)}, u32[]{:S(2)}) collective-permute-start(f32[256,1024]{1,0:T(8,128)S(1)} %shard_map.123.refs_0_.near.refs_10_), channel_id=1, source_target_pairs={{0,4},{4,0},{8,12},{12,8},{16,20},{20,16},{24,28},{28,24},{1,5},{5... | collective-permute-start | bytes 3145736 | tf_op jit(solution)/shard_map/ppermute | solution.py:567
  238.8 25.2 %collective-permute-start.38 = (f32[2048,128]{1,0:T(8,128)S(1)}, f32[2048,128]{1,0:T(8,128)S(1)}, u32[]{:S(2)}, u32[]{:S(2)}) collective-permute-start(f32[2048,128]{1,0:T(8,128)S(1)} %copy-done.32), channel_id=1, source_target_pairs={{0,2},{1,3},{2,0},{3,1},{4,6},{5,7},{6,4},{7,5},{8,10},{9,11},{10,... | collective-permute-start | bytes 3145736 | tf_op jit(solution)/shard_map/ppermute | solution.py:567
  264.1 25.6 %collective-permute-start.41 = (f32[256,1024]{1,0:T(8,128)S(1)}, f32[256,1024]{1,0:T(8,128)S(1)}, u32[]{:S(2)}, u32[]{:S(2)}) collective-permute-start(f32[256,1024]{1,0:T(8,128)S(1)} %shard_map.127.refs_0_.near.refs_12_), channel_id=1, source_target_pairs={{0,4},{4,0},{8,12},{12,8},{16,20},{20,16},{24,28},{28,24},{1,5},{5... | collective-permute-start | bytes 3145736 | tf_op jit(solution)/shard_map/ppermute | solution.py:567
  264.8 25.2 %collective-permute-start.42 = (f32[2048,128]{1,0:T(8,128)S(1)}, f32[2048,128]{1,0:T(8,128)S(1)}, u32[]{:S(2)}, u32[]{:S(2)}) collective-permute-start(f32[2048,128]{1,0:T(8,128)S(1)} %copy-done.33), channel_id=1, source_target_pairs={{0,2},{1,3},{2,0},{3,1},{4,6},{5,7},{6,4},{7,5},{8,10},{9,11},{10,... | collective-permute-start | bytes 3145736 | tf_op jit(solution)/shard_map/ppermute | solution.py:567
  291.7 55.2 %collective-permute-start.44 = (f32[2048,128]{1,0:T(8,128)}, f32[2048,128]{1,0:T(8,128)S(1)}, u32[]{:S(2)}, u32[]{:S(2)}) collective-permute-start(f32[2048,128]{1,0:T(8,128)} %get-tuple-element.249), channel_id=1, source_target_pairs={{0,2},{1,3},{2,0},{3,1},{4,6},{5,7},{6,4},{7,5},{8,10},{9,11},{10,... | collective-permute-start | bytes 3145736 | tf_op jit(solution)/shard_map/ppermute | solution.py:567
  306.1 40.7 %collective-permute-start.45 = (f32[2048,128]{1,0:T(8,128)}, f32[2048,128]{1,0:T(8,128)}, u32[]{:S(2)}, u32[]{:S(2)}) collective-permute-start(f32[2048,128]{1,0:T(8,128)} %get-tuple-element.250), channel_id=1, source_target_pairs={{0,2},{1,3},{2,0},{3,1},{4,6},{5,7},{6,4},{7,5},{8,10},{9,11},{10,... | collective-permute-start | bytes 3145736 | tf_op jit(solution)/shard_map/ppermute | solution.py:567
  (57 other events, 815.5 us)
